TPU v7x, 128 devices: a whole 4x4x4 slice. The times are simulated.
128 devices in a mesh: batch: 64 (over x, y_hi, z, core), seq: 2 (over y_lo).
Axes of the slice: x: 4, y: 4 (y_hi: 2, y_lo: 2; y = y_hi * 2 + y_lo), z: 4, core: 2. Of those that a mesh axis runs over, the one named last changes fastest.
Arguments:
- tokens: bfloat16 [64, 4, 64, 768], P('batch', None, 'seq'), may hold values from -6 to 6
- segment_counts: int32 [64], P('batch'), may hold values from 1 to 4, as said below
- ln1_gain: bfloat16 [768], P(('batch', 'seq')), may hold values from 0.5 to 1.5
- ln1_bias: bfloat16 [768], P(('batch', 'seq')), may hold values from -1.75 to 1.75
- w_qkv: bfloat16 [768, 2304], P(('batch', 'seq')), may hold values from -0.21875 to 0.21875
- q_bias: bfloat16 [768], P(('batch', 'seq')), may hold values from -3 to 3
- v_bias: bfloat16 [768], P(('batch', 'seq')), may hold values from -3 to 3
- w_out: bfloat16 [768, 768], P(('batch', 'seq')), may hold values from -1.25 to 1.25
- out_bias: bfloat16 [768], P(('batch', 'seq')), may hold values from -1.75 to 1.75
- ln2_gain: bfloat16 [768], P(('batch', 'seq')), may hold values from 0.5 to 1.5
- ln2_bias: bfloat16 [768], P(('batch', 'seq')), may hold values from -1.75 to 1.75
- w_up: bfloat16 [768, 3072], P(('batch', 'seq')), may hold values from -0.21875 to 0.21875
- up_bias: bfloat16 [3072], P(('batch', 'seq')), may hold values from -3 to 3
- w_down: bfloat16 [3072, 768], P(('batch', 'seq')), may hold values from -0.109375 to 0.109375
- down_bias: bfloat16 [768], P(('batch', 'seq')), may hold values from -1.75 to 1.75
- cotangent: bfloat16 [64, 4, 64, 768], P('batch', None, 'seq'), may hold values from -6 to 6
Outputs:
- block_out: bfloat16 [64, 4, 64, 768], P('batch', None, 'seq')
- grad_tokens: bfloat16 [64, 4, 64, 768], P('batch', None, 'seq')
- grad_ln1_gain: float32 [768], P(('batch', 'seq'))
- grad_ln1_bias: float32 [768], P(('batch', 'seq'))
- grad_w_qkv: float32 [768, 2304], P(('batch', 'seq'))
- grad_q_bias: float32 [768], P(('batch', 'seq'))
- grad_v_bias: float32 [768], P(('batch', 'seq'))
- grad_w_out: float32 [768, 768], P(('batch', 'seq'))
- grad_out_bias: float32 [768], P(('batch', 'seq'))
- grad_ln2_gain: float32 [768], P(('batch', 'seq'))
- grad_ln2_bias: float32 [768], P(('batch', 'seq'))
- grad_w_up: float32 [768, 3072], P(('batch', 'seq'))
- grad_up_bias: float32 [3072], P(('batch', 'seq'))
- grad_w_down: float32 [3072, 768], P(('batch', 'seq'))
- grad_down_bias: float32 [768], P(('batch', 'seq'))
Inputs may be any that keep to these rules, and one draw needn't show every extreme that they name: `segment_counts`: slots at or beyond an item's count are absent. Some item holds 4 segments and some item holds one.
All inputs are finite; a program needn't handle non-finite values.
Results may differ from a plain program's by a relative error of at most 0.015.
Values may be sent and summed in bfloat16 or wider, within the bound.
No kernel may reach another device: no remote copies, remote signals or barrier semaphores. Data moves between devices by JAX's collectives and lax.ppermute only.
A program may use at most 128 MiB of HBM per device.

v0:
```python
import jax
import jax.numpy as jnp
import numpy as np
from jax import lax
from jax.experimental import pallas as pl
from jax.experimental.pallas import tpu as pltpu
from jax.sharding import Mesh
from jax.sharding import PartitionSpec as P

WIDTH = 768
HEAD = 64
NSUM = 16
SLOTS = 4
SEGLEN = 64
HALFSEG = 32
FF = 3072

EPSILON = 1e-05
MASKED = -1e30
SCALE = HEAD ** (-0.5)

AXES = ("x", "yh", "z", "c", "yl")
SIZES = (4, 2, 4, 2, 2)
QUAD_AXES = ("x", "yh", "z")
QUADS = 32
DEVICES = 128
ROWS = 256
OWN = 128
HALF = WIDTH // 2
QKV = 3 * HALF
UP = FF // 2
SMALL = 128
ATTN = QKV + SMALL + HALF
BLOCK = WIDTH // 4
DOWN_ROWS = UP // 4
RING_Y = ("yh", "yl")
EIGHT = ("yh", "c", "yl")
VMEM_LIMIT = 60 * 1024 * 1024

F32 = jnp.float32
BF16 = jnp.bfloat16


def dot_nn(left, right):
    return jnp.dot(left, right, preferred_element_type=F32)


def dot_tn(left, right):
    return lax.dot_general(left, right, (((0,), (0,)), ((), ())), preferred_element_type=F32)


def dot_nt(left, right):
    return lax.dot_general(left, right, (((1,), (1,)), ((), ())), preferred_element_type=F32)


def normalised(values):
    center = values - jnp.mean(values, axis=-1, keepdims=True)
    spread = jnp.mean(center * center, axis=-1, keepdims=True)
    scale = lax.rsqrt(spread + EPSILON)
    return center * scale, scale


def norm_back(grad, unit, scale, gain):
    inner = grad * gain
    mean = jnp.mean(inner, axis=-1, keepdims=True)
    along = jnp.mean(inner * unit, axis=-1, keepdims=True)
    return scale * (inner - mean - unit * along)


def total(values):
    return jnp.sum(values.astype(F32), axis=0, keepdims=True)


def swap_halves(values):
    return jnp.concatenate([values[OWN:], values[:OWN]], axis=0)


def masks(core):
    def place(dim):
        row = lax.broadcasted_iota(jnp.int32, (ROWS, ROWS), dim)
        second = (row >= OWN).astype(jnp.int32)
        inner = row - second * OWN
        half = core + second - 2 * core * second
        slot = inner // HALFSEG
        return slot, half * HALFSEG + inner - slot * HALFSEG

    query_slot, query_pos = place(0)
    key_slot, key_pos = place(1)
    same = (query_slot == key_slot) & (key_pos <= query_pos)
    earlier = (key_slot < query_slot) & (key_pos >= SEGLEN - NSUM)
    return same | earlier, key_slot >= query_slot - 2


def positions(core, at):
    way = 1 - 2 * core
    return at, lax.rem(at + 4 - way, 4), lax.rem(at + 4 + way, 4), lax.rem(at + 2, 4)


def head_lanes(j):
    lane = lax.broadcasted_iota(jnp.int32, (1, 2 * HEAD), 1)
    return jnp.where(lane // HEAD == j, 1.0, 0.0).astype(BF16)


def up_runs(t):
    for yh, yl, z, x in np.ndindex(2, 2, 4, 4):
        yield 96 * ((x * 2 + yh) * 4 + z) + 48 * t + 24 * yl, 24 * (((yh * 2 + yl) * 4 + z) * 4 + x)


def halves_kernel(qkv_ref, out_ref, up_ref, *refs):
    *vec_refs, up_b_ref, parts_ref, rows_ref, wide_ref, half_ref = refs
    rows_ref[...] = jnp.zeros((16, 128), F32)
    for v, ref in enumerate(vec_refs):
        rows_ref[v : v + 1, 0:6] = ref[...].astype(F32).reshape(1, 6)
    rows_ref[8:9, 0:24] = up_b_ref[...].astype(F32).reshape(1, 24)
    row = lax.broadcasted_iota(jnp.int32, (8, 128), 0)
    lane = lax.broadcasted_iota(jnp.int32, (8, 128), 1)
    src = lax.broadcasted_iota(jnp.int32, (128, 128), 0)
    col = lax.broadcasted_iota(jnp.int32, (128, 128), 1)
    one = jnp.where(row == lane, 1.0, 0.0).astype(BF16)
    vecs = jnp.concatenate([rows_ref[0:8, :].astype(BF16), jnp.zeros((120, 128), BF16)], axis=0)
    up_b = jnp.where(lane // 4 == row, jnp.broadcast_to(rows_ref[8:9, :], (8, 128)), 0.0).astype(BF16)
    put = jnp.where((src < 24) & (8 + lax.rem(src, 4) == col), 1.0, 0.0).astype(BF16)
    small = (dot_nt(one, vecs) + dot_nn(up_b, put)).astype(BF16)
    wide_ref[...] = up_ref[...].astype(F32)
    for t in range(2):
        for src, to in up_runs(t):
            half_ref[:, to : to + 24] = wide_ref[:, src : src + 24]
        up = half_ref[...].astype(BF16)
        for at in (2 * t, 2 * t + 1, 2 * t + 4, 2 * t + 5):
            for j in range(3):
                parts_ref[at, :, j * HALF : (j + 1) * HALF] = qkv_ref[:, j * WIDTH + t * HALF : j * WIDTH + (t + 1) * HALF]
            parts_ref[at, :, QKV : QKV + SMALL] = small[:6]
            parts_ref[at, :, QKV + SMALL : ATTN] = out_ref[:, t * HALF : (t + 1) * HALF]
            parts_ref[at, :, ATTN:] = up


def outputs_kernel(
    got_ref, down_ref, tokens_ref,
    qkv_ref, out_ref, up_ref, out_down_ref, out_tokens_ref, *refs,
):
    *vec_refs, up_b_ref, rows_ref = refs
    out_down_ref[...] = down_ref[...]
    out_tokens_ref[...] = tokens_ref[...]
    small = jnp.zeros((6, SMALL), F32)
    for t in range(2):
        rows = [got_ref[at].astype(F32) for at in (2 * t, 2 * t + 1, 2 * t + 4, 2 * t + 5)]
        rows = (rows[0] + rows[1]) + (rows[2] + rows[3])
        for j in range(3):
            qkv_ref[:, j * WIDTH + t * HALF : j * WIDTH + (t + 1) * HALF] = rows[:, j * HALF : (j + 1) * HALF]
        small += rows[:, QKV : QKV + SMALL]
        out_ref[:, t * HALF : (t + 1) * HALF] = rows[:, QKV + SMALL : ATTN]
        for to, src in up_runs(t):
            up_ref[:, to : to + 24] = rows[:, ATTN + src : ATTN + src + 24]
    small = small[:, 0:12] + small[:, 16:28]
    rows_ref[...] = jnp.zeros((128, 128), F32)
    rows_ref[0:6, 0:12] = small
    flipped = rows_ref[...].T
    for v, ref in enumerate(vec_refs):
        ref[...] = flipped[v : v + 1, 0:6].reshape(6)
    up_b_ref[...] = jnp.concatenate([small[j : j + 1, 8:12] for j in range(6)], axis=1).reshape(24)


def attend_kernel(
    place_ref, x_ref, part_0, part_1, part_2, part_3,
    a_ref, qkv_ref, o_ref, lse_ref, w_ref, out_ref, small_ref, vec_ref,
):
    core = place_ref[0]
    for part, at in zip((part_0, part_1, part_2, part_3), positions(core, place_ref[1])):
        rows = pl.ds(pl.multiple_of(at * BLOCK, 64), BLOCK)
        w_ref[rows, :] = part[:, pl.ds(0, QKV)]
        small_ref[rows, :] = part[:, pl.ds(QKV, SMALL)]
        out_ref[rows, :] = part[:, pl.ds(QKV + SMALL, HALF)]
    vec_ref[...] = small_ref[...].astype(F32).T[:16]
    unit, _ = normalised(x_ref[...].astype(F32))
    a = (unit * vec_ref[0:1, :] + vec_ref[1:2, :]).astype(BF16)
    a_ref[...] = a
    here = pl.ds(pl.multiple_of(core * HALF, 128), HALF)
    shift = jnp.concatenate([vec_ref[2:3, here], jnp.zeros((1, HALF), F32), vec_ref[3:4, here]], axis=1)
    qkv_ref[...] = (dot_nn(a, w_ref[...]) + shift).astype(BF16)
    admitted, _ = masks(core)
    lane = lax.broadcasted_iota(jnp.int32, (ROWS, 128), 1)
    kept = jnp.zeros((ROWS, 128), F32)
    for pair in range(3):
        lanes = pl.ds(128 * pair, 128)
        query = qkv_ref[:, lanes]
        key = qkv_ref[:, pl.ds(HALF + 128 * pair, 128)]
        value = qkv_ref[:, pl.ds(2 * HALF + 128 * pair, 128)]
        out = jnp.zeros((ROWS, 128), F32)
        for j in range(2):
            only = head_lanes(j)
            scores = jnp.where(admitted, dot_nt(query * only, key) * SCALE, MASKED)
            top = jnp.max(scores, axis=-1, keepdims=True)
            grown = jnp.exp(scores - top)
            amount = jnp.sum(grown, axis=-1, keepdims=True)
            kept = jnp.where(lane == 2 * pair + j, top + jnp.log(amount), kept)
            probs = (grown * (1.0 / amount)).astype(BF16)
            out += dot_nn(probs, value * only)
        o_ref[:, lanes] = out.astype(BF16)
    lse_ref[...] = kept


def mlp_kernel(
    place_ref, x_ref, own_o_ref, far_o_ref, own_out_ref, far_out_ref, vec_ref, up_b_ref, g_ref, order_ref,
    up_0, up_1, up_2, up_3, down_0, down_1, down_2, down_3,
    h_ref, m_own_ref, m_far_ref, grad_a_ref, grad_up_b_ref, grad_down_b_ref,
    part_0, part_1, part_2, part_3,
    up_ref, down_ref, grad_up_ref, grad_down_ref,
):
    core = place_ref[0]
    up_at, down_at = positions(core, place_ref[3]), positions(core, place_ref[2])
    for up, at in zip((up_0, up_1, up_2, up_3), up_at):
        up_ref[pl.ds(pl.multiple_of(at * BLOCK, 64), BLOCK), :] = up[...]
    for down, at in zip((down_0, down_1, down_2, down_3), down_at):
        down_ref[pl.ds(pl.multiple_of(at * DOWN_ROWS, 128), DOWN_ROWS), :] = down[...]
    here = pl.multiple_of(core * HALF, 128)
    there = pl.multiple_of((1 - core) * HALF, 128)
    own_o = own_o_ref[...]
    far_o = swap_halves(far_o_ref[...])
    for out_ref, at in ((own_out_ref, here), (far_out_ref, there)):
        part = dot_nn(own_o, out_ref[pl.ds(here, HALF), :]) + dot_nn(far_o, out_ref[pl.ds(there, HALF), :])
        h_ref[:, pl.ds(at, HALF)] = part
    hidden = x_ref[...].astype(F32) + (h_ref[...] + vec_ref[4:5, :])
    h_ref[...] = hidden
    unit, _ = normalised(hidden)
    a = (unit * vec_ref[5:6, :] + vec_ref[6:7, :]).astype(BF16)
    a = dot_nn(a, order_ref[...]).astype(BF16)
    g = g_ref[...]
    branch = jnp.zeros((ROWS, WIDTH), F32)
    grad_a = jnp.zeros((ROWS, WIDTH), F32)
    step = 512
    for i in range(UP // step):
        cols = pl.ds(i * step, step)
        up = up_ref[:, cols]
        down = down_ref[cols, :]
        u = dot_nn(a, up) + up_b_ref[:, cols]
        phi = 0.5 * (1.0 + lax.erf(u * (0.5**0.5)))
        z = (u * phi).astype(BF16)
        slope = phi + u * (jnp.exp(-0.5 * u * u) * (2.0 * jnp.pi) ** (-0.5))
        branch += dot_nn(z, down)
        gu = (dot_nt(g, down) * slope).astype(BF16)
        grad_down_ref[cols, :] = dot_tn(z, g).astype(BF16)
        grad_up_ref[:, cols] = dot_tn(a, gu).astype(BF16)
        grad_up_b_ref[:, cols] = total(gu)
        grad_a += dot_nt(gu, up)
    m_own_ref[...] = branch[:OWN] + hidden[:OWN] + vec_ref[7:8, :]
    m_far_ref[...] = branch[OWN:]
    high = grad_a.astype(BF16)
    low = (grad_a - high.astype(F32)).astype(BF16)
    grad_a_ref[...] = dot_nt(high, order_ref[...]) + dot_nt(low, order_ref[...])
    grad_down_b_ref[...] = total(g[:OWN])
    for part, at in zip((part_0, part_1, part_2, part_3), up_at):
        rows = pl.ds(pl.multiple_of(at * BLOCK, 64), BLOCK)
        part[0:BLOCK, :] = grad_up_ref[rows, pl.ds(0, WIDTH)]
        part[BLOCK : 2 * BLOCK, :] = grad_up_ref[rows, pl.ds(WIDTH, WIDTH)]
        for y in range(4):
            part[2 * BLOCK + 96 * y : 2 * BLOCK + 96 * (y + 1), :] = grad_down_ref[
                pl.ds(pl.multiple_of(DOWN_ROWS * y + 96 * at, 32), 96), :
            ]


def back_kernel(
    place_ref, x_ref, h_ref, g_ref, own_grad_ref, far_grad_ref, vec_ref, own_o_ref, far_o_ref, own_out_ref, far_out_ref,
    qkv_ref, lse_ref, a_ref, w_ref, down_b_ref, up_cols_ref,
    part_0, part_1, part_2, part_3, own_x_ref, far_x_ref, gh_ref,
    gh_low_ref, go_ref, gqkv_ref, rows_ref, message_ref,
):
    core = place_ref[0]
    here = pl.multiple_of(core * HALF, 128)
    there = pl.multiple_of((1 - core) * HALF, 128)
    rows_ref[...] = jnp.zeros((128, WIDTH), F32)
    grad_a = own_grad_ref[...] + swap_halves(far_grad_ref[...])
    unit, scale = normalised(h_ref[...])
    grad_h = g_ref[...].astype(F32) + norm_back(grad_a, unit, scale, vec_ref[5:6, :])
    gh_ref[...] = grad_h[:OWN]
    low = grad_h.astype(BF16)
    gh_low_ref[...] = low
    rows_ref[4:5, :] = total(low[:OWN])
    rows_ref[5:6, :] = total(grad_a[:OWN] * unit[:OWN])
    rows_ref[6:7, :] = total(grad_a[:OWN])
    rows_ref[7:8, :] = down_b_ref[...]
    low_here = gh_low_ref[:, pl.ds(here, HALF)]
    low_there = gh_low_ref[:, pl.ds(there, HALF)]
    rows = pl.ds(here, HALF)
    go_ref[...] = (dot_nt(low_here, own_out_ref[rows, :]) + dot_nt(low_there, far_out_ref[rows, :])).astype(BF16)
    outs = pl.ds(QKV + SMALL, HALF)
    message_ref[pl.ds(here, HALF), outs] = dot_tn(own_o_ref[...], low_here).astype(BF16)
    message_ref[pl.ds(there, HALF), outs] = dot_tn(swap_halves(far_o_ref[...]), low_here).astype(BF16)
    admitted, live = masks(core)
    live = jnp.where(live, 1.0, 0.0)
    lane = lax.broadcasted_iota(jnp.int32, (ROWS, 128), 1)
    for pair in range(3):
        query = qkv_ref[:, pl.ds(128 * pair, 128)]
        key = qkv_ref[:, pl.ds(HALF + 128 * pair, 128)]
        value = qkv_ref[:, pl.ds(2 * HALF + 128 * pair, 128)]
        go = go_ref[:, pl.ds(128 * pair, 128)]
        gq = jnp.zeros((ROWS, 128), F32)
        gk = jnp.zeros((ROWS, 128), F32)
        gv = jnp.zeros((ROWS, 128), F32)
        for j in range(2):
            only = head_lanes(j)
            lse = jnp.sum(jnp.where(lane == 2 * pair + j, lse_ref[...], 0.0), axis=-1, keepdims=True)
            scores = jnp.where(admitted, dot_nt(query * only, key) * SCALE, MASKED)
            probs = jnp.exp(scores - lse)
            grad_p = dot_nt(go * only, value)
            grad_s = probs * (grad_p - jnp.sum(probs * grad_p, axis=-1, keepdims=True))
            gq += dot_nn(grad_s.astype(BF16), key * only)
            gk += dot_tn((grad_s * live).astype(BF16), query * only)
            gv += dot_tn((probs * live).astype(BF16), go * only)
        gqkv_ref[:, pl.ds(128 * pair, 128)] = (gq * SCALE).astype(BF16)
        gqkv_ref[:, pl.ds(HALF + 128 * pair, 128)] = (gk * SCALE).astype(BF16)
        gqkv_ref[:, pl.ds(2 * HALF + 128 * pair, 128)] = gv.astype(BF16)
    gqkv = gqkv_ref[...]
    message_ref[:, pl.ds(0, QKV)] = dot_tn(a_ref[...], gqkv).astype(BF16)
    grad_x = dot_nt(gqkv, w_ref[...])
    own_x_ref[...] = grad_x[:OWN]
    far_x_ref[...] = grad_x[OWN:]
    unit, _ = normalised(x_ref[...].astype(F32))
    sums = total(gqkv)
    rows_ref[0:1, :] = total(grad_x * unit)
    rows_ref[1:2, :] = total(grad_x)
    rows_ref[2:3, pl.ds(here, HALF)] = sums[:, :HALF]
    rows_ref[3:4, pl.ds(here, HALF)] = sums[:, 2 * HALF :]
    full = rows_ref[0:8, :]
    high = full.astype(BF16).astype(F32)
    rows_ref[0:8, :] = high
    rows_ref[16:24, :] = full - high
    message_ref[:, pl.ds(QKV, SMALL)] = (rows_ref[...].T + up_cols_ref[...]).astype(BF16)
    for part, at in zip((part_0, part_1, part_2, part_3), positions(core, place_ref[1])):
        part[...] = message_ref[pl.ds(pl.multiple_of(at * BLOCK, 64), BLOCK), :]


def tokens_kernel(place_ref, x_ref, own_x_ref, far_x_ref, gh_ref, vec_ref, out_ref):
    unit, scale = normalised(x_ref[0:OWN, :].astype(F32))
    grad = own_x_ref[...] + far_x_ref[...]
    out_ref[...] = (gh_ref[...] + norm_back(grad, unit, scale, vec_ref[0:1, :])).astype(BF16)


def call(kernel, place, args, outs, scratch=()):
    specs = [pl.BlockSpec(memory_space=pltpu.VMEM)] * len(args)
    if place is not None:
        args = (place,) + tuple(args)
        specs = [pl.BlockSpec(memory_space=pltpu.SMEM)] + specs
    return pl.pallas_call(
        kernel,
        out_shape=tuple(jax.ShapeDtypeStruct(s, d) for s, d in outs),
        in_specs=specs,
        out_specs=tuple(pl.BlockSpec(memory_space=pltpu.VMEM) for _ in outs),
        scratch_shapes=[pltpu.VMEM(s, d) for s, d in scratch],
        compiler_params=pltpu.CompilerParams(vmem_limit_bytes=VMEM_LIMIT),
        cost_estimate=pl.CostEstimate(flops=1, bytes_accessed=1, transcendentals=0),
    )(*args)


def between_cores(values):
    return lax.ppermute(values, "c", [(0, 1), (1, 0)])


def between_chips(values):
    return lax.ppermute(values, "yl", [(0, 1), (1, 0)])


def swap_items(values):
    return lax.ppermute(values, ("c", "yl"), [(0, 0), (1, 2), (2, 1), (3, 3)])


def up_order():
    u = lax.optimization_barrier(jnp.arange(WIDTH, dtype=jnp.int32))
    z, x, yh, i = u // BLOCK, u % BLOCK // 48, u % 48 // 24, u % 24
    n = ((x * 2 + yh) * 4 + z) * 24 + i
    return (n[None, :] == lax.broadcasted_iota(jnp.int32, (WIDTH, WIDTH), 0)).astype(BF16)


def ring(values, axis, by):
    return lax.ppermute(values, axis, [(i, (i + by) % 4) for i in range(4)])


def ring_gather(block, axis):
    return [block, ring(block, axis, -1), ring(block, axis, 2), ring(block, axis, 1)]


def ring_order(blocks, at):
    return [lax.select_n(lax.rem(j - at + 4, 4), *blocks) for j in range(4)]


def ring_reduce(blocks, axis):
    got = [ring(blocks[1], axis, 1), ring(blocks[2], axis, 2), ring(blocks[3], axis, -1)]
    return sum((g.astype(F32) for g in got), blocks[0].astype(F32))


def ring_split(values, at, axis=0):
    size = values.shape[axis] // 4
    return [lax.dynamic_slice_in_dim(values, lax.rem(at + j, 4) * size, size, axis) for j in range(4)]


def along(axis, by):
    pairs = []
    for x, yh, z, c, yl in np.ndindex(*SIZES):
        at = {"x": x, "y": 2 * yh + yl, "z": z}
        at[axis] = (at[axis] + (by if c == 0 else -by)) % 4
        to = (at["x"], at["y"] // 2, at["z"], c, at["y"] % 2)
        pairs.append((int(np.ravel_multi_index((x, yh, z, c, yl), SIZES)), int(np.ravel_multi_index(to, SIZES))))
    return pairs


def send(values, axis, by):
    return lax.ppermute(values, AXES, along(axis, by))


def relay_gather(block, axis):
    behind = send(block, axis, 1)
    return [block, behind, send(block, axis, -1), send(behind, axis, 1)]


def relay_start(blocks, axis):
    return send(blocks[3], axis, 1), send(blocks[1], axis, -1)


def relay_end(blocks, got, axis):
    ahead = (blocks[2].astype(F32) + got[0].astype(F32)).astype(BF16)
    return blocks[0].astype(F32) + got[1].astype(F32) + send(ahead, axis, 1).astype(F32)


def by_place(place, first, second, axis=0):
    return jnp.where(
        place == 0, jnp.concatenate([first, second], axis), jnp.concatenate([second, first], axis)
    )


def other_half(values, place):
    rows = values.shape[0] // 2
    return (
        lax.dynamic_slice_in_dim(values, (1 - place) * rows, rows, 0),
        lax.dynamic_slice_in_dim(values, place * rows, rows, 0),
    )


def shards(
    tokens,
    segment_counts,
    ln1_gain,
    ln1_bias,
    w_qkv,
    q_bias,
    v_bias,
    w_out,
    out_bias,
    ln2_gain,
    ln2_bias,
    w_up,
    up_bias,
    w_down,
    down_bias,
    cotangent,
):
    core = lax.axis_index("c")
    x_at, z_at = lax.axis_index("x"), lax.axis_index("z")
    y_at = lax.axis_index(RING_Y)
    place = jnp.stack([core, x_at, y_at, z_at]).astype(jnp.int32)
    present = jnp.arange(SLOTS) < segment_counts[0]
    present_rows = jnp.repeat(present, HALFSEG)[:, None]
    cot = jnp.where(present_rows, cotangent.reshape(OWN, WIDTH), 0).astype(BF16)

    mine = swap_items(jnp.concatenate([tokens.reshape(OWN, WIDTH), cot], axis=1))
    downs = ring_gather(w_down, "x")
    (parts,) = call(
        halves_kernel,
        None,
        (
            w_qkv, w_out, w_up, ln1_gain, ln1_bias, q_bias, v_bias, out_bias, ln2_gain, ln2_bias, down_bias, up_bias,
        ),
        (((8, 6, ATTN + UP), BF16),),
        (((16, 128), F32), ((6, FF), F32), ((6, UP), F32)),
    )
    rows = lax.all_to_all(parts, EIGHT, 0, 0, tiled=True).reshape(2, 24, ATTN + UP)
    attn, ups = rows[:, :, :ATTN], rows[:, :, ATTN:].reshape(48, UP)
    downs = jnp.concatenate(ring_order(downs, x_at), axis=0)

    attn = ring_gather(attn, "z")
    ups = ring_gather(ups, "x")
    *attn, downs = lax.optimization_barrier((*attn, downs))
    downs = ring_gather(downs, "z")
    item = jnp.concatenate([mine, between_cores(mine)], axis=0)
    x, g = item[:, :WIDTH], item[:, WIDTH:]
    attn = jnp.concatenate(ring_order(attn, z_at), axis=1).reshape(BLOCK, ATTN)
    ups = jnp.concatenate(ring_order(ups, x_at), axis=0)
    downs = jnp.concatenate(ring_order(downs, z_at), axis=0)

    attn = relay_gather(attn, "x")
    ups = relay_gather(ups, "z")
    downs = relay_gather(downs, "y")

    a1, qkv, own_o, lse, w_in, own_out, small_all, vectors = call(
        attend_kernel,
        place,
        (x, *attn),
        (
            ((ROWS, WIDTH), BF16),
            ((ROWS, QKV), BF16),
            ((ROWS, HALF), BF16),
            ((ROWS, 128), F32),
            ((WIDTH, QKV), BF16),
            ((WIDTH, HALF), BF16),
            ((WIDTH, SMALL), BF16),
            ((16, WIDTH), F32),
        ),
    )
    far_o, far_out = between_cores(own_o), between_cores(own_out)
    up_b = small_all[:, 8:12].reshape(4, 2, 4, 2, 2, 24)
    up_b = lax.dynamic_index_in_dim(up_b, core, 3, keepdims=False)
    up_b = up_b.transpose(1, 3, 2, 0, 4).reshape(1, UP).astype(F32)
    hidden, m_own, m_far, grad_a_own, grad_up_b, grad_down_b, *grads = call(
        mlp_kernel,
        place,
        (x, own_o, far_o, own_out, far_out, vectors, up_b, g, up_order(), *ups, *downs),
        (
            ((ROWS, WIDTH), F32),
            ((OWN, WIDTH), F32),
            ((OWN, WIDTH), F32),
            ((ROWS, WIDTH), F32),
            ((1, UP), F32),
            ((1, WIDTH), F32),
        )
        + (((2 * BLOCK + DOWN_ROWS, WIDTH), BF16),) * 4,
        (((WIDTH, UP), BF16), ((UP, WIDTH), BF16), ((WIDTH, UP), BF16), ((UP, WIDTH), BF16)),
    )
    grad_a_far = between_cores(grad_a_own)
    grad_a_far, *grads = lax.optimization_barrier((grad_a_far, *grads))
    got = relay_start(grads, "z")
    block = swap_items((m_own + between_cores(m_far)).astype(BF16))
    block_out = jnp.where(present_rows, block, 0).reshape(tokens.shape)
    up_cols = grad_up_b.reshape(2, 2, 4, 4, 24).transpose(3, 0, 2, 1, 4)[:, :, :, None]
    up_cols = jnp.where((jnp.arange(2) == core)[:, None, None], up_cols, 0.0).reshape(WIDTH, 4)
    up_high = up_cols.astype(BF16).astype(F32)
    up_cols = jnp.pad(up_high, ((0, 0), (8, SMALL - 12))) + jnp.pad(up_cols - up_high, ((0, 0), (24, SMALL - 28)))

    *grad_attn, own_x, far_x, gh = call(
        back_kernel,
        place,
        (
            x, hidden, g, grad_a_own, grad_a_far, vectors, own_o, far_o, own_out, far_out, qkv, lse, a1, w_in,
            grad_down_b, up_cols,
        ),
        (((BLOCK, ATTN), BF16),) * 4 + (((OWN, WIDTH), F32),) * 3,
        (
            ((ROWS, WIDTH), BF16),
            ((ROWS, HALF), BF16),
            ((ROWS, QKV), BF16),
            ((128, WIDTH), F32),
            ((WIDTH, ATTN), BF16),
        ),
    )
    (grad_x,) = call(
        tokens_kernel, place, (x, own_x, between_cores(far_x), gh, vectors), (((OWN, WIDTH), BF16),)
    )
    grad_x = swap_items(grad_x)

    attn_sum = relay_end(grad_attn, relay_start(grad_attn, "x"), "x").astype(BF16).reshape(2, 4, 24, ATTN)
    attn_sum = ring_reduce([a[:, 0] for a in ring_split(attn_sum, z_at, 1)], "z")
    mlp_sum = relay_end(grads, got, "z").astype(BF16)
    up_parts = ring_split(mlp_sum[: 2 * BLOCK].reshape(2, 4, 48, WIDTH), x_at, 1)
    down_parts = ring_split(mlp_sum[2 * BLOCK :].reshape(4, 4, 24, WIDTH), x_at, 1)
    mlp_sum = ring_reduce(
        [jnp.concatenate([u.reshape(96, WIDTH), d.reshape(96, WIDTH)]) for u, d in zip(up_parts, down_parts)], "x"
    )
    up_sum = jnp.concatenate([mlp_sum[:48], mlp_sum[48:96]], axis=1).reshape(2, 24, UP)
    down_sum = ring_reduce(ring_split(mlp_sum[96:].astype(BF16), y_at), RING_Y)
    sums = jnp.concatenate([attn_sum.astype(BF16), up_sum.astype(BF16)], axis=2)
    got = lax.all_to_all(sums.reshape(8, 6, ATTN + UP), EIGHT, 0, 0, tiled=True)
    out_qkv, out_out, out_up, out_down, grad_tokens, *vecs, out_up_b = call(
        outputs_kernel,
        None,
        (got, down_sum, grad_x),
        (
            ((6, 3 * WIDTH), F32),
            ((6, WIDTH), F32),
            ((6, FF), F32),
            ((24, WIDTH), F32),
            ((OWN, WIDTH), BF16),
        )
        + (((6,), F32),) * 8
        + (((24,), F32),),
        (((128, 128), F32),),
    )
    gain_1, bias_1, bias_q, bias_v, bias_out, gain_2, bias_2, bias_down = vecs
    return (
        block_out,
        grad_tokens.reshape(tokens.shape),
        gain_1,
        bias_1,
        out_qkv,
        bias_q,
        bias_v,
        out_out,
        bias_out,
        gain_2,
        bias_2,
        out_up,
        out_up_b,
        out_down,
        bias_down,
    )


def solution(mesh):
    torus = Mesh(np.asarray(mesh.devices).reshape(SIZES), AXES)
    items = P(("x", "yh", "z", "c"), None, "yl", None)
    part, rows = P(AXES), P(AXES, None)
    return jax.shard_map(
        shards,
        mesh=torus,
        in_specs=(
            items, P(("x", "yh", "z", "c")), part, part, rows, part, part, rows, part, part, part, rows, part, rows,
            part, items,
        ),
        out_specs=(
            items, items, part, part, rows, part, part, rows, part, part, part, rows, part, rows, part,
        ),
        check_vma=False,
    )
```

profile of v0, /device:TPU:1, one launch (start us, length us, event | category | flops | bytes accessed | tf_op | source)
XLA Modules:
  0.0 187.4 jit_solution(8472551799807438529)
XLA Ops:
  0.7 3.4 %collective-permute-start.5 = (bf16[24,768]{1,0:T(8,128)(2,1)}, bf16[24,768]{1,0:T(8,128)(2,1)S(1)}, u32[]{:S(2)}, u32[]{:S(2)}) collective-permute-start(bf16[24,768]{1,0:T(8,128)(2,1)} %param.29), channel_id=1, source_target_pairs={{0,96},{32,0},{64,32},{96,64},{1,97},{33,1},{65,33},{97,65},{2,98}... | collective-permute-start | bytes 110600 | tf_op jit(solution)/shard_map/ppermute | solution.py:374
  5.2 1.9 %shard_map.271 = bf16[8,6,3200]{2,1,0:T(8,128)(2,1)} custom-call(bf16[6,2304]{1,0:T(8,128)(2,1)} %qkv_ref.1, bf16[6,768]{1,0:T(8,128)(2,1)} %out_ref.1, bf16[6,3072]{1,0:T(8,128)(2,1)} %up_ref.1, bf16[6]{0:T(256)(128)(2,1)} %refs_0_.1, bf16[6]{0:T(256)(128)(2,1)} %refs_1_.1, bf16[6]{0:T(256)(128)(2,1)} %refs_2_.1, bf16[6]{0:T(256)(128)(2,1)} %refs_3_.1, ...), custom_call_target="tpu_custom_call" | custom-call | flops 1 | bytes 1 | tf_op jit(solution)/shard_map/pallas_call | solution.py:343
  7.1 6.0 %all-to-all-start = ((bf16[8,6,3200]{2,1,0:T(8,128)(2,1)}), bf16[8,6,3200]{2,1,0:T(8,128)(2,1)S(1)}, u32[]{:S(2)}, u32[]{:S(2)}) async-start(bf16[8,6,3200]{2,1,0:T(8,128)(2,1)} %shard_map.271), calls=%async_computation | async-start | bytes 819200 | tf_op jit(solution)/shard_map/all_to_all | solution.py:474
  14.0 3.5 %collective-permute-start = (bf16[128,1536]{1,0:T(8,128)(2,1)S(1)}, bf16[128,1536]{1,0:T(8,128)(2,1)S(1)}, u32[]{:S(2)}, u32[]{:S(2)}) collective-permute-start(bf16[128,1536]{1,0:T(8,128)(2,1)S(1)} %pad_maximum_fusion.3), channel_id=1, source_target_pairs={{0,0},{1,2},{2,1},{3,3},{4,4},{5,6},{6,5},{7,7},{8,8},{9,10},{10,9... | collective-permute-start | bytes 1179656 | tf_op jit(solution)/shard_map/ppermute | solution.py:363
  18.2 3.1 %all-to-all-done = bf16[8,6,3200]{2,1,0:T(8,128)(2,1)S(1)} async-done(((bf16[8,6,3200]{2,1,0:T(8,128)(2,1)}), bf16[8,6,3200]{2,1,0:T(8,128)(2,1)S(1)}, u32[]{:S(2)}, u32[]{:S(2)}) %all-to-all-start) | async-done | bytes 307232 | tf_op jit(solution)/shard_map/all_to_all | solution.py:474
  21.5 3.8 %collective-permute-start.2 = (bf16[2,24,1664]{2,1,0:T(8,128)(2,1)S(1)}, bf16[2,24,1664]{2,1,0:T(8,128)(2,1)S(1)}, u32[]{:S(2)}, u32[]{:S(2)}) collective-permute-start(bf16[2,24,1664]{2,1,0:T(8,128)(2,1)S(1)} %slice.44), channel_id=1, source_target_pairs={{0,12},{4,0},{8,4},{12,8},{1,13},{5,1},{9,5},{13,9},{2,14},{6,2},{... | collective-permute-start | bytes 479240 | tf_op jit(solution)/shard_map/ppermute | solution.py:374
  26.1 2.1 %collective-permute-start.13 = (bf16[48,1536]{1,0:T(8,128)(2,1)S(1)}, bf16[48,1536]{1,0:T(8,128)(2,1)S(1)}, u32[]{:S(2)}, u32[]{:S(2)}) collective-permute-start(bf16[48,1536]{1,0:T(8,128)(2,1)S(1)} %bitcast.71), channel_id=1, source_target_pairs={{0,96},{32,0},{64,32},{96,64},{1,97},{33,1},{65,33},{97,65},{2,98}... | collective-permute-start | bytes 442376 | tf_op jit(solution)/shard_map/ppermute | solution.py:374
  29.5 1.9 collective-permute-done.2
  31.3 1.5 collective-permute-start.15
  32.8 2.3 %collective-permute-start.1 = (bf16[128,1536]{1,0:T(8,128)(2,1)S(1)}, bf16[128,1536]{1,0:T(8,128)(2,1)S(1)}, u32[]{:S(2)}, u32[]{:S(2)}) collective-permute-start(bf16[128,1536]{1,0:T(8,128)(2,1)S(1)} %collective-permute-done), channel_id=1, source_target_pairs={{0,2},{2,0},{1,3},{3,1},{4,6},{6,4},{5,7},{7,5},{8,10},{10,8},{9,1... | collective-permute-start | bytes 1179656 | tf_op jit(solution)/shard_map/ppermute | solution.py:355
  35.9 2.1 %collective-permute-start.8 = (bf16[192,1664]{1,0:T(8,128)(2,1)S(1)}, bf16[192,1664]{1,0:T(8,128)(2,1)S(1)}, u32[]{:S(2)}, u32[]{:S(2)}) collective-permute-start(bf16[192,1664]{1,0:T(8,128)(2,1)S(1)} %bitcast.64), channel_id=1, source_target_pairs={{0,32},{1,33},{2,98},{3,99},{4,36},{5,37},{6,102},{7,103},{8,40},{... | collective-permute-start | bytes 1916936 | tf_op jit(solution)/shard_map/ppermute | solution.py:406
  40.9 2.4 %collective-permute-done.19 = bf16[96,768]{1,0:T(8,128)(2,1)S(1)} collective-permute-done((bf16[96,768]{1,0:T(8,128)(2,1)S(1)}, bf16[96,768]{1,0:T(8,128)(2,1)S(1)}, u32[]{:S(2)}, u32[]{:S(2)}) %collective-permute-start.19) | collective-permute-done | bytes 147488 | tf_op jit(solution)/shard_map/ppermute | solution.py:374
  43.4 2.3 %collective-permute-start.16 = (bf16[192,1536]{1,0:T(8,128)(2,1)S(1)}, bf16[192,1536]{1,0:T(8,128)(2,1)}, u32[]{:S(2)}, u32[]{:S(2)}) collective-permute-start(bf16[192,1536]{1,0:T(8,128)(2,1)S(1)} %pad_maximum_fusion.1.up_0), channel_id=1, source_target_pairs={{0,4},{1,5},{2,14},{3,15},{4,8},{5,9},{6,2},{7,3},{8,12},{9,13},{1... | collective-permute-start | bytes 1769480 | tf_op jit(solution)/shard_map/ppermute | solution.py:406
  47.5 1.5 collective-permute-start.22
  48.9 1.7 collective-permute-start.10
  52.0 2.5 %collective-permute-done.16.up_1 = bf16[192,1536]{1,0:T(8,128)(2,1)} collective-permute-done((bf16[192,1536]{1,0:T(8,128)(2,1)S(1)}, bf16[192,1536]{1,0:T(8,128)(2,1)}, u32[]{:S(2)}, u32[]{:S(2)}) %collective-permute-start.16) | collective-permute-done | bytes 589856 | tf_op jit(solution)/shard_map/ppermute | solution.py:406
  54.5 2.2 %collective-permute-done.9.part_2 = bf16[192,1664]{1,0:T(8,128)(2,1)S(1)} collective-permute-done((bf16[192,1664]{1,0:T(8,128)(2,1)S(1)}, bf16[192,1664]{1,0:T(8,128)(2,1)S(1)}, u32[]{:S(2)}, u32[]{:S(2)}) %collective-permute-start.9) | collective-permute-done | bytes 639008 | tf_op jit(solution)/shard_map/ppermute | solution.py:406
  56.7 3.8 %collective-permute-start.18 = (bf16[192,1536]{1,0:T(8,128)(2,1)}, bf16[192,1536]{1,0:T(8,128)(2,1)}, u32[]{:S(2)}, u32[]{:S(2)}) collective-permute-start(bf16[192,1536]{1,0:T(8,128)(2,1)} %collective-permute-done.16.up_1), channel_id=1, source_target_pairs={{0,4},{1,5},{2,14},{3,15},{4,8},{5,9},{6,2},{7,3},{8,12},{9,13},{1... | collective-permute-start | bytes 1769480 | tf_op jit(solution)/shard_map/ppermute | solution.py:406
  60.5 3.6 %collective-permute-done.10.part_3 = bf16[192,1664]{1,0:T(8,128)(2,1)S(1)} collective-permute-done((bf16[192,1664]{1,0:T(8,128)(2,1)S(1)}, bf16[192,1664]{1,0:T(8,128)(2,1)S(1)}, u32[]{:S(2)}, u32[]{:S(2)}) %collective-permute-start.10) | collective-permute-done | bytes 639008 | tf_op jit(solution)/shard_map/ppermute | solution.py:406
  64.9 5.6 %shard_map.272 = (bf16[256,768]{1,0:T(8,128)(2,1)}, bf16[256,1152]{1,0:T(8,128)(2,1)}, bf16[256,384]{1,0:T(8,128)(2,1)}, f32[256,128]{1,0:T(8,128)}, bf16[768,11...) custom-call(s32[4]{0:T(128)} %pad_add_fusion.1.place_ref, ...), custom_call_target="tpu_custom_call" | custom-call | flops 1 | bytes 1 | tf_op jit(solution)/shard_map/pallas_call | solution.py:343
  70.6 4.4 %collective-permute-start.12 = (bf16[768,384]{1,0:T(8,128)(2,1)}, bf16[768,384]{1,0:T(8,128)(2,1)S(1)}, u32[]{:S(2)}, u32[]{:S(2)}) collective-permute-start(bf16[768,384]{1,0:T(8,128)(2,1)} %get-tuple-element.69.own_out_ref), channel_id=1, source_target_pairs={{0,2},{2,0},{1,3},{3,1},{4,6},{6,4},{5,7},{7,5},{8,10},{10,8},{9,1... | collective-permute-start | bytes 1769480 | tf_op jit(solution)/shard_map/ppermute | solution.py:355
  75.1 1.4 fusion.order_ref
  78.5 12.3 %shard_map.273 = (f32[256,768]{1,0:T(8,128)}, f32[128,768]{1,0:T(8,128)}, f32[128,768]{1,0:T(8,128)}, f32[256,768]{1,0:T(8,128)}, f32[1,1536]{1,0:T(1,128)}, /*i...) custom-call(s32[4]{0:T(128)} %pad_add_fusion.1.place_ref, ...), custom_call_target="tpu_custom_call" | custom-call | flops 1 | bytes 1 | tf_op jit(solution)/shard_map/pallas_call | solution.py:343
  90.8 2.1 %collective-permute-start.27 = (f32[256,768]{1,0:T(8,128)}, f32[256,768]{1,0:T(8,128)S(1)}, u32[]{:S(2)}, u32[]{:S(2)}) collective-permute-start(f32[256,768]{1,0:T(8,128)} %get-tuple-element.76.own_grad_ref), channel_id=1, source_target_pairs={{0,2},{2,0},{1,3},{3,1},{4,6},{6,4},{5,7},{7,5},{8,10},{10,8},{9,1... | collective-permute-start | bytes 2359304 | tf_op jit(solution)/shard_map/ppermute | solution.py:355
  96.6 9.3 %shard_map.274 = (bf16[192,1664]{1,0:T(8,128)(2,1)}, bf16[192,1664]{1,0:T(8,128)(2,1)}, bf16[192,1664]{1,0:T(8,128)(2,1)}, bf16[192,1664]{1,0:T(8,128)(2,1)}, f3...) custom-call(s32[4]{0:T(128)} %pad_add_fusion.1.place_ref, bf16[256,768]{1,0:T(8,128)(2,1)} %get-tuple-element.116.x_ref, ...), custom_call_target="tpu_custom_call" | custom-call | flops 1 | bytes 1 | tf_op jit(solution)/shard_map/pallas_call | solution.py:343
  105.9 3.0 %collective-permute-start.29 = (bf16[192,1664]{1,0:T(8,128)(2,1)}, bf16[192,1664]{1,0:T(8,128)(2,1)S(1)}, u32[]{:S(2)}, u32[]{:S(2)}) collective-permute-start(bf16[192,1664]{1,0:T(8,128)(2,1)} %get-tuple-element.91), channel_id=1, source_target_pairs={{0,32},{1,33},{2,98},{3,99},{4,36},{5,37},{6,102},{7,103},{8,40},{... | collective-permute-start | bytes 1916936 | tf_op jit(solution)/shard_map/ppermute | solution.py:406
  108.9 10.8 %collective-permute-done.29 = bf16[192,1664]{1,0:T(8,128)(2,1)S(1)} collective-permute-done((bf16[192,1664]{1,0:T(8,128)(2,1)}, bf16[192,1664]{1,0:T(8,128)(2,1)S(1)}, u32[]{:S(2)}, u32[]{:S(2)}) %collective-permute-start.29) | collective-permute-done | bytes 639008 | tf_op jit(solution)/shard_map/ppermute | solution.py:406
  119.7 2.1 %add_convert_fusion.3 = bf16[192,1664]{1,0:T(8,128)(2,1)} fusion(bf16[192,1664]{1,0:T(8,128)(2,1)S(1)} %collective-permute-done.29, bf16[192,1664]{1,0:T(8,128)(2,1)} %get-tuple-element.90), kind=kLoop, calls=%fused_computation.5 | loop fusion | flops 1277952 | bytes 1916928 | tf_op jit(solution)/shard_map/convert_element_type | solution.py:419
  121.7 3.4 %collective-permute-start.30 = (bf16[192,1664]{1,0:T(8,128)(2,1)}, bf16[192,1664]{1,0:T(8,128)(2,1)}, u32[]{:S(2)}, u32[]{:S(2)}) collective-permute-start(bf16[192,1664]{1,0:T(8,128)(2,1)} %add_convert_fusion.3), channel_id=1, source_target_pairs={{0,32},{1,33},{2,98},{3,99},{4,36},{5,37},{6,102},{7,103},{8,40},{... | collective-permute-start | bytes 1916936 | tf_op jit(solution)/shard_map/ppermute | solution.py:406
  125.8 1.9 %add_convert_fusion.5 = bf16[128,768]{1,0:T(8,128)(2,1)} fusion(f32[128,768]{1,0:T(8,128)} %get-tuple-element.73, f32[128,768]{1,0:T(8,128)} %collective-permute-done.25), kind=kLoop, calls=%fused_computation.12 | loop fusion | flops 196608 | bytes 983040 | tf_op jit(solution)/shard_map/convert_element_type | solution.py:529
  127.7 1.9 %collective-permute-start.26 = (bf16[128,768]{1,0:T(8,128)(2,1)}, bf16[128,768]{1,0:T(8,128)(2,1)}, u32[]{:S(2)}, u32[]{:S(2)}) collective-permute-start(bf16[128,768]{1,0:T(8,128)(2,1)} %add_convert_fusion.5), channel_id=1, source_target_pairs={{0,0},{1,2},{2,1},{3,3},{4,4},{5,6},{6,5},{7,7},{8,8},{9,10},{10,9... | collective-permute-start | bytes 589832 | tf_op jit(solution)/shard_map/ppermute | solution.py:363
  129.7 2.8 %collective-permute-start.43 = (f32[128,768]{1,0:T(8,128)}, f32[128,768]{1,0:T(8,128)}, u32[]{:S(2)}, u32[]{:S(2)}) collective-permute-start(f32[128,768]{1,0:T(8,128)} %get-tuple-element.97), channel_id=1, source_target_pairs={{0,2},{2,0},{1,3},{3,1},{4,6},{6,4},{5,7},{7,5},{8,10},{10,8},{9,1... | collective-permute-start | bytes 1179656 | tf_op jit(solution)/shard_map/ppermute | solution.py:355
  132.8 1.6 add_convert_fusion.2
  134.5 1.3 collective-permute-start.31
  135.8 2.5 %collective-permute-start.32 = (bf16[2,24,1664]{2,1,0:T(8,128)(2,1)S(1)}, bf16[2,24,1664]{2,1,0:T(8,128)(2,1)S(1)}, u32[]{:S(2)}, u32[]{:S(2)}) collective-permute-start(bf16[2,24,1664]{2,1,0:T(8,128)(2,1)S(1)} %get-tuple-element.119), channel_id=1, source_target_pairs={{0,8},{4,12},{8,0},{12,4},{1,9},{5,13},{9,1},{13,5},{2,10},{6,14},... | collective-permute-start | bytes 479240 | tf_op jit(solution)/shard_map/ppermute | solution.py:374
  138.3 2.6 %collective-permute-done.36 = bf16[768,768]{1,0:T(8,128)(2,1)S(1)} collective-permute-done((bf16[768,768]{1,0:T(8,128)(2,1)S(1)}, bf16[768,768]{1,0:T(8,128)(2,1)S(1)}, u32[]{:S(2)}, u32[]{:S(2)}) %collective-permute-start.36) | collective-permute-done | bytes 1179680 | tf_op jit(solution)/shard_map/ppermute | solution.py:406
  143.0 3.2 %collective-permute-done.32 = bf16[2,24,1664]{2,1,0:T(8,128)(2,1)S(1)} collective-permute-done((bf16[2,24,1664]{2,1,0:T(8,128)(2,1)S(1)}, bf16[2,24,1664]{2,1,0:T(8,128)(2,1)S(1)}, u32[]{:S(2)}, u32[]{:S(2)}) %collective-permute-start.32) | collective-permute-done | bytes 159776 | tf_op jit(solution)/shard_map/ppermute | solution.py:374
  146.2 1.8 collective-permute-start.38
  148.4 2.8 %collective-permute-done.37 = bf16[192,768]{1,0:T(8,128)(2,1)S(1)} collective-permute-done((bf16[192,768]{1,0:T(8,128)(2,1)S(1)}, bf16[192,768]{1,0:T(8,128)(2,1)S(1)}, u32[]{:S(2)}, u32[]{:S(2)}) %collective-permute-start.37) | collective-permute-done | bytes 294944 | tf_op jit(solution)/shard_map/ppermute | solution.py:374
  151.1 5.2 %collective-permute-done.38 = bf16[192,768]{1,0:T(8,128)(2,1)S(1)} collective-permute-done((bf16[192,768]{1,0:T(8,128)(2,1)S(1)}, bf16[192,768]{1,0:T(8,128)(2,1)S(1)}, u32[]{:S(2)}, u32[]{:S(2)}) %collective-permute-start.38) | collective-permute-done | bytes 294944 | tf_op jit(solution)/shard_map/ppermute | solution.py:374
  156.5 3.3 %collective-permute-start.40 = (bf16[24,768]{1,0:T(8,128)(2,1)S(1)}, bf16[24,768]{1,0:T(8,128)(2,1)S(1)}, u32[]{:S(2)}, u32[]{:S(2)}) collective-permute-start(bf16[24,768]{1,0:T(8,128)(2,1)S(1)} %get-tuple-element.144), channel_id=1, source_target_pairs={{0,1},{1,16},{16,17},{17,0},{2,3},{3,18},{18,19},{19,2},{4,5},{5,2... | collective-permute-start | bytes 110600 | tf_op jit(solution)/shard_map/ppermute | solution.py:374
  159.9 2.5 %collective-permute-start.42 = (bf16[24,768]{1,0:T(8,128)(2,1)S(1)}, bf16[24,768]{1,0:T(8,128)(2,1)S(1)}, u32[]{:S(2)}, u32[]{:S(2)}) collective-permute-start(bf16[24,768]{1,0:T(8,128)(2,1)S(1)} %get-tuple-element.145), channel_id=1, source_target_pairs={{0,17},{1,0},{16,1},{17,16},{2,19},{3,2},{18,3},{19,18},{4,21},{5,... | collective-permute-start | bytes 110600 | tf_op jit(solution)/shard_map/ppermute | solution.py:374
  163.3 9.1 %all-to-all-start.1 = ((bf16[8,6,3200]{2,1,0:T(8,128)(2,1)}), bf16[8,6,3200]{2,1,0:T(8,128)(2,1)S(1)}, u32[]{:S(2)}, u32[]{:S(2)}) async-start(bf16[8,6,3200]{2,1,0:T(8,128)(2,1)} %reshape.141), calls=%async_computation.1 | async-start | bytes 819200 | tf_op jit(solution)/shard_map/all_to_all | solution.py:568
  172.4 1.7 broadcast_select_fusion
  174.1 2.4 %shard_map.275 = bf16[128,768]{1,0:T(8,128)(2,1)} custom-call(s32[4]{0:T(128)} %pad_add_fusion.1.place_ref, bf16[256,768]{1,0:T(8,128)(2,1)} %get-tuple-element.116.x_ref, f32[128,768]{1,0:T(8,128)} %get-tuple-element.96.own_x_ref, f32[128,768]{1,0:T(8,128)} %collective-permute-done.43.far_x_ref, f32[128,768]{1,0:T(8,128)} %get-tuple-element.98.gh_ref, ...), custom_call_target="tpu_custom_call" | custom-call | flops 1 | bytes 1 | tf_op jit(solution)/shard_map/pallas_call | solution.py:343
  176.5 3.5 %collective-permute-start.44 = (bf16[128,768]{1,0:T(8,128)(2,1)}, bf16[128,768]{1,0:T(8,128)(2,1)S(1)}, u32[]{:S(2)}, u32[]{:S(2)}) collective-permute-start(bf16[128,768]{1,0:T(8,128)(2,1)} %shard_map.275), channel_id=1, source_target_pairs={{0,0},{1,2},{2,1},{3,3},{4,4},{5,6},{6,5},{7,7},{8,8},{9,10},{10,9... | collective-permute-start | bytes 589832 | tf_op jit(solution)/shard_map/ppermute | solution.py:363
  180.7 3.0 %collective-permute-done.44.tokens_ref = bf16[128,768]{1,0:T(8,128)(2,1)S(1)} collective-permute-done((bf16[128,768]{1,0:T(8,128)(2,1)}, bf16[128,768]{1,0:T(8,128)(2,1)S(1)}, u32[]{:S(2)}, u32[]{:S(2)}) %collective-permute-start.44) | collective-permute-done | bytes 196640 | tf_op jit(solution)/shard_map/ppermute | solution.py:363
  185.1 2.0 %shard_map.276 = (f32[6,2304]{1,0:T(8,128)}, f32[6,768]{1,0:T(8,128)}, f32[6,3072]{1,0:T(8,128)}, f32[24,768]{1,0:T(8,128)}, bf16[128,768]{1,0:T(8,128)(2,1)}, /...) custom-call(bf16[8,6,3200]{2,1,0:T(8,128)(2,1)} %copy-done.4, ...), custom_call_target="tpu_custom_call" | custom-call | flops 1 | bytes 1 | tf_op jit(solution)/shard_map/pallas_call | solution.py:343
  (148 shorter events, 24.1 us)
Async XLA Ops:
  0.7 24.6 %collective-permute-start.5 = (bf16[24,768]{1,0:T(8,128)(2,1)}, bf16[24,768]{1,0:T(8,128)(2,1)S(1)}, u32[]{:S(2)}, u32[]{:S(2)}) collective-permute-start(bf16[24,768]{1,0:T(8,128)(2,1)} %param.29), channel_id=1, source_target_pairs={{0,96},{32,0},{64,32},{96,64},{1,97},{33,1},{65,33},{97,65},{2,98}... | collective-permute-start | bytes 110600 | tf_op jit(solution)/shard_map/ppermute | solution.py:374
  4.0 21.2 %collective-permute-start.6 = (bf16[24,768]{1,0:T(8,128)(2,1)}, bf16[24,768]{1,0:T(8,128)(2,1)S(1)}, u32[]{:S(2)}, u32[]{:S(2)}) collective-permute-start(bf16[24,768]{1,0:T(8,128)(2,1)} %param.29), channel_id=1, source_target_pairs={{0,64},{32,96},{64,0},{96,32},{1,65},{33,97},{65,1},{97,33},{2,66}... | collective-permute-start | bytes 110600 | tf_op jit(solution)/shard_map/ppermute | solution.py:374
  4.6 21.4 %collective-permute-start.7 = (bf16[24,768]{1,0:T(8,128)(2,1)}, bf16[24,768]{1,0:T(8,128)(2,1)S(1)}, u32[]{:S(2)}, u32[]{:S(2)}) collective-permute-start(bf16[24,768]{1,0:T(8,128)(2,1)} %param.29), channel_id=1, source_target_pairs={{0,32},{32,64},{64,96},{96,0},{1,33},{33,65},{65,97},{97,1},{2,34}... | collective-permute-start | bytes 110600 | tf_op jit(solution)/shard_map/ppermute | solution.py:374
  7.1 14.2 %all-to-all-start = ((bf16[8,6,3200]{2,1,0:T(8,128)(2,1)}), bf16[8,6,3200]{2,1,0:T(8,128)(2,1)S(1)}, u32[]{:S(2)}, u32[]{:S(2)}) async-start(bf16[8,6,3200]{2,1,0:T(8,128)(2,1)} %shard_map.271), calls=%async_computation | async-start | bytes 819200 | tf_op jit(solution)/shard_map/all_to_all | solution.py:474
  14.0 14.2 %collective-permute-start = (bf16[128,1536]{1,0:T(8,128)(2,1)S(1)}, bf16[128,1536]{1,0:T(8,128)(2,1)S(1)}, u32[]{:S(2)}, u32[]{:S(2)}) collective-permute-start(bf16[128,1536]{1,0:T(8,128)(2,1)S(1)} %pad_maximum_fusion.3), channel_id=1, source_target_pairs={{0,0},{1,2},{2,1},{3,3},{4,4},{5,6},{6,5},{7,7},{8,8},{9,10},{10,9... | collective-permute-start | bytes 1179656 | tf_op jit(solution)/shard_map/ppermute | solution.py:363
  21.5 9.8 %collective-permute-start.2 = (bf16[2,24,1664]{2,1,0:T(8,128)(2,1)S(1)}, bf16[2,24,1664]{2,1,0:T(8,128)(2,1)S(1)}, u32[]{:S(2)}, u32[]{:S(2)}) collective-permute-start(bf16[2,24,1664]{2,1,0:T(8,128)(2,1)S(1)} %slice.44), channel_id=1, source_target_pairs={{0,12},{4,0},{8,4},{12,8},{1,13},{5,1},{9,5},{13,9},{2,14},{6,2},{... | collective-permute-start | bytes 479240 | tf_op jit(solution)/shard_map/ppermute | solution.py:374
  25.3 7.5 %collective-permute-start.3 = (bf16[2,24,1664]{2,1,0:T(8,128)(2,1)S(1)}, bf16[2,24,1664]{2,1,0:T(8,128)(2,1)S(1)}, u32[]{:S(2)}, u32[]{:S(2)}) collective-permute-start(bf16[2,24,1664]{2,1,0:T(8,128)(2,1)S(1)} %slice.44), channel_id=1, source_target_pairs={{0,8},{4,12},{8,0},{12,4},{1,9},{5,13},{9,1},{13,5},{2,10},{6,14},... | collective-permute-start | bytes 479240 | tf_op jit(solution)/shard_map/ppermute | solution.py:374
  25.3 10.4 %collective-permute-start.4 = (bf16[2,24,1664]{2,1,0:T(8,128)(2,1)S(1)}, bf16[2,24,1664]{2,1,0:T(8,128)(2,1)S(1)}, u32[]{:S(2)}, u32[]{:S(2)}) collective-permute-start(bf16[2,24,1664]{2,1,0:T(8,128)(2,1)S(1)} %slice.44), channel_id=1, source_target_pairs={{0,4},{4,8},{8,12},{12,0},{1,5},{5,9},{9,13},{13,1},{2,6},{6,10},{... | collective-permute-start | bytes 479240 | tf_op jit(solution)/shard_map/ppermute | solution.py:374
  26.1 12.0 %collective-permute-start.13 = (bf16[48,1536]{1,0:T(8,128)(2,1)S(1)}, bf16[48,1536]{1,0:T(8,128)(2,1)S(1)}, u32[]{:S(2)}, u32[]{:S(2)}) collective-permute-start(bf16[48,1536]{1,0:T(8,128)(2,1)S(1)} %bitcast.71), channel_id=1, source_target_pairs={{0,96},{32,0},{64,32},{96,64},{1,97},{33,1},{65,33},{97,65},{2,98}... | collective-permute-start | bytes 442376 | tf_op jit(solution)/shard_map/ppermute | solution.py:374
  28.2 9.8 %collective-permute-start.14 = (bf16[48,1536]{1,0:T(8,128)(2,1)S(1)}, bf16[48,1536]{1,0:T(8,128)(2,1)S(1)}, u32[]{:S(2)}, u32[]{:S(2)}) collective-permute-start(bf16[48,1536]{1,0:T(8,128)(2,1)S(1)} %bitcast.72), channel_id=1, source_target_pairs={{0,64},{32,96},{64,0},{96,32},{1,65},{33,97},{65,1},{97,33},{2,66}... | collective-permute-start | bytes 442376 | tf_op jit(solution)/shard_map/ppermute | solution.py:374
  31.3 7.6 %collective-permute-start.15 = (bf16[48,1536]{1,0:T(8,128)(2,1)S(1)}, bf16[48,1536]{1,0:T(8,128)(2,1)S(1)}, u32[]{:S(2)}, u32[]{:S(2)}) collective-permute-start(bf16[48,1536]{1,0:T(8,128)(2,1)S(1)} %bitcast.73), channel_id=1, source_target_pairs={{0,32},{32,64},{64,96},{96,0},{1,33},{33,65},{65,97},{97,1},{2,34}... | collective-permute-start | bytes 442376 | tf_op jit(solution)/shard_map/ppermute | solution.py:374
  32.8 17.8 %collective-permute-start.1 = (bf16[128,1536]{1,0:T(8,128)(2,1)S(1)}, bf16[128,1536]{1,0:T(8,128)(2,1)S(1)}, u32[]{:S(2)}, u32[]{:S(2)}) collective-permute-start(bf16[128,1536]{1,0:T(8,128)(2,1)S(1)} %collective-permute-done), channel_id=1, source_target_pairs={{0,2},{2,0},{1,3},{3,1},{4,6},{6,4},{5,7},{7,5},{8,10},{10,8},{9,1... | collective-permute-start | bytes 1179656 | tf_op jit(solution)/shard_map/ppermute | solution.py:355
  35.9 13.1 %collective-permute-start.8 = (bf16[192,1664]{1,0:T(8,128)(2,1)S(1)}, bf16[192,1664]{1,0:T(8,128)(2,1)S(1)}, u32[]{:S(2)}, u32[]{:S(2)}) collective-permute-start(bf16[192,1664]{1,0:T(8,128)(2,1)S(1)} %bitcast.64), channel_id=1, source_target_pairs={{0,32},{1,33},{2,98},{3,99},{4,36},{5,37},{6,102},{7,103},{8,40},{... | collective-permute-start | bytes 1916936 | tf_op jit(solution)/shard_map/ppermute | solution.py:406
  39.0 4.4 %collective-permute-start.19 = (bf16[96,768]{1,0:T(8,128)(2,1)S(1)}, bf16[96,768]{1,0:T(8,128)(2,1)S(1)}, u32[]{:S(2)}, u32[]{:S(2)}) collective-permute-start(bf16[96,768]{1,0:T(8,128)(2,1)S(1)} %pad_maximum_fusion.8), channel_id=1, source_target_pairs={{0,12},{4,0},{8,4},{12,8},{1,13},{5,1},{9,5},{13,9},{2,14},{6,2},{... | collective-permute-start | bytes 442376 | tf_op jit(solution)/shard_map/ppermute | solution.py:374
  40.2 5.6 %collective-permute-start.20 = (bf16[96,768]{1,0:T(8,128)(2,1)S(1)}, bf16[96,768]{1,0:T(8,128)(2,1)S(1)}, u32[]{:S(2)}, u32[]{:S(2)}) collective-permute-start(bf16[96,768]{1,0:T(8,128)(2,1)S(1)} %pad_maximum_fusion.8), channel_id=1, source_target_pairs={{0,8},{4,12},{8,0},{12,4},{1,9},{5,13},{9,1},{13,5},{2,10},{6,14},... | collective-permute-start | bytes 442376 | tf_op jit(solution)/shard_map/ppermute | solution.py:374
  40.2 7.1 %collective-permute-start.21 = (bf16[96,768]{1,0:T(8,128)(2,1)S(1)}, bf16[96,768]{1,0:T(8,128)(2,1)S(1)}, u32[]{:S(2)}, u32[]{:S(2)}) collective-permute-start(bf16[96,768]{1,0:T(8,128)(2,1)S(1)} %pad_maximum_fusion.8), channel_id=1, source_target_pairs={{0,4},{4,8},{8,12},{12,0},{1,5},{5,9},{9,13},{13,1},{2,6},{6,10},{... | collective-permute-start | bytes 442376 | tf_op jit(solution)/shard_map/ppermute | solution.py:374
  43.4 11.2 %collective-permute-start.16 = (bf16[192,1536]{1,0:T(8,128)(2,1)S(1)}, bf16[192,1536]{1,0:T(8,128)(2,1)}, u32[]{:S(2)}, u32[]{:S(2)}) collective-permute-start(bf16[192,1536]{1,0:T(8,128)(2,1)S(1)} %pad_maximum_fusion.1.up_0), channel_id=1, source_target_pairs={{0,4},{1,5},{2,14},{3,15},{4,8},{5,9},{6,2},{7,3},{8,12},{9,13},{1... | collective-permute-start | bytes 1769480 | tf_op jit(solution)/shard_map/ppermute | solution.py:406
  45.8 10.9 %collective-permute-start.9 = (bf16[192,1664]{1,0:T(8,128)(2,1)S(1)}, bf16[192,1664]{1,0:T(8,128)(2,1)S(1)}, u32[]{:S(2)}, u32[]{:S(2)}) collective-permute-start(bf16[192,1664]{1,0:T(8,128)(2,1)S(1)} %bitcast.65), channel_id=1, source_target_pairs={{0,96},{1,97},{2,34},{3,35},{4,100},{5,101},{6,38},{7,39},{8,104},... | collective-permute-start | bytes 1916936 | tf_op jit(solution)/shard_map/ppermute | solution.py:406
  47.5 13.0 %collective-permute-start.22 = (bf16[384,768]{1,0:T(8,128)(2,1)S(1)}, bf16[384,768]{1,0:T(8,128)(2,1)}, u32[]{:S(2)}, u32[]{:S(2)}) collective-permute-start(bf16[384,768]{1,0:T(8,128)(2,1)S(1)} %pad_maximum_fusion.2.down_0), channel_id=1, source_target_pairs={{0,1},{1,16},{2,19},{3,2},{4,5},{5,20},{6,23},{7,6},{8,9},{9,24},{... | collective-permute-start | bytes 1769480 | tf_op jit(solution)/shard_map/ppermute | solution.py:406
  48.9 15.2 %collective-permute-start.10 = (bf16[192,1664]{1,0:T(8,128)(2,1)S(1)}, bf16[192,1664]{1,0:T(8,128)(2,1)S(1)}, u32[]{:S(2)}, u32[]{:S(2)}) collective-permute-start(bf16[192,1664]{1,0:T(8,128)(2,1)S(1)} %collective-permute-done.8.part_1), channel_id=1, source_target_pairs={{0,32},{1,33},{2,98},{3,99},{4,36},{5,37},{6,102},{7,103},{8,40},{... | collective-permute-start | bytes 1916936 | tf_op jit(solution)/shard_map/ppermute | solution.py:406
  50.7 24.3 %collective-permute-start.17 = (bf16[192,1536]{1,0:T(8,128)(2,1)S(1)}, bf16[192,1536]{1,0:T(8,128)(2,1)}, u32[]{:S(2)}, u32[]{:S(2)}) collective-permute-start(bf16[192,1536]{1,0:T(8,128)(2,1)S(1)} %pad_maximum_fusion.1.up_0), channel_id=1, source_target_pairs={{0,12},{1,13},{2,6},{3,7},{4,0},{5,1},{6,10},{7,11},{8,4},{9,5},{1... | collective-permute-start | bytes 1769480 | tf_op jit(solution)/shard_map/ppermute | solution.py:406
  54.5 23.0 %collective-permute-start.23 = (bf16[384,768]{1,0:T(8,128)(2,1)S(1)}, bf16[384,768]{1,0:T(8,128)(2,1)}, u32[]{:S(2)}, u32[]{:S(2)}) collective-permute-start(bf16[384,768]{1,0:T(8,128)(2,1)S(1)} %pad_maximum_fusion.2.down_0), channel_id=1, source_target_pairs={{0,17},{1,0},{2,3},{3,18},{4,21},{5,4},{6,7},{7,22},{8,25},{9,8},{... | collective-permute-start | bytes 1769480 | tf_op jit(solution)/shard_map/ppermute | solution.py:406
  56.7 20.9 %collective-permute-start.18 = (bf16[192,1536]{1,0:T(8,128)(2,1)}, bf16[192,1536]{1,0:T(8,128)(2,1)}, u32[]{:S(2)}, u32[]{:S(2)}) collective-permute-start(bf16[192,1536]{1,0:T(8,128)(2,1)} %collective-permute-done.16.up_1), channel_id=1, source_target_pairs={{0,4},{1,5},{2,14},{3,15},{4,8},{5,9},{6,2},{7,3},{8,12},{9,13},{1... | collective-permute-start | bytes 1769480 | tf_op jit(solution)/shard_map/ppermute | solution.py:406
  60.5 17.1 %collective-permute-start.24 = (bf16[384,768]{1,0:T(8,128)(2,1)}, bf16[384,768]{1,0:T(8,128)(2,1)}, u32[]{:S(2)}, u32[]{:S(2)}) collective-permute-start(bf16[384,768]{1,0:T(8,128)(2,1)} %collective-permute-done.22.down_1), channel_id=1, source_target_pairs={{0,1},{1,16},{2,19},{3,2},{4,5},{5,20},{6,23},{7,6},{8,9},{9,24},{... | collective-permute-start | bytes 1769480 | tf_op jit(solution)/shard_map/ppermute | solution.py:406
  70.6 7.0 %collective-permute-start.12 = (bf16[768,384]{1,0:T(8,128)(2,1)}, bf16[768,384]{1,0:T(8,128)(2,1)S(1)}, u32[]{:S(2)}, u32[]{:S(2)}) collective-permute-start(bf16[768,384]{1,0:T(8,128)(2,1)} %get-tuple-element.69.own_out_ref), channel_id=1, source_target_pairs={{0,2},{2,0},{1,3},{3,1},{4,6},{6,4},{5,7},{7,5},{8,10},{10,8},{9,1... | collective-permute-start | bytes 1769480 | tf_op jit(solution)/shard_map/ppermute | solution.py:355
  75.0 2.6 %collective-permute-start.11 = (bf16[256,384]{1,0:T(8,128)(2,1)}, bf16[256,384]{1,0:T(8,128)(2,1)S(1)}, u32[]{:S(2)}, u32[]{:S(2)}) collective-permute-start(bf16[256,384]{1,0:T(8,128)(2,1)} %get-tuple-element.68.own_o_ref), channel_id=1, source_target_pairs={{0,2},{2,0},{1,3},{3,1},{4,6},{6,4},{5,7},{7,5},{8,10},{10,8},{9,1... | collective-permute-start | bytes 589832 | tf_op jit(solution)/shard_map/ppermute | solution.py:355
  90.8 4.2 %collective-permute-start.27 = (f32[256,768]{1,0:T(8,128)}, f32[256,768]{1,0:T(8,128)S(1)}, u32[]{:S(2)}, u32[]{:S(2)}) collective-permute-start(f32[256,768]{1,0:T(8,128)} %get-tuple-element.76.own_grad_ref), channel_id=1, source_target_pairs={{0,2},{2,0},{1,3},{3,1},{4,6},{6,4},{5,7},{7,5},{8,10},{10,8},{9,1... | collective-permute-start | bytes 2359304 | tf_op jit(solution)/shard_map/ppermute | solution.py:355
  95.1 30.1 %collective-permute-start.35 = (bf16[768,768]{1,0:T(8,128)(2,1)S(1)}, bf16[768,768]{1,0:T(8,128)(2,1)S(1)}, u32[]{:S(2)}, u32[]{:S(2)}) collective-permute-start(bf16[768,768]{1,0:T(8,128)(2,1)S(1)} %copy-done.18), channel_id=1, source_target_pairs={{0,4},{1,5},{2,14},{3,15},{4,8},{5,9},{6,2},{7,3},{8,12},{9,13},{1... | collective-permute-start | bytes 3538952 | tf_op jit(solution)/shard_map/ppermute | solution.py:406
  105.9 19.3 %copy-start.5 = (bf16[768,768]{1,0:T(8,128)(2,1)S(1)}, bf16[768,768]{1,0:T(8,128)(2,1)}, u32[]{:S(2)}) copy-start(bf16[768,768]{1,0:T(8,128)(2,1)} %get-tuple-element.94) | copy-start | bytes 3538948
  105.9 13.8 %collective-permute-start.29 = (bf16[192,1664]{1,0:T(8,128)(2,1)}, bf16[192,1664]{1,0:T(8,128)(2,1)S(1)}, u32[]{:S(2)}, u32[]{:S(2)}) collective-permute-start(bf16[192,1664]{1,0:T(8,128)(2,1)} %get-tuple-element.91), channel_id=1, source_target_pairs={{0,32},{1,33},{2,98},{3,99},{4,36},{5,37},{6,102},{7,103},{8,40},{... | collective-permute-start | bytes 1916936 | tf_op jit(solution)/shard_map/ppermute | solution.py:406
  108.9 16.9 %collective-permute-start.25 = (f32[128,768]{1,0:T(8,128)}, f32[128,768]{1,0:T(8,128)}, u32[]{:S(2)}, u32[]{:S(2)}) collective-permute-start(f32[128,768]{1,0:T(8,128)} %get-tuple-element.74), channel_id=1, source_target_pairs={{0,2},{2,0},{1,3},{3,1},{4,6},{6,4},{5,7},{7,5},{8,10},{10,8},{9,1... | collective-permute-start | bytes 1179656 | tf_op jit(solution)/shard_map/ppermute | solution.py:355
  108.9 26.9 %collective-permute-start.34 = (bf16[768,768]{1,0:T(8,128)(2,1)}, bf16[768,768]{1,0:T(8,128)(2,1)S(1)}, u32[]{:S(2)}, u32[]{:S(2)}) collective-permute-start(bf16[768,768]{1,0:T(8,128)(2,1)} %get-tuple-element.93), channel_id=1, source_target_pairs={{0,12},{1,13},{2,6},{3,7},{4,0},{5,1},{6,10},{7,11},{8,4},{9,5},{1... | collective-permute-start | bytes 3538952 | tf_op jit(solution)/shard_map/ppermute | solution.py:406
  108.9 20.8 %collective-permute-start.28 = (bf16[192,1664]{1,0:T(8,128)(2,1)}, bf16[192,1664]{1,0:T(8,128)(2,1)}, u32[]{:S(2)}, u32[]{:S(2)}) collective-permute-start(bf16[192,1664]{1,0:T(8,128)(2,1)} %get-tuple-element.89), channel_id=1, source_target_pairs={{0,96},{1,97},{2,34},{3,35},{4,100},{5,101},{6,38},{7,39},{8,104},... | collective-permute-start | bytes 1916936 | tf_op jit(solution)/shard_map/ppermute | solution.py:406
  121.7 11.1 %collective-permute-start.30 = (bf16[192,1664]{1,0:T(8,128)(2,1)}, bf16[192,1664]{1,0:T(8,128)(2,1)}, u32[]{:S(2)}, u32[]{:S(2)}) collective-permute-start(bf16[192,1664]{1,0:T(8,128)(2,1)} %add_convert_fusion.3), channel_id=1, source_target_pairs={{0,32},{1,33},{2,98},{3,99},{4,36},{5,37},{6,102},{7,103},{8,40},{... | collective-permute-start | bytes 1916936 | tf_op jit(solution)/shard_map/ppermute | solution.py:406
  125.5 15.4 %collective-permute-start.36 = (bf16[768,768]{1,0:T(8,128)(2,1)S(1)}, bf16[768,768]{1,0:T(8,128)(2,1)S(1)}, u32[]{:S(2)}, u32[]{:S(2)}) collective-permute-start(bf16[768,768]{1,0:T(8,128)(2,1)S(1)} %add_convert_fusion.1), channel_id=1, source_target_pairs={{0,4},{1,5},{2,14},{3,15},{4,8},{5,9},{6,2},{7,3},{8,12},{9,13},{1... | collective-permute-start | bytes 3538952 | tf_op jit(solution)/shard_map/ppermute | solution.py:406
  127.7 44.7 %collective-permute-start.26 = (bf16[128,768]{1,0:T(8,128)(2,1)}, bf16[128,768]{1,0:T(8,128)(2,1)}, u32[]{:S(2)}, u32[]{:S(2)}) collective-permute-start(bf16[128,768]{1,0:T(8,128)(2,1)} %add_convert_fusion.5), channel_id=1, source_target_pairs={{0,0},{1,2},{2,1},{3,3},{4,4},{5,6},{6,5},{7,7},{8,8},{9,10},{10,9... | collective-permute-start | bytes 589832 | tf_op jit(solution)/shard_map/ppermute | solution.py:363
  129.7 44.5 %collective-permute-start.43 = (f32[128,768]{1,0:T(8,128)}, f32[128,768]{1,0:T(8,128)}, u32[]{:S(2)}, u32[]{:S(2)}) collective-permute-start(f32[128,768]{1,0:T(8,128)} %get-tuple-element.97), channel_id=1, source_target_pairs={{0,2},{2,0},{1,3},{3,1},{4,6},{6,4},{5,7},{7,5},{8,10},{10,8},{9,1... | collective-permute-start | bytes 1179656 | tf_op jit(solution)/shard_map/ppermute | solution.py:355
  134.5 8.4 %collective-permute-start.31 = (bf16[2,24,1664]{2,1,0:T(8,128)(2,1)S(1)}, bf16[2,24,1664]{2,1,0:T(8,128)(2,1)S(1)}, u32[]{:S(2)}, u32[]{:S(2)}) collective-permute-start(bf16[2,24,1664]{2,1,0:T(8,128)(2,1)S(1)} %get-tuple-element.117), channel_id=1, source_target_pairs={{0,4},{4,8},{8,12},{12,0},{1,5},{5,9},{9,13},{13,1},{2,6},{6,10},{... | collective-permute-start | bytes 479240 | tf_op jit(solution)/shard_map/ppermute | solution.py:374
  135.8 10.3 %collective-permute-start.32 = (bf16[2,24,1664]{2,1,0:T(8,128)(2,1)S(1)}, bf16[2,24,1664]{2,1,0:T(8,128)(2,1)S(1)}, u32[]{:S(2)}, u32[]{:S(2)}) collective-permute-start(bf16[2,24,1664]{2,1,0:T(8,128)(2,1)S(1)} %get-tuple-element.119), channel_id=1, source_target_pairs={{0,8},{4,12},{8,0},{12,4},{1,9},{5,13},{9,1},{13,5},{2,10},{6,14},... | collective-permute-start | bytes 479240 | tf_op jit(solution)/shard_map/ppermute | solution.py:374
  140.9 7.0 %collective-permute-start.33 = (bf16[2,24,1664]{2,1,0:T(8,128)(2,1)S(1)}, bf16[2,24,1664]{2,1,0:T(8,128)(2,1)S(1)}, u32[]{:S(2)}, u32[]{:S(2)}) collective-permute-start(bf16[2,24,1664]{2,1,0:T(8,128)(2,1)S(1)} %get-tuple-element.118), channel_id=1, source_target_pairs={{0,12},{4,0},{8,4},{12,8},{1,13},{5,1},{9,5},{13,9},{2,14},{6,2},{... | collective-permute-start | bytes 479240 | tf_op jit(solution)/shard_map/ppermute | solution.py:374
  142.9 8.2 %collective-permute-start.37 = (bf16[192,768]{1,0:T(8,128)(2,1)S(1)}, bf16[192,768]{1,0:T(8,128)(2,1)S(1)}, u32[]{:S(2)}, u32[]{:S(2)}) collective-permute-start(bf16[192,768]{1,0:T(8,128)(2,1)S(1)} %pad_maximum_fusion.5), channel_id=1, source_target_pairs={{0,32},{32,64},{64,96},{96,0},{1,33},{33,65},{65,97},{97,1},{2,34}... | collective-permute-start | bytes 884744 | tf_op jit(solution)/shard_map/ppermute | solution.py:374
  146.2 10.1 %collective-permute-start.38 = (bf16[192,768]{1,0:T(8,128)(2,1)S(1)}, bf16[192,768]{1,0:T(8,128)(2,1)S(1)}, u32[]{:S(2)}, u32[]{:S(2)}) collective-permute-start(bf16[192,768]{1,0:T(8,128)(2,1)S(1)} %pad_maximum_fusion.6), channel_id=1, source_target_pairs={{0,64},{32,96},{64,0},{96,32},{1,65},{33,97},{65,1},{97,33},{2,66}... | collective-permute-start | bytes 884744 | tf_op jit(solution)/shard_map/ppermute | solution.py:374
  147.9 8.4 %collective-permute-start.39 = (bf16[192,768]{1,0:T(8,128)(2,1)S(1)}, bf16[192,768]{1,0:T(8,128)(2,1)S(1)}, u32[]{:S(2)}, u32[]{:S(2)}) collective-permute-start(bf16[192,768]{1,0:T(8,128)(2,1)S(1)} %pad_maximum_fusion.7), channel_id=1, source_target_pairs={{0,96},{32,0},{64,32},{96,64},{1,97},{33,1},{65,33},{97,65},{2,98}... | collective-permute-start | bytes 884744 | tf_op jit(solution)/shard_map/ppermute | solution.py:374
  156.5 23.5 %collective-permute-start.40 = (bf16[24,768]{1,0:T(8,128)(2,1)S(1)}, bf16[24,768]{1,0:T(8,128)(2,1)S(1)}, u32[]{:S(2)}, u32[]{:S(2)}) collective-permute-start(bf16[24,768]{1,0:T(8,128)(2,1)S(1)} %get-tuple-element.144), channel_id=1, source_target_pairs={{0,1},{1,16},{16,17},{17,0},{2,3},{3,18},{18,19},{19,2},{4,5},{5,2... | collective-permute-start | bytes 110600 | tf_op jit(solution)/shard_map/ppermute | solution.py:374
  159.9 20.2 %collective-permute-start.41 = (bf16[24,768]{1,0:T(8,128)(2,1)S(1)}, bf16[24,768]{1,0:T(8,128)(2,1)S(1)}, u32[]{:S(2)}, u32[]{:S(2)}) collective-permute-start(bf16[24,768]{1,0:T(8,128)(2,1)S(1)} %get-tuple-element.146), channel_id=1, source_target_pairs={{0,16},{1,17},{16,0},{17,1},{2,18},{3,19},{18,2},{19,3},{4,20},{5,... | collective-permute-start | bytes 110600 | tf_op jit(solution)/shard_map/ppermute | solution.py:374
  159.9 20.2 %collective-permute-start.42 = (bf16[24,768]{1,0:T(8,128)(2,1)S(1)}, bf16[24,768]{1,0:T(8,128)(2,1)S(1)}, u32[]{:S(2)}, u32[]{:S(2)}) collective-permute-start(bf16[24,768]{1,0:T(8,128)(2,1)S(1)} %get-tuple-element.145), channel_id=1, source_target_pairs={{0,17},{1,0},{16,1},{17,16},{2,19},{3,2},{18,3},{19,18},{4,21},{5,... | collective-permute-start | bytes 110600 | tf_op jit(solution)/shard_map/ppermute | solution.py:374
  163.3 20.4 %all-to-all-start.1 = ((bf16[8,6,3200]{2,1,0:T(8,128)(2,1)}), bf16[8,6,3200]{2,1,0:T(8,128)(2,1)S(1)}, u32[]{:S(2)}, u32[]{:S(2)}) async-start(bf16[8,6,3200]{2,1,0:T(8,128)(2,1)} %reshape.141), calls=%async_computation.1 | async-start | bytes 819200 | tf_op jit(solution)/shard_map/all_to_all | solution.py:568
  176.5 7.2 %collective-permute-start.44 = (bf16[128,768]{1,0:T(8,128)(2,1)}, bf16[128,768]{1,0:T(8,128)(2,1)S(1)}, u32[]{:S(2)}, u32[]{:S(2)}) collective-permute-start(bf16[128,768]{1,0:T(8,128)(2,1)} %shard_map.275), channel_id=1, source_target_pairs={{0,0},{1,2},{2,1},{3,3},{4,4},{5,6},{6,5},{7,7},{8,8},{9,10},{10,9... | collective-permute-start | bytes 589832 | tf_op jit(solution)/shard_map/ppermute | solution.py:363
  (18 other events, 107.8 us)
where the time goes:
time: 188 us; the launch traced here: 187 us
  starting transfers between devices  84.6 us (45%)
  waiting for transfers between devices  46.6 us (25%)
  Pallas kernels  33.6 us (18%)
  other arithmetic  13.6 us (7%)
  local copies, waits for them, and re-layouts  6.96 us (4%)
  between operations  2.01 us (1%)
    pallas_call x6, Pallas kernels, call(): pl.pallas_call(kernel, out_shape=tuple((jax.ShapeDtypeStruct(s, d) for s,...  33.6 us
    ppermute x21, starting transfers between devices, ring(): return lax.ppermute(values, axis, [(i, (i + by) % 4) for i in range(4)])  28.8 us
    ppermute x15, waiting for transfers between devices, send(): return lax.ppermute(values, AXES, along(axis, by))  22 us
    ppermute x15, starting transfers between devices, send(): return lax.ppermute(values, AXES, along(axis, by))  20 us
    ppermute x21, waiting for transfers between devices, ring(): return lax.ppermute(values, axis, [(i, (i + by) % 4) for i in range(4)])  17.5 us
    ppermute x6, starting transfers between devices, between_cores(): return lax.ppermute(values, 'c', [(0, 1), (1, 0)])  11.7 us
    all_to_all x1, starting transfers between devices, shards(): got = lax.all_to_all(sums.reshape(8, 6, ATTN + UP), EIGHT, 0, 0, tiled=True)  9.13 us
    ppermute x3, starting transfers between devices, swap_items(): return lax.ppermute(values, ('c', 'yl'), [(0, 0), (1, 2), (2, 1), (3, 3)])  8.98 us
  transfers between devices with their start and end apart: 47, of which 18 were waited for; matrix products, arithmetic and copies ran while one was open for 9% of the time, Pallas kernels for 10%

commit v1 on v0

--- a/solution.py
+++ b/solution.py
@@ -203,7 +203,7 @@
     place_ref, x_ref, own_o_ref, far_o_ref, own_out_ref, far_out_ref, vec_ref, up_b_ref, g_ref, order_ref,
     up_0, up_1, up_2, up_3, down_0, down_1, down_2, down_3,
     h_ref, m_own_ref, m_far_ref, grad_a_ref, grad_up_b_ref, grad_down_b_ref,
-    part_0, part_1, part_2, part_3,
+    gup_0, gup_1, gup_2, gup_3, gdown_0, gdown_1, gdown_2, gdown_3,
     up_ref, down_ref, grad_up_ref, grad_down_ref,
 ):
     core = place_ref[0]
@@ -248,14 +248,10 @@
     low = (grad_a - high.astype(F32)).astype(BF16)
     grad_a_ref[...] = dot_nt(high, order_ref[...]) + dot_nt(low, order_ref[...])
     grad_down_b_ref[...] = total(g[:OWN])
-    for part, at in zip((part_0, part_1, part_2, part_3), up_at):
-        rows = pl.ds(pl.multiple_of(at * BLOCK, 64), BLOCK)
-        part[0:BLOCK, :] = grad_up_ref[rows, pl.ds(0, WIDTH)]
-        part[BLOCK : 2 * BLOCK, :] = grad_up_ref[rows, pl.ds(WIDTH, WIDTH)]
-        for y in range(4):
-            part[2 * BLOCK + 96 * y : 2 * BLOCK + 96 * (y + 1), :] = grad_down_ref[
-                pl.ds(pl.multiple_of(DOWN_ROWS * y + 96 * at, 32), 96), :
-            ]
+    for gup, at in zip((gup_0, gup_1, gup_2, gup_3), up_at):
+        gup[...] = grad_up_ref[pl.ds(pl.multiple_of(at * BLOCK, 64), BLOCK), :]
+    for gdown, at in zip((gdown_0, gdown_1, gdown_2, gdown_3), down_at):
+        gdown[...] = grad_down_ref[pl.ds(pl.multiple_of(at * DOWN_ROWS, 128), DOWN_ROWS), :]
 
 
 def back_kernel(
@@ -335,7 +331,7 @@
     out_ref[...] = (gh_ref[...] + norm_back(grad, unit, scale, vec_ref[0:1, :])).astype(BF16)
 
 
-def call(kernel, place, args, outs, scratch=()):
+def call(kernel, place, args, outs, scratch=(), limit=VMEM_LIMIT):
     specs = [pl.BlockSpec(memory_space=pltpu.VMEM)] * len(args)
     if place is not None:
         args = (place,) + tuple(args)
@@ -346,7 +342,7 @@
         in_specs=specs,
         out_specs=tuple(pl.BlockSpec(memory_space=pltpu.VMEM) for _ in outs),
         scratch_shapes=[pltpu.VMEM(s, d) for s, d in scratch],
-        compiler_params=pltpu.CompilerParams(vmem_limit_bytes=VMEM_LIMIT),
+        compiler_params=pltpu.CompilerParams(vmem_limit_bytes=limit),
         cost_estimate=pl.CostEstimate(flops=1, bytes_accessed=1, transcendentals=0),
     )(*args)
 
@@ -382,9 +378,16 @@
     return [lax.select_n(lax.rem(j - at + 4, 4), *blocks) for j in range(4)]
 
 
+def ring_sent(blocks, axis):
+    return [ring(blocks[1], axis, 1), ring(blocks[2], axis, 2), ring(blocks[3], axis, -1)]
+
+
+def ring_total(blocks, got):
+    return sum((g.astype(F32) for g in got), blocks[0].astype(F32))
+
+
 def ring_reduce(blocks, axis):
-    got = [ring(blocks[1], axis, 1), ring(blocks[2], axis, 2), ring(blocks[3], axis, -1)]
-    return sum((g.astype(F32) for g in got), blocks[0].astype(F32))
+    return ring_total(blocks, ring_sent(blocks, axis))
 
 
 def ring_split(values, at, axis=0):
@@ -415,9 +418,17 @@
     return send(blocks[3], axis, 1), send(blocks[1], axis, -1)
 
 
-def relay_end(blocks, got, axis):
-    ahead = (blocks[2].astype(F32) + got[0].astype(F32)).astype(BF16)
-    return blocks[0].astype(F32) + got[1].astype(F32) + send(ahead, axis, 1).astype(F32)
+def relay_ahead(blocks, got):
+    return (blocks[2].astype(F32) + got[0].astype(F32)).astype(BF16)
+
+
+def relay_end(blocks, got, far):
+    return blocks[0].astype(F32) + got[1].astype(F32) + far.astype(F32)
+
+
+def after(values, *others):
+    tied = lax.optimization_barrier((*values, *others))
+    return list(tied[: len(values)])
 
 
 def by_place(place, first, second, axis=0):
@@ -461,7 +472,6 @@
     cot = jnp.where(present_rows, cotangent.reshape(OWN, WIDTH), 0).astype(BF16)
 
     mine = swap_items(jnp.concatenate([tokens.reshape(OWN, WIDTH), cot], axis=1))
-    downs = ring_gather(w_down, "x")
     (parts,) = call(
         halves_kernel,
         None,
@@ -471,6 +481,7 @@
         (((8, 6, ATTN + UP), BF16),),
         (((16, 128), F32), ((6, FF), F32), ((6, UP), F32)),
     )
+    downs = ring_gather(after([w_down], parts)[0], "x")
     rows = lax.all_to_all(parts, EIGHT, 0, 0, tiled=True).reshape(2, 24, ATTN + UP)
     attn, ups = rows[:, :, :ATTN], rows[:, :, ATTN:].reshape(48, UP)
     downs = jnp.concatenate(ring_order(downs, x_at), axis=0)
@@ -489,6 +500,8 @@
     ups = relay_gather(ups, "z")
     downs = relay_gather(downs, "y")
 
+    order = up_order()
+    (x,) = after([x], order)
     a1, qkv, own_o, lse, w_in, own_out, small_all, vectors = call(
         attend_kernel,
         place,
@@ -511,7 +524,7 @@
     hidden, m_own, m_far, grad_a_own, grad_up_b, grad_down_b, *grads = call(
         mlp_kernel,
         place,
-        (x, own_o, far_o, own_out, far_out, vectors, up_b, g, up_order(), *ups, *downs),
+        (x, own_o, far_o, own_out, far_out, vectors, up_b, g, order, *ups, *downs),
         (
             ((ROWS, WIDTH), F32),
             ((OWN, WIDTH), F32),
@@ -520,14 +533,15 @@
             ((1, UP), F32),
             ((1, WIDTH), F32),
         )
-        + (((2 * BLOCK + DOWN_ROWS, WIDTH), BF16),) * 4,
+        + (((BLOCK, UP), BF16),) * 4
+        + (((DOWN_ROWS, WIDTH), BF16),) * 4,
         (((WIDTH, UP), BF16), ((UP, WIDTH), BF16), ((WIDTH, UP), BF16), ((UP, WIDTH), BF16)),
     )
     grad_a_far = between_cores(grad_a_own)
     grad_a_far, *grads = lax.optimization_barrier((grad_a_far, *grads))
-    got = relay_start(grads, "z")
-    block = swap_items((m_own + between_cores(m_far)).astype(BF16))
-    block_out = jnp.where(present_rows, block, 0).reshape(tokens.shape)
+    grad_ups, grad_downs = grads[:4], grads[4:]
+    got_ups, got_downs = relay_start(grad_ups, "z"), relay_start(grad_downs, "y")
+    block = (m_own + between_cores(m_far)).astype(BF16)
     up_cols = grad_up_b.reshape(2, 2, 4, 4, 24).transpose(3, 0, 2, 1, 4)[:, :, :, None]
     up_cols = jnp.where((jnp.arange(2) == core)[:, None, None], up_cols, 0.0).reshape(WIDTH, 4)
     up_high = up_cols.astype(BF16).astype(F32)
@@ -549,27 +563,40 @@
             ((WIDTH, ATTN), BF16),
         ),
     )
-    (grad_x,) = call(
-        tokens_kernel, place, (x, own_x, between_cores(far_x), gh, vectors), (((OWN, WIDTH), BF16),)
-    )
-    grad_x = swap_items(grad_x)
-
-    attn_sum = relay_end(grad_attn, relay_start(grad_attn, "x"), "x").astype(BF16).reshape(2, 4, 24, ATTN)
+    ups_ahead, downs_ahead = relay_ahead(grad_ups, got_ups), relay_ahead(grad_downs, got_downs)
+    (far_x,) = after([between_cores(far_x)], ups_ahead, downs_ahead)
+    (grad_x,) = call(tokens_kernel, place, (x, own_x, far_x, gh, vectors), (((OWN, WIDTH), BF16),))
+
+    got_attn = relay_start(grad_attn, "x")
+    got_attn = after(got_attn, grad_x, block)
+    attn_ahead = relay_ahead(grad_attn, got_attn)
+    far_ups, far_downs = after([send(ups_ahead, "z", 1), send(downs_ahead, "y", 1)], attn_ahead)
+    up_sum = relay_end(grad_ups, got_ups, far_ups).astype(BF16)
+    down_sum = relay_end(grad_downs, got_downs, far_downs).astype(BF16)
+    (far_attn,) = after([send(attn_ahead, "x", 1)], up_sum, down_sum)
+    up_parts = ring_split(up_sum, x_at)
+    down_parts = ring_split(down_sum.reshape(4, 4, 24, WIDTH), x_at, 1)
+    mlp_sum = ring_reduce(
+        [
+            jnp.concatenate([u[:, :WIDTH], u[:, WIDTH:], d.reshape(96, WIDTH)])
+            for u, d in zip(up_parts, down_parts)
+        ],
+        "x",
+    )
+    attn_sum = relay_end(grad_attn, got_attn, far_attn).astype(BF16).reshape(2, 4, 24, ATTN)
+    results = swap_items(after([jnp.concatenate([block, grad_x], axis=1)], attn_sum)[0])
     attn_sum = ring_reduce([a[:, 0] for a in ring_split(attn_sum, z_at, 1)], "z")
-    mlp_sum = relay_end(grads, got, "z").astype(BF16)
-    up_parts = ring_split(mlp_sum[: 2 * BLOCK].reshape(2, 4, 48, WIDTH), x_at, 1)
-    down_parts = ring_split(mlp_sum[2 * BLOCK :].reshape(4, 4, 24, WIDTH), x_at, 1)
-    mlp_sum = ring_reduce(
-        [jnp.concatenate([u.reshape(96, WIDTH), d.reshape(96, WIDTH)]) for u, d in zip(up_parts, down_parts)], "x"
-    )
+    block_out = jnp.where(present_rows, results[:, :WIDTH], 0).reshape(tokens.shape)
     up_sum = jnp.concatenate([mlp_sum[:48], mlp_sum[48:96]], axis=1).reshape(2, 24, UP)
-    down_sum = ring_reduce(ring_split(mlp_sum[96:].astype(BF16), y_at), RING_Y)
     sums = jnp.concatenate([attn_sum.astype(BF16), up_sum.astype(BF16)], axis=2)
-    got = lax.all_to_all(sums.reshape(8, 6, ATTN + UP), EIGHT, 0, 0, tiled=True)
+    sums = sums.reshape(8, 6, ATTN + UP)
+    got = lax.all_to_all(sums, EIGHT, 0, 0, tiled=True)
+    down_parts = ring_split(mlp_sum[96:].astype(BF16), z_at)
+    down_sum = ring_total(down_parts, after(ring_sent(down_parts, "z"), got))
     out_qkv, out_out, out_up, out_down, grad_tokens, *vecs, out_up_b = call(
         outputs_kernel,
         None,
-        (got, down_sum, grad_x),
+        (got, down_sum, results[:, WIDTH:]),
         (
             ((6, 3 * WIDTH), F32),
             ((6, WIDTH), F32),
@@ -580,6 +607,7 @@
         + (((6,), F32),) * 8
         + (((24,), F32),),
         (((128, 128), F32),),
+        8 * 1024 * 1024,
     )
     gain_1, bias_1, bias_q, bias_v, bias_out, gain_2, bias_2, bias_down = vecs
     return (

time: 188 us -> 172 us (0.915)
  starting transfers between devices: 84.6 us -> 74.8 us
  other arithmetic: 13.6 us -> 10.5 us
    ppermute x21, starting transfers between devices: 28.8 us -> 23 us  [ring(): return lax.ppermute(values, axis, [(i, (i + by) % 4) for i in range(4)])]
    convert_element_type x5 -> x7, other arithmetic: 6.4 us -> 3.06 us  [the longest x1 1.28 us: shards(): down_sum = relay_end(grad_downs, got_downs, far_downs).astype(BF16)]
    ppermute x3 -> x2, waiting for transfers between devices: 2.97 us -> 0.01 us  [swap_items(): return lax.ppermute(values, ('c', 'yl'), [(0, 0), (1, 2), (2, 1), (3, 3)])]
    all_to_all x1, waiting for transfers between devices: 0.01 us -> 2.8 us  [shards(): got = lax.all_to_all(sums, EIGHT, 0, 0, tiled=True)]
    ppermute x6, starting transfers between devices: 11.7 us -> 9.09 us  [between_cores(): return lax.ppermute(values, 'c', [(0, 1), (1, 0)])]
    ppermute x15 -> x18, waiting for transfers between devices: 22 us -> 24 us  [send(): return lax.ppermute(values, AXES, along(axis, by))]
    all_to_all x1, starting transfers between devices: 9.13 us -> 7.2 us  [shards(): got = lax.all_to_all(sums, EIGHT, 0, 0, tiled=True)]
    ppermute x15 -> x18, starting transfers between devices: 20 us -> 21.1 us  [send(): return lax.ppermute(values, AXES, along(axis, by))]
  transfers between devices with their start and end apart: 47 -> 49, of which waited for: 18 -> 23; matrix products, arithmetic and copies ran while one was open for 9% -> 9% of each run, Pallas kernels for 10% -> 10%
where the time goes in v1:
time: 172 us; the launch traced here: 171 us
  starting transfers between devices  74.8 us (43%)
  waiting for transfers between devices  45.2 us (26%)
  Pallas kernels  32.2 us (19%)
  other arithmetic  10.5 us (6%)
  local copies, waits for them, and re-layouts  6.5 us (4%)
  between operations  2.03 us (1%)
    pallas_call x6, Pallas kernels, call(): pl.pallas_call(kernel, out_shape=tuple((jax.ShapeDtypeStruct(s, d) for s,...  32.2 us
    ppermute x18, waiting for transfers between devices, send(): return lax.ppermute(values, AXES, along(axis, by))  24 us
    ppermute x21, starting transfers between devices, ring(): return lax.ppermute(values, axis, [(i, (i + by) % 4) for i in range(4)])  23 us
    ppermute x18, starting transfers between devices, send(): return lax.ppermute(values, AXES, along(axis, by))  21.1 us
    ppermute x21, waiting for transfers between devices, ring(): return lax.ppermute(values, axis, [(i, (i + by) % 4) for i in range(4)])  16 us
    ppermute x6, starting transfers between devices, between_cores(): return lax.ppermute(values, 'c', [(0, 1), (1, 0)])  9.09 us
    ppermute x2, starting transfers between devices, swap_items(): return lax.ppermute(values, ('c', 'yl'), [(0, 0), (1, 2), (2, 1), (3, 3)])  8.48 us
    all_to_all x1, starting transfers between devices, shards(): got = lax.all_to_all(sums, EIGHT, 0, 0, tiled=True)  7.2 us
  transfers between devices with their start and end apart: 49, of which 23 were waited for; matrix products, arithmetic and copies ran while one was open for 9% of the time, Pallas kernels for 10%

profile of v1, /device:TPU:1, one launch (start us, length us, event | category | flops | bytes accessed | tf_op | source)
XLA Modules:
  0.0 171.3 jit_solution(2002415572689589822)
XLA Ops:
  0.7 2.0 %shard_map.271 = bf16[8,6,3200]{2,1,0:T(8,128)(2,1)} custom-call(bf16[6,2304]{1,0:T(8,128)(2,1)} %qkv_ref.1, bf16[6,768]{1,0:T(8,128)(2,1)} %out_ref.1, bf16[6,3072]{1,0:T(8,128)(2,1)} %up_ref.1, bf16[6]{0:T(256)(128)(2,1)} %refs_0_.1, bf16[6]{0:T(256)(128)(2,1)} %refs_1_.1, bf16[6]{0:T(256)(128)(2,1)} %refs_2_.1, bf16[6]{0:T(256)(128)(2,1)} %refs_3_.1, ...), custom_call_target="tpu_custom_call" | custom-call | flops 1 | bytes 1 | tf_op jit(solution)/shard_map/pallas_call | solution.py:339
  2.6 3.3 %collective-permute-start.5 = (bf16[24,768]{1,0:T(8,128)(2,1)}, bf16[24,768]{1,0:T(8,128)(2,1)S(1)}, u32[]{:S(2)}, u32[]{:S(2)}) collective-permute-start(bf16[24,768]{1,0:T(8,128)(2,1)} %param.29), channel_id=1, source_target_pairs={{0,96},{32,0},{64,32},{96,64},{1,97},{33,1},{65,33},{97,65},{2,98}... | collective-permute-start | bytes 110600 | tf_op jit(solution)/shard_map/ppermute | solution.py:370
  7.1 6.0 %all-to-all-start = ((bf16[8,6,3200]{2,1,0:T(8,128)(2,1)}), bf16[8,6,3200]{2,1,0:T(8,128)(2,1)S(1)}, u32[]{:S(2)}, u32[]{:S(2)}) async-start(bf16[8,6,3200]{2,1,0:T(8,128)(2,1)} %shard_map.271), calls=%async_computation | async-start | bytes 819200 | tf_op jit(solution)/shard_map/all_to_all | solution.py:485
  14.0 3.5 %collective-permute-start = (bf16[128,1536]{1,0:T(8,128)(2,1)S(1)}, bf16[128,1536]{1,0:T(8,128)(2,1)S(1)}, u32[]{:S(2)}, u32[]{:S(2)}) collective-permute-start(bf16[128,1536]{1,0:T(8,128)(2,1)S(1)} %pad_maximum_fusion.3), channel_id=1, source_target_pairs={{0,0},{1,2},{2,1},{3,3},{4,4},{5,6},{6,5},{7,7},{8,8},{9,10},{10,9... | collective-permute-start | bytes 1179656 | tf_op jit(solution)/shard_map/ppermute | solution.py:359
  17.6 1.4 fusion.order_ref
  19.7 1.6 all-to-all-done
  21.4 3.8 %collective-permute-start.2 = (bf16[2,24,1664]{2,1,0:T(8,128)(2,1)S(1)}, bf16[2,24,1664]{2,1,0:T(8,128)(2,1)S(1)}, u32[]{:S(2)}, u32[]{:S(2)}) collective-permute-start(bf16[2,24,1664]{2,1,0:T(8,128)(2,1)S(1)} %slice.76), channel_id=1, source_target_pairs={{0,12},{4,0},{8,4},{12,8},{1,13},{5,1},{9,5},{13,9},{2,14},{6,2},{... | collective-permute-start | bytes 479240 | tf_op jit(solution)/shard_map/ppermute | solution.py:370
  26.0 2.1 %collective-permute-start.13 = (bf16[48,1536]{1,0:T(8,128)(2,1)S(1)}, bf16[48,1536]{1,0:T(8,128)(2,1)S(1)}, u32[]{:S(2)}, u32[]{:S(2)}) collective-permute-start(bf16[48,1536]{1,0:T(8,128)(2,1)S(1)} %bitcast.56), channel_id=1, source_target_pairs={{0,96},{32,0},{64,32},{96,64},{1,97},{33,1},{65,33},{97,65},{2,98}... | collective-permute-start | bytes 442376 | tf_op jit(solution)/shard_map/ppermute | solution.py:370
  28.2 1.2 collective-permute-start.14
  29.4 1.9 %collective-permute-done.2 = bf16[2,24,1664]{2,1,0:T(8,128)(2,1)S(1)} collective-permute-done((bf16[2,24,1664]{2,1,0:T(8,128)(2,1)S(1)}, bf16[2,24,1664]{2,1,0:T(8,128)(2,1)S(1)}, u32[]{:S(2)}, u32[]{:S(2)}) %collective-permute-start.2) | collective-permute-done | bytes 159776 | tf_op jit(solution)/shard_map/ppermute | solution.py:370
  31.3 1.5 collective-permute-start.15
  32.8 2.3 %collective-permute-start.1 = (bf16[128,1536]{1,0:T(8,128)(2,1)S(1)}, bf16[128,1536]{1,0:T(8,128)(2,1)S(1)}, u32[]{:S(2)}, u32[]{:S(2)}) collective-permute-start(bf16[128,1536]{1,0:T(8,128)(2,1)S(1)} %collective-permute-done), channel_id=1, source_target_pairs={{0,2},{2,0},{1,3},{3,1},{4,6},{6,4},{5,7},{7,5},{8,10},{10,8},{9,1... | collective-permute-start | bytes 1179656 | tf_op jit(solution)/shard_map/ppermute | solution.py:351
  35.9 2.1 %collective-permute-start.8 = (bf16[192,1664]{1,0:T(8,128)(2,1)S(1)}, bf16[192,1664]{1,0:T(8,128)(2,1)S(1)}, u32[]{:S(2)}, u32[]{:S(2)}) collective-permute-start(bf16[192,1664]{1,0:T(8,128)(2,1)S(1)} %bitcast.51), channel_id=1, source_target_pairs={{0,32},{1,33},{2,98},{3,99},{4,36},{5,37},{6,102},{7,103},{8,40},{... | collective-permute-start | bytes 1916936 | tf_op jit(solution)/shard_map/ppermute | solution.py:409
  39.0 1.2 collective-permute-start.19
  40.9 2.4 %collective-permute-done.19 = bf16[96,768]{1,0:T(8,128)(2,1)S(1)} collective-permute-done((bf16[96,768]{1,0:T(8,128)(2,1)S(1)}, bf16[96,768]{1,0:T(8,128)(2,1)S(1)}, u32[]{:S(2)}, u32[]{:S(2)}) %collective-permute-start.19) | collective-permute-done | bytes 147488 | tf_op jit(solution)/shard_map/ppermute | solution.py:370
  43.3 2.3 %collective-permute-start.16 = (bf16[192,1536]{1,0:T(8,128)(2,1)S(1)}, bf16[192,1536]{1,0:T(8,128)(2,1)}, u32[]{:S(2)}, u32[]{:S(2)}) collective-permute-start(bf16[192,1536]{1,0:T(8,128)(2,1)S(1)} %pad_maximum_fusion.1.up_0), channel_id=1, source_target_pairs={{0,4},{1,5},{2,14},{3,15},{4,8},{5,9},{6,2},{7,3},{8,12},{9,13},{1... | collective-permute-start | bytes 1769480 | tf_op jit(solution)/shard_map/ppermute | solution.py:409
  47.4 1.5 collective-permute-start.22
  48.9 1.7 collective-permute-start.10
  52.0 2.5 %collective-permute-done.16.up_1 = bf16[192,1536]{1,0:T(8,128)(2,1)} collective-permute-done((bf16[192,1536]{1,0:T(8,128)(2,1)S(1)}, bf16[192,1536]{1,0:T(8,128)(2,1)}, u32[]{:S(2)}, u32[]{:S(2)}) %collective-permute-start.16) | collective-permute-done | bytes 589856 | tf_op jit(solution)/shard_map/ppermute | solution.py:409
  54.5 2.2 %collective-permute-done.9.part_2 = bf16[192,1664]{1,0:T(8,128)(2,1)S(1)} collective-permute-done((bf16[192,1664]{1,0:T(8,128)(2,1)S(1)}, bf16[192,1664]{1,0:T(8,128)(2,1)S(1)}, u32[]{:S(2)}, u32[]{:S(2)}) %collective-permute-start.9) | collective-permute-done | bytes 639008 | tf_op jit(solution)/shard_map/ppermute | solution.py:409
  56.7 3.8 %collective-permute-start.18 = (bf16[192,1536]{1,0:T(8,128)(2,1)}, bf16[192,1536]{1,0:T(8,128)(2,1)}, u32[]{:S(2)}, u32[]{:S(2)}) collective-permute-start(bf16[192,1536]{1,0:T(8,128)(2,1)} %collective-permute-done.16.up_1), channel_id=1, source_target_pairs={{0,4},{1,5},{2,14},{3,15},{4,8},{5,9},{6,2},{7,3},{8,12},{9,13},{1... | collective-permute-start | bytes 1769480 | tf_op jit(solution)/shard_map/ppermute | solution.py:409
  60.5 3.6 %collective-permute-done.10.part_3 = bf16[192,1664]{1,0:T(8,128)(2,1)S(1)} collective-permute-done((bf16[192,1664]{1,0:T(8,128)(2,1)S(1)}, bf16[192,1664]{1,0:T(8,128)(2,1)S(1)}, u32[]{:S(2)}, u32[]{:S(2)}) %collective-permute-start.10) | collective-permute-done | bytes 639008 | tf_op jit(solution)/shard_map/ppermute | solution.py:409
  64.9 5.6 %shard_map.272 = (bf16[256,768]{1,0:T(8,128)(2,1)}, bf16[256,1152]{1,0:T(8,128)(2,1)}, bf16[256,384]{1,0:T(8,128)(2,1)}, f32[256,128]{1,0:T(8,128)}, bf16[768,11...) custom-call(s32[4]{0:T(128)} %pad_add_fusion.1.place_ref, ...), custom_call_target="tpu_custom_call" | custom-call | flops 1 | bytes 1 | tf_op jit(solution)/shard_map/pallas_call | solution.py:339
  70.5 3.6 %collective-permute-start.12 = (bf16[768,384]{1,0:T(8,128)(2,1)}, bf16[768,384]{1,0:T(8,128)(2,1)S(1)}, u32[]{:S(2)}, u32[]{:S(2)}) collective-permute-start(bf16[768,384]{1,0:T(8,128)(2,1)} %get-tuple-element.91.own_out_ref), channel_id=1, source_target_pairs={{0,2},{2,0},{1,3},{3,1},{4,6},{6,4},{5,7},{7,5},{8,10},{10,8},{9,1... | collective-permute-start | bytes 1769480 | tf_op jit(solution)/shard_map/ppermute | solution.py:351
  74.2 1.0 slice.59
  77.1 11.9 %shard_map.273 = (f32[256,768]{1,0:T(8,128)}, f32[128,768]{1,0:T(8,128)}, f32[128,768]{1,0:T(8,128)}, f32[256,768]{1,0:T(8,128)}, f32[1,1536]{1,0:T(1,128)}, /*i...) custom-call(s32[4]{0:T(128)} %pad_add_fusion.1.place_ref, ...), custom_call_target="tpu_custom_call" | custom-call | flops 1 | bytes 1 | tf_op jit(solution)/shard_map/pallas_call | solution.py:339
  89.0 2.9 %collective-permute-start.26 = (f32[256,768]{1,0:T(8,128)}, f32[256,768]{1,0:T(8,128)S(1)}, u32[]{:S(2)}, u32[]{:S(2)}) collective-permute-start(f32[256,768]{1,0:T(8,128)} %get-tuple-element.98.own_grad_ref), channel_id=1, source_target_pairs={{0,2},{2,0},{1,3},{3,1},{4,6},{6,4},{5,7},{7,5},{8,10},{10,8},{9,1... | collective-permute-start | bytes 2359304 | tf_op jit(solution)/shard_map/ppermute | solution.py:351
  94.0 1.1 collective-permute-start.29
  95.1 2.1 %collective-permute-start.28 = (bf16[192,1536]{1,0:T(8,128)(2,1)}, bf16[192,1536]{1,0:T(8,128)(2,1)S(1)}, u32[]{:S(2)}, u32[]{:S(2)}) collective-permute-start(bf16[192,1536]{1,0:T(8,128)(2,1)} %get-tuple-element.117), channel_id=1, source_target_pairs={{0,4},{1,5},{2,14},{3,15},{4,8},{5,9},{6,2},{7,3},{8,12},{9,13},{1... | collective-permute-start | bytes 1769480 | tf_op jit(solution)/shard_map/ppermute | solution.py:409
  98.3 9.4 %shard_map.274 = (bf16[192,1664]{1,0:T(8,128)(2,1)}, bf16[192,1664]{1,0:T(8,128)(2,1)}, bf16[192,1664]{1,0:T(8,128)(2,1)}, bf16[192,1664]{1,0:T(8,128)(2,1)}, f3...) custom-call(s32[4]{0:T(128)} %pad_add_fusion.1.place_ref, bf16[256,768]{1,0:T(8,128)(2,1)} %get-tuple-element.84.x_ref, ...), custom_call_target="tpu_custom_call" | custom-call | flops 1 | bytes 1 | tf_op jit(solution)/shard_map/pallas_call | solution.py:339
  107.8 1.8 %collective-permute-start.30 = (bf16[192,1664]{1,0:T(8,128)(2,1)}, bf16[192,1664]{1,0:T(8,128)(2,1)S(1)}, u32[]{:S(2)}, u32[]{:S(2)}) collective-permute-start(bf16[192,1664]{1,0:T(8,128)(2,1)} %get-tuple-element.123), channel_id=1, source_target_pairs={{0,32},{1,33},{2,98},{3,99},{4,36},{5,37},{6,102},{7,103},{8,40},{... | collective-permute-start | bytes 1916936 | tf_op jit(solution)/shard_map/ppermute | solution.py:409
  111.5 1.8 %collective-permute-start.35 = (bf16[384,768]{1,0:T(8,128)(2,1)}, bf16[384,768]{1,0:T(8,128)(2,1)S(1)}, u32[]{:S(2)}, u32[]{:S(2)}) collective-permute-start(bf16[384,768]{1,0:T(8,128)(2,1)} %add_convert_fusion.4), channel_id=1, source_target_pairs={{0,1},{1,16},{2,19},{3,2},{4,5},{5,20},{6,23},{7,6},{8,9},{9,24},{... | collective-permute-start | bytes 1769480 | tf_op jit(solution)/shard_map/ppermute | solution.py:409
  114.2 2.4 %shard_map.275 = bf16[128,768]{1,0:T(8,128)(2,1)} custom-call(s32[4]{0:T(128)} %pad_add_fusion.1.place_ref, bf16[256,768]{1,0:T(8,128)(2,1)} %get-tuple-element.84.x_ref, f32[128,768]{1,0:T(8,128)} %get-tuple-element.114.own_x_ref, f32[128,768]{1,0:T(8,128)} %copy-done.16, f32[128,768]{1,0:T(8,128)} %get-tuple-element.121.gh_ref, ...), custom_call_target="tpu_custom_call" | custom-call | flops 1 | bytes 1 | tf_op jit(solution)/shard_map/pallas_call | solution.py:339
  116.6 1.8 %pad_maximum_fusion.4 = bf16[128,1536]{1,0:T(8,128)(2,1)} fusion(bf16[128,768]{1,0:T(8,128)(2,1)} %shard_map.275, bf16[128,768]{1,0:T(8,128)(2,1)S(1)} %add_convert_fusion.7), kind=kLoop, calls=%fused_computation.13 | loop fusion | flops 786432 | bytes 786432 | tf_op jit(solution)/shard_map/concatenate | solution.py:587
  118.4 4.7 %collective-permute-done.30 = bf16[192,1664]{1,0:T(8,128)(2,1)S(1)} collective-permute-done((bf16[192,1664]{1,0:T(8,128)(2,1)}, bf16[192,1664]{1,0:T(8,128)(2,1)S(1)}, u32[]{:S(2)}, u32[]{:S(2)}) %collective-permute-start.30) | collective-permute-done | bytes 639008 | tf_op jit(solution)/shard_map/ppermute | solution.py:409
  123.1 3.3 %collective-permute-done.31 = bf16[192,1664]{1,0:T(8,128)(2,1)S(1)} collective-permute-done((bf16[192,1664]{1,0:T(8,128)(2,1)}, bf16[192,1664]{1,0:T(8,128)(2,1)S(1)}, u32[]{:S(2)}, u32[]{:S(2)}) %collective-permute-start.31) | collective-permute-done | bytes 639008 | tf_op jit(solution)/shard_map/ppermute | solution.py:409
  126.7 1.3 add_convert_fusion.2
  128.0 5.5 %collective-permute-done.33 = bf16[192,1536]{1,0:T(8,128)(2,1)S(1)} collective-permute-done((bf16[192,1536]{1,0:T(8,128)(2,1)}, bf16[192,1536]{1,0:T(8,128)(2,1)S(1)}, u32[]{:S(2)}, u32[]{:S(2)}) %collective-permute-start.33) | collective-permute-done | bytes 589856 | tf_op jit(solution)/shard_map/ppermute | solution.py:409
  133.9 2.2 %collective-permute-done.32 = bf16[192,1664]{1,0:T(8,128)(2,1)S(1)} collective-permute-done((bf16[192,1664]{1,0:T(8,128)(2,1)S(1)}, bf16[192,1664]{1,0:T(8,128)(2,1)S(1)}, u32[]{:S(2)}, u32[]{:S(2)}) %collective-permute-start.32) | collective-permute-done | bytes 639008 | tf_op jit(solution)/shard_map/ppermute | solution.py:409
  136.5 1.5 collective-permute-start.39
  138.0 1.2 collective-permute-start.40
  139.2 1.5 collective-permute-start.42
  140.8 3.9 %collective-permute-done.38 = bf16[2,24,1664]{2,1,0:T(8,128)(2,1)S(1)} collective-permute-done((bf16[2,24,1664]{2,1,0:T(8,128)(2,1)S(1)}, bf16[2,24,1664]{2,1,0:T(8,128)(2,1)S(1)}, u32[]{:S(2)}, u32[]{:S(2)}) %collective-permute-start.38) | collective-permute-done | bytes 159776 | tf_op jit(solution)/shard_map/ppermute | solution.py:370
  144.7 4.9 %collective-permute-start.37 = (bf16[128,1536]{1,0:T(8,128)(2,1)}, bf16[128,1536]{1,0:T(8,128)(2,1)S(1)}, u32[]{:S(2)}, u32[]{:S(2)}) collective-permute-start(bf16[128,1536]{1,0:T(8,128)(2,1)} %pad_maximum_fusion.4), channel_id=1, source_target_pairs={{0,0},{1,2},{2,1},{3,3},{4,4},{5,6},{6,5},{7,7},{8,8},{9,10},{10,9... | collective-permute-start | bytes 1179656 | tf_op jit(solution)/shard_map/ppermute | solution.py:359
  149.8 3.8 %collective-permute-done.43 = bf16[192,768]{1,0:T(8,128)(2,1)S(1)} collective-permute-done((bf16[192,768]{1,0:T(8,128)(2,1)S(1)}, bf16[192,768]{1,0:T(8,128)(2,1)S(1)}, u32[]{:S(2)}, u32[]{:S(2)}) %collective-permute-start.43) | collective-permute-done | bytes 294944 | tf_op jit(solution)/shard_map/ppermute | solution.py:370
  154.8 7.2 %all-to-all-start.1 = ((bf16[8,6,3200]{2,1,0:T(8,128)(2,1)}), bf16[8,6,3200]{2,1,0:T(8,128)(2,1)S(1)}, u32[]{:S(2)}, u32[]{:S(2)}) async-start(bf16[8,6,3200]{2,1,0:T(8,128)(2,1)} %reshape.121), calls=%async_computation.1 | async-start | bytes 819200 | tf_op jit(solution)/shard_map/all_to_all | solution.py:593
  162.1 1.9 %collective-permute-start.45 = (bf16[24,768]{1,0:T(8,128)(2,1)S(1)}, bf16[24,768]{1,0:T(8,128)(2,1)S(1)}, u32[]{:S(2)}, u32[]{:S(2)}) collective-permute-start(bf16[24,768]{1,0:T(8,128)(2,1)S(1)} %get-tuple-element.189), channel_id=1, source_target_pairs={{0,8},{4,12},{8,0},{12,4},{1,9},{5,13},{9,1},{13,5},{2,10},{6,14},... | collective-permute-start | bytes 110600 | tf_op jit(solution)/shard_map/ppermute | solution.py:370
  167.4 2.8 %all-to-all-done.1.got_ref = bf16[8,6,3200]{2,1,0:T(8,128)(2,1)S(1)} async-done(((bf16[8,6,3200]{2,1,0:T(8,128)(2,1)}), bf16[8,6,3200]{2,1,0:T(8,128)(2,1)S(1)}, u32[]{:S(2)}, u32[]{:S(2)}) %all-to-all-start.1) | async-done | bytes 307232 | tf_op jit(solution)/shard_map/all_to_all | solution.py:593
  (156 shorter events, 24.2 us)
Async XLA Ops:
  2.6 22.6 %collective-permute-start.5 = (bf16[24,768]{1,0:T(8,128)(2,1)}, bf16[24,768]{1,0:T(8,128)(2,1)S(1)}, u32[]{:S(2)}, u32[]{:S(2)}) collective-permute-start(bf16[24,768]{1,0:T(8,128)(2,1)} %param.29), channel_id=1, source_target_pairs={{0,96},{32,0},{64,32},{96,64},{1,97},{33,1},{65,33},{97,65},{2,98}... | collective-permute-start | bytes 110600 | tf_op jit(solution)/shard_map/ppermute | solution.py:370
  5.9 19.3 %collective-permute-start.6 = (bf16[24,768]{1,0:T(8,128)(2,1)}, bf16[24,768]{1,0:T(8,128)(2,1)S(1)}, u32[]{:S(2)}, u32[]{:S(2)}) collective-permute-start(bf16[24,768]{1,0:T(8,128)(2,1)} %param.29), channel_id=1, source_target_pairs={{0,64},{32,96},{64,0},{96,32},{1,65},{33,97},{65,1},{97,33},{2,66}... | collective-permute-start | bytes 110600 | tf_op jit(solution)/shard_map/ppermute | solution.py:370
  6.5 19.5 %collective-permute-start.7 = (bf16[24,768]{1,0:T(8,128)(2,1)}, bf16[24,768]{1,0:T(8,128)(2,1)S(1)}, u32[]{:S(2)}, u32[]{:S(2)}) collective-permute-start(bf16[24,768]{1,0:T(8,128)(2,1)} %param.29), channel_id=1, source_target_pairs={{0,32},{32,64},{64,96},{96,0},{1,33},{33,65},{65,97},{97,1},{2,34}... | collective-permute-start | bytes 110600 | tf_op jit(solution)/shard_map/ppermute | solution.py:370
  7.1 14.2 %all-to-all-start = ((bf16[8,6,3200]{2,1,0:T(8,128)(2,1)}), bf16[8,6,3200]{2,1,0:T(8,128)(2,1)S(1)}, u32[]{:S(2)}, u32[]{:S(2)}) async-start(bf16[8,6,3200]{2,1,0:T(8,128)(2,1)} %shard_map.271), calls=%async_computation | async-start | bytes 819200 | tf_op jit(solution)/shard_map/all_to_all | solution.py:485
  14.0 14.2 %collective-permute-start = (bf16[128,1536]{1,0:T(8,128)(2,1)S(1)}, bf16[128,1536]{1,0:T(8,128)(2,1)S(1)}, u32[]{:S(2)}, u32[]{:S(2)}) collective-permute-start(bf16[128,1536]{1,0:T(8,128)(2,1)S(1)} %pad_maximum_fusion.3), channel_id=1, source_target_pairs={{0,0},{1,2},{2,1},{3,3},{4,4},{5,6},{6,5},{7,7},{8,8},{9,10},{10,9... | collective-permute-start | bytes 1179656 | tf_op jit(solution)/shard_map/ppermute | solution.py:359
  21.4 9.8 %collective-permute-start.2 = (bf16[2,24,1664]{2,1,0:T(8,128)(2,1)S(1)}, bf16[2,24,1664]{2,1,0:T(8,128)(2,1)S(1)}, u32[]{:S(2)}, u32[]{:S(2)}) collective-permute-start(bf16[2,24,1664]{2,1,0:T(8,128)(2,1)S(1)} %slice.76), channel_id=1, source_target_pairs={{0,12},{4,0},{8,4},{12,8},{1,13},{5,1},{9,5},{13,9},{2,14},{6,2},{... | collective-permute-start | bytes 479240 | tf_op jit(solution)/shard_map/ppermute | solution.py:370
  25.3 7.5 %collective-permute-start.3 = (bf16[2,24,1664]{2,1,0:T(8,128)(2,1)S(1)}, bf16[2,24,1664]{2,1,0:T(8,128)(2,1)S(1)}, u32[]{:S(2)}, u32[]{:S(2)}) collective-permute-start(bf16[2,24,1664]{2,1,0:T(8,128)(2,1)S(1)} %slice.76), channel_id=1, source_target_pairs={{0,8},{4,12},{8,0},{12,4},{1,9},{5,13},{9,1},{13,5},{2,10},{6,14},... | collective-permute-start | bytes 479240 | tf_op jit(solution)/shard_map/ppermute | solution.py:370
  25.3 10.4 %collective-permute-start.4 = (bf16[2,24,1664]{2,1,0:T(8,128)(2,1)S(1)}, bf16[2,24,1664]{2,1,0:T(8,128)(2,1)S(1)}, u32[]{:S(2)}, u32[]{:S(2)}) collective-permute-start(bf16[2,24,1664]{2,1,0:T(8,128)(2,1)S(1)} %slice.76), channel_id=1, source_target_pairs={{0,4},{4,8},{8,12},{12,0},{1,5},{5,9},{9,13},{13,1},{2,6},{6,10},{... | collective-permute-start | bytes 479240 | tf_op jit(solution)/shard_map/ppermute | solution.py:370
  26.0 12.0 %collective-permute-start.13 = (bf16[48,1536]{1,0:T(8,128)(2,1)S(1)}, bf16[48,1536]{1,0:T(8,128)(2,1)S(1)}, u32[]{:S(2)}, u32[]{:S(2)}) collective-permute-start(bf16[48,1536]{1,0:T(8,128)(2,1)S(1)} %bitcast.56), channel_id=1, source_target_pairs={{0,96},{32,0},{64,32},{96,64},{1,97},{33,1},{65,33},{97,65},{2,98}... | collective-permute-start | bytes 442376 | tf_op jit(solution)/shard_map/ppermute | solution.py:370
  28.2 9.8 %collective-permute-start.14 = (bf16[48,1536]{1,0:T(8,128)(2,1)S(1)}, bf16[48,1536]{1,0:T(8,128)(2,1)S(1)}, u32[]{:S(2)}, u32[]{:S(2)}) collective-permute-start(bf16[48,1536]{1,0:T(8,128)(2,1)S(1)} %bitcast.57), channel_id=1, source_target_pairs={{0,64},{32,96},{64,0},{96,32},{1,65},{33,97},{65,1},{97,33},{2,66}... | collective-permute-start | bytes 442376 | tf_op jit(solution)/shard_map/ppermute | solution.py:370
  31.3 7.6 %collective-permute-start.15 = (bf16[48,1536]{1,0:T(8,128)(2,1)S(1)}, bf16[48,1536]{1,0:T(8,128)(2,1)S(1)}, u32[]{:S(2)}, u32[]{:S(2)}) collective-permute-start(bf16[48,1536]{1,0:T(8,128)(2,1)S(1)} %bitcast.58), channel_id=1, source_target_pairs={{0,32},{32,64},{64,96},{96,0},{1,33},{33,65},{65,97},{97,1},{2,34}... | collective-permute-start | bytes 442376 | tf_op jit(solution)/shard_map/ppermute | solution.py:370
  32.8 17.8 %collective-permute-start.1 = (bf16[128,1536]{1,0:T(8,128)(2,1)S(1)}, bf16[128,1536]{1,0:T(8,128)(2,1)S(1)}, u32[]{:S(2)}, u32[]{:S(2)}) collective-permute-start(bf16[128,1536]{1,0:T(8,128)(2,1)S(1)} %collective-permute-done), channel_id=1, source_target_pairs={{0,2},{2,0},{1,3},{3,1},{4,6},{6,4},{5,7},{7,5},{8,10},{10,8},{9,1... | collective-permute-start | bytes 1179656 | tf_op jit(solution)/shard_map/ppermute | solution.py:351
  35.9 13.1 %collective-permute-start.8 = (bf16[192,1664]{1,0:T(8,128)(2,1)S(1)}, bf16[192,1664]{1,0:T(8,128)(2,1)S(1)}, u32[]{:S(2)}, u32[]{:S(2)}) collective-permute-start(bf16[192,1664]{1,0:T(8,128)(2,1)S(1)} %bitcast.51), channel_id=1, source_target_pairs={{0,32},{1,33},{2,98},{3,99},{4,36},{5,37},{6,102},{7,103},{8,40},{... | collective-permute-start | bytes 1916936 | tf_op jit(solution)/shard_map/ppermute | solution.py:409
  39.0 4.4 %collective-permute-start.19 = (bf16[96,768]{1,0:T(8,128)(2,1)S(1)}, bf16[96,768]{1,0:T(8,128)(2,1)S(1)}, u32[]{:S(2)}, u32[]{:S(2)}) collective-permute-start(bf16[96,768]{1,0:T(8,128)(2,1)S(1)} %pad_maximum_fusion.9), channel_id=1, source_target_pairs={{0,12},{4,0},{8,4},{12,8},{1,13},{5,1},{9,5},{13,9},{2,14},{6,2},{... | collective-permute-start | bytes 442376 | tf_op jit(solution)/shard_map/ppermute | solution.py:370
  40.2 5.6 %collective-permute-start.20 = (bf16[96,768]{1,0:T(8,128)(2,1)S(1)}, bf16[96,768]{1,0:T(8,128)(2,1)S(1)}, u32[]{:S(2)}, u32[]{:S(2)}) collective-permute-start(bf16[96,768]{1,0:T(8,128)(2,1)S(1)} %pad_maximum_fusion.9), channel_id=1, source_target_pairs={{0,8},{4,12},{8,0},{12,4},{1,9},{5,13},{9,1},{13,5},{2,10},{6,14},... | collective-permute-start | bytes 442376 | tf_op jit(solution)/shard_map/ppermute | solution.py:370
  40.2 7.1 %collective-permute-start.21 = (bf16[96,768]{1,0:T(8,128)(2,1)S(1)}, bf16[96,768]{1,0:T(8,128)(2,1)S(1)}, u32[]{:S(2)}, u32[]{:S(2)}) collective-permute-start(bf16[96,768]{1,0:T(8,128)(2,1)S(1)} %pad_maximum_fusion.9), channel_id=1, source_target_pairs={{0,4},{4,8},{8,12},{12,0},{1,5},{5,9},{9,13},{13,1},{2,6},{6,10},{... | collective-permute-start | bytes 442376 | tf_op jit(solution)/shard_map/ppermute | solution.py:370
  43.3 11.2 %collective-permute-start.16 = (bf16[192,1536]{1,0:T(8,128)(2,1)S(1)}, bf16[192,1536]{1,0:T(8,128)(2,1)}, u32[]{:S(2)}, u32[]{:S(2)}) collective-permute-start(bf16[192,1536]{1,0:T(8,128)(2,1)S(1)} %pad_maximum_fusion.1.up_0), channel_id=1, source_target_pairs={{0,4},{1,5},{2,14},{3,15},{4,8},{5,9},{6,2},{7,3},{8,12},{9,13},{1... | collective-permute-start | bytes 1769480 | tf_op jit(solution)/shard_map/ppermute | solution.py:409
  45.8 10.9 %collective-permute-start.9 = (bf16[192,1664]{1,0:T(8,128)(2,1)S(1)}, bf16[192,1664]{1,0:T(8,128)(2,1)S(1)}, u32[]{:S(2)}, u32[]{:S(2)}) collective-permute-start(bf16[192,1664]{1,0:T(8,128)(2,1)S(1)} %bitcast.52), channel_id=1, source_target_pairs={{0,96},{1,97},{2,34},{3,35},{4,100},{5,101},{6,38},{7,39},{8,104},... | collective-permute-start | bytes 1916936 | tf_op jit(solution)/shard_map/ppermute | solution.py:409
  47.4 13.0 %collective-permute-start.22 = (bf16[384,768]{1,0:T(8,128)(2,1)S(1)}, bf16[384,768]{1,0:T(8,128)(2,1)}, u32[]{:S(2)}, u32[]{:S(2)}) collective-permute-start(bf16[384,768]{1,0:T(8,128)(2,1)S(1)} %pad_maximum_fusion.2.down_0), channel_id=1, source_target_pairs={{0,1},{1,16},{2,19},{3,2},{4,5},{5,20},{6,23},{7,6},{8,9},{9,24},{... | collective-permute-start | bytes 1769480 | tf_op jit(solution)/shard_map/ppermute | solution.py:409
  48.9 15.2 %collective-permute-start.10 = (bf16[192,1664]{1,0:T(8,128)(2,1)S(1)}, bf16[192,1664]{1,0:T(8,128)(2,1)S(1)}, u32[]{:S(2)}, u32[]{:S(2)}) collective-permute-start(bf16[192,1664]{1,0:T(8,128)(2,1)S(1)} %collective-permute-done.8.part_1), channel_id=1, source_target_pairs={{0,32},{1,33},{2,98},{3,99},{4,36},{5,37},{6,102},{7,103},{8,40},{... | collective-permute-start | bytes 1916936 | tf_op jit(solution)/shard_map/ppermute | solution.py:409
  50.6 23.5 %collective-permute-start.17 = (bf16[192,1536]{1,0:T(8,128)(2,1)S(1)}, bf16[192,1536]{1,0:T(8,128)(2,1)}, u32[]{:S(2)}, u32[]{:S(2)}) collective-permute-start(bf16[192,1536]{1,0:T(8,128)(2,1)S(1)} %pad_maximum_fusion.1.up_0), channel_id=1, source_target_pairs={{0,12},{1,13},{2,6},{3,7},{4,0},{5,1},{6,10},{7,11},{8,4},{9,5},{1... | collective-permute-start | bytes 1769480 | tf_op jit(solution)/shard_map/ppermute | solution.py:409
  54.5 21.7 %collective-permute-start.23 = (bf16[384,768]{1,0:T(8,128)(2,1)S(1)}, bf16[384,768]{1,0:T(8,128)(2,1)}, u32[]{:S(2)}, u32[]{:S(2)}) collective-permute-start(bf16[384,768]{1,0:T(8,128)(2,1)S(1)} %pad_maximum_fusion.2.down_0), channel_id=1, source_target_pairs={{0,17},{1,0},{2,3},{3,18},{4,21},{5,4},{6,7},{7,22},{8,25},{9,8},{... | collective-permute-start | bytes 1769480 | tf_op jit(solution)/shard_map/ppermute | solution.py:409
  56.7 19.5 %collective-permute-start.18 = (bf16[192,1536]{1,0:T(8,128)(2,1)}, bf16[192,1536]{1,0:T(8,128)(2,1)}, u32[]{:S(2)}, u32[]{:S(2)}) collective-permute-start(bf16[192,1536]{1,0:T(8,128)(2,1)} %collective-permute-done.16.up_1), channel_id=1, source_target_pairs={{0,4},{1,5},{2,14},{3,15},{4,8},{5,9},{6,2},{7,3},{8,12},{9,13},{1... | collective-permute-start | bytes 1769480 | tf_op jit(solution)/shard_map/ppermute | solution.py:409
  60.5 15.7 %collective-permute-start.24 = (bf16[384,768]{1,0:T(8,128)(2,1)}, bf16[384,768]{1,0:T(8,128)(2,1)}, u32[]{:S(2)}, u32[]{:S(2)}) collective-permute-start(bf16[384,768]{1,0:T(8,128)(2,1)} %collective-permute-done.22.down_1), channel_id=1, source_target_pairs={{0,1},{1,16},{2,19},{3,2},{4,5},{5,20},{6,23},{7,6},{8,9},{9,24},{... | collective-permute-start | bytes 1769480 | tf_op jit(solution)/shard_map/ppermute | solution.py:409
  70.5 5.7 %collective-permute-start.12 = (bf16[768,384]{1,0:T(8,128)(2,1)}, bf16[768,384]{1,0:T(8,128)(2,1)S(1)}, u32[]{:S(2)}, u32[]{:S(2)}) collective-permute-start(bf16[768,384]{1,0:T(8,128)(2,1)} %get-tuple-element.91.own_out_ref), channel_id=1, source_target_pairs={{0,2},{2,0},{1,3},{3,1},{4,6},{6,4},{5,7},{7,5},{8,10},{10,8},{9,1... | collective-permute-start | bytes 1769480 | tf_op jit(solution)/shard_map/ppermute | solution.py:351
  89.0 5.0 %collective-permute-start.26 = (f32[256,768]{1,0:T(8,128)}, f32[256,768]{1,0:T(8,128)S(1)}, u32[]{:S(2)}, u32[]{:S(2)}) collective-permute-start(f32[256,768]{1,0:T(8,128)} %get-tuple-element.98.own_grad_ref), channel_id=1, source_target_pairs={{0,2},{2,0},{1,3},{3,1},{4,6},{6,4},{5,7},{7,5},{8,10},{10,8},{9,1... | collective-permute-start | bytes 2359304 | tf_op jit(solution)/shard_map/ppermute | solution.py:351
  91.9 6.3 %collective-permute-start.25 = (f32[128,768]{1,0:T(8,128)}, f32[128,768]{1,0:T(8,128)S(1)}, u32[]{:S(2)}, u32[]{:S(2)}) collective-permute-start(f32[128,768]{1,0:T(8,128)} %get-tuple-element.96), channel_id=1, source_target_pairs={{0,2},{2,0},{1,3},{3,1},{4,6},{6,4},{5,7},{7,5},{8,10},{10,8},{9,1... | collective-permute-start | bytes 1179656 | tf_op jit(solution)/shard_map/ppermute | solution.py:351
  94.0 15.6 %collective-permute-start.29 = (bf16[384,768]{1,0:T(8,128)(2,1)}, bf16[384,768]{1,0:T(8,128)(2,1)S(1)}, u32[]{:S(2)}, u32[]{:S(2)}) collective-permute-start(bf16[384,768]{1,0:T(8,128)(2,1)} %get-tuple-element.119), channel_id=1, source_target_pairs={{0,1},{1,16},{2,19},{3,2},{4,5},{5,20},{6,23},{7,6},{8,9},{9,24},{... | collective-permute-start | bytes 1769480 | tf_op jit(solution)/shard_map/ppermute | solution.py:409
  95.1 16.3 %collective-permute-start.28 = (bf16[192,1536]{1,0:T(8,128)(2,1)}, bf16[192,1536]{1,0:T(8,128)(2,1)S(1)}, u32[]{:S(2)}, u32[]{:S(2)}) collective-permute-start(bf16[192,1536]{1,0:T(8,128)(2,1)} %get-tuple-element.117), channel_id=1, source_target_pairs={{0,4},{1,5},{2,14},{3,15},{4,8},{5,9},{6,2},{7,3},{8,12},{9,13},{1... | collective-permute-start | bytes 1769480 | tf_op jit(solution)/shard_map/ppermute | solution.py:409
  107.7 5.7 %collective-permute-start.27 = (f32[128,768]{1,0:T(8,128)}, f32[128,768]{1,0:T(8,128)S(1)}, u32[]{:S(2)}, u32[]{:S(2)}) collective-permute-start(f32[128,768]{1,0:T(8,128)} %get-tuple-element.115), channel_id=1, source_target_pairs={{0,2},{2,0},{1,3},{3,1},{4,6},{6,4},{5,7},{7,5},{8,10},{10,8},{9,1... | collective-permute-start | bytes 1179656 | tf_op jit(solution)/shard_map/ppermute | solution.py:351
  107.8 15.3 %collective-permute-start.30 = (bf16[192,1664]{1,0:T(8,128)(2,1)}, bf16[192,1664]{1,0:T(8,128)(2,1)S(1)}, u32[]{:S(2)}, u32[]{:S(2)}) collective-permute-start(bf16[192,1664]{1,0:T(8,128)(2,1)} %get-tuple-element.123), channel_id=1, source_target_pairs={{0,32},{1,33},{2,98},{3,99},{4,36},{5,37},{6,102},{7,103},{8,40},{... | collective-permute-start | bytes 1916936 | tf_op jit(solution)/shard_map/ppermute | solution.py:409
  109.6 16.8 %collective-permute-start.31 = (bf16[192,1664]{1,0:T(8,128)(2,1)}, bf16[192,1664]{1,0:T(8,128)(2,1)S(1)}, u32[]{:S(2)}, u32[]{:S(2)}) collective-permute-start(bf16[192,1664]{1,0:T(8,128)(2,1)} %get-tuple-element.124), channel_id=1, source_target_pairs={{0,96},{1,97},{2,34},{3,35},{4,100},{5,101},{6,38},{7,39},{8,104},... | collective-permute-start | bytes 1916936 | tf_op jit(solution)/shard_map/ppermute | solution.py:409
  109.6 17.1 %collective-permute-start.36 = (bf16[384,768]{1,0:T(8,128)(2,1)}, bf16[384,768]{1,0:T(8,128)(2,1)}, u32[]{:S(2)}, u32[]{:S(2)}) collective-permute-start(bf16[384,768]{1,0:T(8,128)(2,1)} %get-tuple-element.132), channel_id=1, source_target_pairs={{0,17},{1,0},{2,3},{3,18},{4,21},{5,4},{6,7},{7,22},{8,25},{9,8},{... | collective-permute-start | bytes 1769480 | tf_op jit(solution)/shard_map/ppermute | solution.py:409
  111.5 15.2 %collective-permute-start.35 = (bf16[384,768]{1,0:T(8,128)(2,1)}, bf16[384,768]{1,0:T(8,128)(2,1)S(1)}, u32[]{:S(2)}, u32[]{:S(2)}) collective-permute-start(bf16[384,768]{1,0:T(8,128)(2,1)} %add_convert_fusion.4), channel_id=1, source_target_pairs={{0,1},{1,16},{2,19},{3,2},{4,5},{5,20},{6,23},{7,6},{8,9},{9,24},{... | collective-permute-start | bytes 1769480 | tf_op jit(solution)/shard_map/ppermute | solution.py:409
  113.4 13.2 %collective-permute-start.34 = (bf16[192,1536]{1,0:T(8,128)(2,1)S(1)}, bf16[192,1536]{1,0:T(8,128)(2,1)S(1)}, u32[]{:S(2)}, u32[]{:S(2)}) collective-permute-start(bf16[192,1536]{1,0:T(8,128)(2,1)S(1)} %add_convert_fusion.5), channel_id=1, source_target_pairs={{0,4},{1,5},{2,14},{3,15},{4,8},{5,9},{6,2},{7,3},{8,12},{9,13},{1... | collective-permute-start | bytes 1769480 | tf_op jit(solution)/shard_map/ppermute | solution.py:409
  123.1 10.4 %collective-permute-start.33 = (bf16[192,1536]{1,0:T(8,128)(2,1)}, bf16[192,1536]{1,0:T(8,128)(2,1)S(1)}, u32[]{:S(2)}, u32[]{:S(2)}) collective-permute-start(bf16[192,1536]{1,0:T(8,128)(2,1)} %get-tuple-element.129), channel_id=1, source_target_pairs={{0,12},{1,13},{2,6},{3,7},{4,0},{5,1},{6,10},{7,11},{8,4},{9,5},{1... | collective-permute-start | bytes 1769480 | tf_op jit(solution)/shard_map/ppermute | solution.py:409
  126.5 9.6 %collective-permute-start.32 = (bf16[192,1664]{1,0:T(8,128)(2,1)S(1)}, bf16[192,1664]{1,0:T(8,128)(2,1)S(1)}, u32[]{:S(2)}, u32[]{:S(2)}) collective-permute-start(bf16[192,1664]{1,0:T(8,128)(2,1)S(1)} %add_convert_fusion.1), channel_id=1, source_target_pairs={{0,32},{1,33},{2,98},{3,99},{4,36},{5,37},{6,102},{7,103},{8,40},{... | collective-permute-start | bytes 1916936 | tf_op jit(solution)/shard_map/ppermute | solution.py:409
  133.8 15.9 %collective-permute-start.41 = (bf16[192,768]{1,0:T(8,128)(2,1)S(1)}, bf16[192,768]{1,0:T(8,128)(2,1)S(1)}, u32[]{:S(2)}, u32[]{:S(2)}) collective-permute-start(bf16[192,768]{1,0:T(8,128)(2,1)S(1)} %pad_maximum_fusion.6), channel_id=1, source_target_pairs={{0,32},{32,64},{64,96},{96,0},{1,33},{33,65},{65,97},{97,1},{2,34}... | collective-permute-start | bytes 884744 | tf_op jit(solution)/shard_map/ppermute | solution.py:370
  136.5 8.3 %collective-permute-start.38 = (bf16[2,24,1664]{2,1,0:T(8,128)(2,1)S(1)}, bf16[2,24,1664]{2,1,0:T(8,128)(2,1)S(1)}, u32[]{:S(2)}, u32[]{:S(2)}) collective-permute-start(bf16[2,24,1664]{2,1,0:T(8,128)(2,1)S(1)} %get-tuple-element.155), channel_id=1, source_target_pairs={{0,4},{4,8},{8,12},{12,0},{1,5},{5,9},{9,13},{13,1},{2,6},{6,10},{... | collective-permute-start | bytes 479240 | tf_op jit(solution)/shard_map/ppermute | solution.py:370
  136.5 8.2 %collective-permute-start.39 = (bf16[2,24,1664]{2,1,0:T(8,128)(2,1)S(1)}, bf16[2,24,1664]{2,1,0:T(8,128)(2,1)S(1)}, u32[]{:S(2)}, u32[]{:S(2)}) collective-permute-start(bf16[2,24,1664]{2,1,0:T(8,128)(2,1)S(1)} %get-tuple-element.157), channel_id=1, source_target_pairs={{0,8},{4,12},{8,0},{12,4},{1,9},{5,13},{9,1},{13,5},{2,10},{6,14},... | collective-permute-start | bytes 479240 | tf_op jit(solution)/shard_map/ppermute | solution.py:370
  138.0 11.7 %collective-permute-start.40 = (bf16[2,24,1664]{2,1,0:T(8,128)(2,1)S(1)}, bf16[2,24,1664]{2,1,0:T(8,128)(2,1)S(1)}, u32[]{:S(2)}, u32[]{:S(2)}) collective-permute-start(bf16[2,24,1664]{2,1,0:T(8,128)(2,1)S(1)} %get-tuple-element.156), channel_id=1, source_target_pairs={{0,12},{4,0},{8,4},{12,8},{1,13},{5,1},{9,5},{13,9},{2,14},{6,2},{... | collective-permute-start | bytes 479240 | tf_op jit(solution)/shard_map/ppermute | solution.py:370
  139.2 10.6 %collective-permute-start.42 = (bf16[192,768]{1,0:T(8,128)(2,1)S(1)}, bf16[192,768]{1,0:T(8,128)(2,1)S(1)}, u32[]{:S(2)}, u32[]{:S(2)}) collective-permute-start(bf16[192,768]{1,0:T(8,128)(2,1)S(1)} %pad_maximum_fusion.7), channel_id=1, source_target_pairs={{0,64},{32,96},{64,0},{96,32},{1,65},{33,97},{65,1},{97,33},{2,66}... | collective-permute-start | bytes 884744 | tf_op jit(solution)/shard_map/ppermute | solution.py:370
  144.7 8.9 %collective-permute-start.43 = (bf16[192,768]{1,0:T(8,128)(2,1)S(1)}, bf16[192,768]{1,0:T(8,128)(2,1)S(1)}, u32[]{:S(2)}, u32[]{:S(2)}) collective-permute-start(bf16[192,768]{1,0:T(8,128)(2,1)S(1)} %pad_maximum_fusion.8), channel_id=1, source_target_pairs={{0,96},{32,0},{64,32},{96,64},{1,97},{33,1},{65,33},{97,65},{2,98}... | collective-permute-start | bytes 884744 | tf_op jit(solution)/shard_map/ppermute | solution.py:370
  144.7 20.1 %collective-permute-start.37 = (bf16[128,1536]{1,0:T(8,128)(2,1)}, bf16[128,1536]{1,0:T(8,128)(2,1)S(1)}, u32[]{:S(2)}, u32[]{:S(2)}) collective-permute-start(bf16[128,1536]{1,0:T(8,128)(2,1)} %pad_maximum_fusion.4), channel_id=1, source_target_pairs={{0,0},{1,2},{2,1},{3,3},{4,4},{5,6},{6,5},{7,7},{8,8},{9,10},{10,9... | collective-permute-start | bytes 1179656 | tf_op jit(solution)/shard_map/ppermute | solution.py:359
  154.8 15.5 %all-to-all-start.1 = ((bf16[8,6,3200]{2,1,0:T(8,128)(2,1)}), bf16[8,6,3200]{2,1,0:T(8,128)(2,1)S(1)}, u32[]{:S(2)}, u32[]{:S(2)}) async-start(bf16[8,6,3200]{2,1,0:T(8,128)(2,1)} %reshape.121), calls=%async_computation.1 | async-start | bytes 819200 | tf_op jit(solution)/shard_map/all_to_all | solution.py:593
  162.0 4.1 %collective-permute-start.44 = (bf16[24,768]{1,0:T(8,128)(2,1)S(1)}, bf16[24,768]{1,0:T(8,128)(2,1)S(1)}, u32[]{:S(2)}, u32[]{:S(2)}) collective-permute-start(bf16[24,768]{1,0:T(8,128)(2,1)S(1)} %get-tuple-element.190), channel_id=1, source_target_pairs={{0,4},{4,8},{8,12},{12,0},{1,5},{5,9},{9,13},{13,1},{2,6},{6,10},{... | collective-permute-start | bytes 110600 | tf_op jit(solution)/shard_map/ppermute | solution.py:370
  162.1 4.4 %collective-permute-start.45 = (bf16[24,768]{1,0:T(8,128)(2,1)S(1)}, bf16[24,768]{1,0:T(8,128)(2,1)S(1)}, u32[]{:S(2)}, u32[]{:S(2)}) collective-permute-start(bf16[24,768]{1,0:T(8,128)(2,1)S(1)} %get-tuple-element.189), channel_id=1, source_target_pairs={{0,8},{4,12},{8,0},{12,4},{1,9},{5,13},{9,1},{13,5},{2,10},{6,14},... | collective-permute-start | bytes 110600 | tf_op jit(solution)/shard_map/ppermute | solution.py:370
  164.0 3.4 %collective-permute-start.46 = (bf16[24,768]{1,0:T(8,128)(2,1)S(1)}, bf16[24,768]{1,0:T(8,128)(2,1)S(1)}, u32[]{:S(2)}, u32[]{:S(2)}) collective-permute-start(bf16[24,768]{1,0:T(8,128)(2,1)S(1)} %get-tuple-element.188), channel_id=1, source_target_pairs={{0,12},{4,0},{8,4},{12,8},{1,13},{5,1},{9,5},{13,9},{2,14},{6,2},{... | collective-permute-start | bytes 110600 | tf_op jit(solution)/shard_map/ppermute | solution.py:370
  (21 other events, 133.7 us)

commit v2 on v1

--- a/solution.py
+++ b/solution.py
@@ -91,6 +91,22 @@
     return same | earlier, key_slot >= query_slot - 2
 
 
+def bring(copies, sems):
+    started = [pltpu.make_async_copy(src, dst, sems.at[i]) for i, (src, dst) in enumerate(copies)]
+    for copy in started:
+        copy.start()
+    return [copy.wait for copy in started]
+
+
+def finish(waits):
+    for wait in waits:
+        wait()
+
+
+def row_block(at, size):
+    return pl.ds(pl.multiple_of(at * size, 64), size)
+
+
 def positions(core, at):
     way = 1 - 2 * core
     return at, lax.rem(at + 4 - way, 4), lax.rem(at + 4 + way, 4), lax.rem(at + 2, 4)
@@ -102,8 +118,8 @@
 
 
 def up_runs(t):
-    for yh, yl, z, x in np.ndindex(2, 2, 4, 4):
-        yield 96 * ((x * 2 + yh) * 4 + z) + 48 * t + 24 * yl, 24 * (((yh * 2 + yl) * 4 + z) * 4 + x)
+    for yh, yl, x, z in np.ndindex(2, 2, 4, 4):
+        yield 96 * ((x * 2 + yh) * 4 + z) + 48 * t + 24 * yl, 24 * (((yh * 2 + yl) * 4 + x) * 4 + z)
 
 
 def halves_kernel(qkv_ref, out_ref, up_ref, *refs):
@@ -199,59 +215,81 @@
     lse_ref[...] = kept
 
 
+def whole_copies(core, own_o, far_o, own_out, far_out, o_ref, out_ref):
+    here = pl.ds(pl.multiple_of(core * HALF, 128), HALF)
+    there = pl.ds(pl.multiple_of((1 - core) * HALF, 128), HALF)
+    return [
+        (own_o, o_ref.at[:, here]),
+        (far_o.at[pl.ds(0, OWN)], o_ref.at[pl.ds(OWN, OWN), there]),
+        (far_o.at[pl.ds(OWN, OWN)], o_ref.at[pl.ds(0, OWN), there]),
+        (own_out, out_ref.at[:, here]),
+        (far_out, out_ref.at[:, there]),
+    ]
+
+
 def mlp_kernel(
-    place_ref, x_ref, own_o_ref, far_o_ref, own_out_ref, far_out_ref, vec_ref, up_b_ref, g_ref, order_ref,
+    place_ref, vec_ref, up_b_ref, x_hbm, own_o, far_o, own_out, far_out, g_hbm, order_hbm,
     up_0, up_1, up_2, up_3, down_0, down_1, down_2, down_3,
     h_ref, m_own_ref, m_far_ref, grad_a_ref, grad_up_b_ref, grad_down_b_ref,
     gup_0, gup_1, gup_2, gup_3, gdown_0, gdown_1, gdown_2, gdown_3,
-    up_ref, down_ref, grad_up_ref, grad_down_ref,
+    o_ref, out_ref, x_ref, g_ref, order_ref, up_ref, down_ref, grad_up_ref, grad_down_ref, sems, out_sems,
 ):
     core = place_ref[0]
-    up_at, down_at = positions(core, place_ref[3]), positions(core, place_ref[2])
-    for up, at in zip((up_0, up_1, up_2, up_3), up_at):
-        up_ref[pl.ds(pl.multiple_of(at * BLOCK, 64), BLOCK), :] = up[...]
-    for down, at in zip((down_0, down_1, down_2, down_3), down_at):
-        down_ref[pl.ds(pl.multiple_of(at * DOWN_ROWS, 128), DOWN_ROWS), :] = down[...]
-    here = pl.multiple_of(core * HALF, 128)
-    there = pl.multiple_of((1 - core) * HALF, 128)
-    own_o = own_o_ref[...]
-    far_o = swap_halves(far_o_ref[...])
-    for out_ref, at in ((own_out_ref, here), (far_out_ref, there)):
-        part = dot_nn(own_o, out_ref[pl.ds(here, HALF), :]) + dot_nn(far_o, out_ref[pl.ds(there, HALF), :])
-        h_ref[:, pl.ds(at, HALF)] = part
-    hidden = x_ref[...].astype(F32) + (h_ref[...] + vec_ref[4:5, :])
+    ups = list(zip((up_0, up_1, up_2, up_3), (gup_0, gup_1, gup_2, gup_3), positions(core, place_ref[3])))
+    downs = list(zip((down_0, down_1, down_2, down_3), (gdown_0, gdown_1, gdown_2, gdown_3)))
+    units = [pl.ds(pl.multiple_of(at * DOWN_ROWS, 128), DOWN_ROWS) for at in positions(core, place_ref[2])]
+    pieces = [pl.ds(0, DOWN_ROWS), pl.ds(DOWN_ROWS, DOWN_ROWS)]
+    copies = whole_copies(core, own_o, far_o, own_out, far_out, o_ref, out_ref)
+    copies += [(x_hbm, x_ref), (order_hbm, order_ref)]
+    for half in range(2):
+        for e in range(2):
+            unit = units[2 * half + e]
+            copies += [(up.at[:, unit], up_ref.at[half, row_block(at, BLOCK), pieces[e]]) for up, _, at in ups]
+        if half == 0:
+            copies += [(g_hbm, g_ref)]
+        copies += [(downs[2 * half + e][0], down_ref.at[half, pieces[e]]) for e in range(2)]
+    waits = bring(copies, sems)
+    finish(waits[:6])
+    hidden = x_ref[...].astype(F32) + (dot_nn(o_ref[...], out_ref[...]) + vec_ref[4:5, :])
     h_ref[...] = hidden
     unit, _ = normalised(hidden)
     a = (unit * vec_ref[5:6, :] + vec_ref[6:7, :]).astype(BF16)
+    finish(waits[6:7])
     a = dot_nn(a, order_ref[...]).astype(BF16)
-    g = g_ref[...]
     branch = jnp.zeros((ROWS, WIDTH), F32)
     grad_a = jnp.zeros((ROWS, WIDTH), F32)
-    step = 512
-    for i in range(UP // step):
-        cols = pl.ds(i * step, step)
-        up = up_ref[:, cols]
-        down = down_ref[cols, :]
-        u = dot_nn(a, up) + up_b_ref[:, cols]
+    out_waits = []
+    for half in range(2):
+        finish(waits[7:18] if half == 0 else waits[18:])
+        g = g_ref[...]
+        up = up_ref[half]
+        down = down_ref[half]
+        first, second = units[2 * half], units[2 * half + 1]
+        u = dot_nn(a, up) + jnp.concatenate([up_b_ref[:, first], up_b_ref[:, second]], axis=1)
         phi = 0.5 * (1.0 + lax.erf(u * (0.5**0.5)))
         z = (u * phi).astype(BF16)
         slope = phi + u * (jnp.exp(-0.5 * u * u) * (2.0 * jnp.pi) ** (-0.5))
         branch += dot_nn(z, down)
         gu = (dot_nt(g, down) * slope).astype(BF16)
-        grad_down_ref[cols, :] = dot_tn(z, g).astype(BF16)
-        grad_up_ref[:, cols] = dot_tn(a, gu).astype(BF16)
-        grad_up_b_ref[:, cols] = total(gu)
+        grad_down_ref[half] = dot_tn(z, g).astype(BF16)
+        grad_up_ref[half] = dot_tn(a, gu).astype(BF16)
+        copies = []
+        for e in range(2):
+            unit = units[2 * half + e]
+            copies += [(grad_up_ref.at[half, row_block(at, BLOCK), pieces[e]], gup.at[:, unit]) for _, gup, at in ups]
+            copies += [(grad_down_ref.at[half, pieces[e]], downs[2 * half + e][1])]
+        out_waits += bring(copies, out_sems.at[pl.ds(10 * half, 10)])
+        sums = total(gu)
+        grad_up_b_ref[:, first] = sums[:, :DOWN_ROWS]
+        grad_up_b_ref[:, second] = sums[:, DOWN_ROWS:]
         grad_a += dot_nt(gu, up)
-    m_own_ref[...] = branch[:OWN] + hidden[:OWN] + vec_ref[7:8, :]
-    m_far_ref[...] = branch[OWN:]
     high = grad_a.astype(BF16)
     low = (grad_a - high.astype(F32)).astype(BF16)
     grad_a_ref[...] = dot_nt(high, order_ref[...]) + dot_nt(low, order_ref[...])
-    grad_down_b_ref[...] = total(g[:OWN])
-    for gup, at in zip((gup_0, gup_1, gup_2, gup_3), up_at):
-        gup[...] = grad_up_ref[pl.ds(pl.multiple_of(at * BLOCK, 64), BLOCK), :]
-    for gdown, at in zip((gdown_0, gdown_1, gdown_2, gdown_3), down_at):
-        gdown[...] = grad_down_ref[pl.ds(pl.multiple_of(at * DOWN_ROWS, 128), DOWN_ROWS), :]
+    m_own_ref[...] = branch[:OWN] + h_ref[0:OWN, :] + vec_ref[7:8, :]
+    m_far_ref[...] = branch[OWN:]
+    grad_down_b_ref[...] = total(g_ref[0:OWN, :])
+    finish(out_waits)
 
 
 def back_kernel(
@@ -331,8 +369,11 @@
     out_ref[...] = (gh_ref[...] + norm_back(grad, unit, scale, vec_ref[0:1, :])).astype(BF16)
 
 
-def call(kernel, place, args, outs, scratch=(), limit=VMEM_LIMIT):
-    specs = [pl.BlockSpec(memory_space=pltpu.VMEM)] * len(args)
+VMEM, ANY = pltpu.VMEM, pl.ANY
+
+
+def call(kernel, place, args, outs, scratch=(), sems=(), in_any=None, out_any=(), limit=VMEM_LIMIT):
+    specs = [pl.BlockSpec(memory_space=ANY if in_any is not None and i >= in_any else VMEM) for i in range(len(args))]
     if place is not None:
         args = (place,) + tuple(args)
         specs = [pl.BlockSpec(memory_space=pltpu.SMEM)] + specs
@@ -340,8 +381,8 @@
         kernel,
         out_shape=tuple(jax.ShapeDtypeStruct(s, d) for s, d in outs),
         in_specs=specs,
-        out_specs=tuple(pl.BlockSpec(memory_space=pltpu.VMEM) for _ in outs),
-        scratch_shapes=[pltpu.VMEM(s, d) for s, d in scratch],
+        out_specs=tuple(pl.BlockSpec(memory_space=ANY if i in out_any else VMEM) for i in range(len(outs))),
+        scratch_shapes=[VMEM(s, d) for s, d in scratch] + [pltpu.SemaphoreType.DMA((n,)) for n in sems],
         compiler_params=pltpu.CompilerParams(vmem_limit_bytes=limit),
         cost_estimate=pl.CostEstimate(flops=1, bytes_accessed=1, transcendentals=0),
     )(*args)
@@ -481,23 +522,22 @@
         (((8, 6, ATTN + UP), BF16),),
         (((16, 128), F32), ((6, FF), F32), ((6, UP), F32)),
     )
-    downs = ring_gather(after([w_down], parts)[0], "x")
-    rows = lax.all_to_all(parts, EIGHT, 0, 0, tiled=True).reshape(2, 24, ATTN + UP)
+    rows = lax.all_to_all(parts, EIGHT, 0, 0, tiled=True)
+    rows = rows.reshape(2, 24, ATTN + UP)
     attn, ups = rows[:, :, :ATTN], rows[:, :, ATTN:].reshape(48, UP)
-    downs = jnp.concatenate(ring_order(downs, x_at), axis=0)
 
     attn = ring_gather(attn, "z")
     ups = ring_gather(ups, "x")
-    *attn, downs = lax.optimization_barrier((*attn, downs))
-    downs = ring_gather(downs, "z")
+    (downs,) = after([w_down], *attn)
+    downs = lax.all_to_all(jnp.broadcast_to(downs[None], (16, 24, WIDTH)), ("x", "z"), 0, 0, tiled=True)
     item = jnp.concatenate([mine, between_cores(mine)], axis=0)
     x, g = item[:, :WIDTH], item[:, WIDTH:]
     attn = jnp.concatenate(ring_order(attn, z_at), axis=1).reshape(BLOCK, ATTN)
     ups = jnp.concatenate(ring_order(ups, x_at), axis=0)
-    downs = jnp.concatenate(ring_order(downs, z_at), axis=0)
 
     attn = relay_gather(attn, "x")
     ups = relay_gather(ups, "z")
+    (downs,) = after([downs.reshape(DOWN_ROWS, WIDTH)], attn[1])
     downs = relay_gather(downs, "y")
 
     order = up_order()
@@ -520,11 +560,11 @@
     far_o, far_out = between_cores(own_o), between_cores(own_out)
     up_b = small_all[:, 8:12].reshape(4, 2, 4, 2, 2, 24)
     up_b = lax.dynamic_index_in_dim(up_b, core, 3, keepdims=False)
-    up_b = up_b.transpose(1, 3, 2, 0, 4).reshape(1, UP).astype(F32)
+    up_b = up_b.transpose(1, 3, 0, 2, 4).reshape(1, UP).astype(F32)
     hidden, m_own, m_far, grad_a_own, grad_up_b, grad_down_b, *grads = call(
         mlp_kernel,
         place,
-        (x, own_o, far_o, own_out, far_out, vectors, up_b, g, order, *ups, *downs),
+        (vectors, up_b, x, own_o, far_o, own_out, far_out, g, order, *ups, *downs),
         (
             ((ROWS, WIDTH), F32),
             ((OWN, WIDTH), F32),
@@ -535,14 +575,24 @@
         )
         + (((BLOCK, UP), BF16),) * 4
         + (((DOWN_ROWS, WIDTH), BF16),) * 4,
-        (((WIDTH, UP), BF16), ((UP, WIDTH), BF16), ((WIDTH, UP), BF16), ((UP, WIDTH), BF16)),
+        (
+            ((ROWS, WIDTH), BF16),
+            ((WIDTH, WIDTH), BF16),
+            ((ROWS, WIDTH), BF16),
+            ((ROWS, WIDTH), BF16),
+            ((WIDTH, WIDTH), BF16),
+        )
+        + (((2, WIDTH, WIDTH), BF16),) * 4,
+        (28, 20),
+        in_any=2,
+        out_any=range(6, 14),
     )
     grad_a_far = between_cores(grad_a_own)
     grad_a_far, *grads = lax.optimization_barrier((grad_a_far, *grads))
     grad_ups, grad_downs = grads[:4], grads[4:]
     got_ups, got_downs = relay_start(grad_ups, "z"), relay_start(grad_downs, "y")
     block = (m_own + between_cores(m_far)).astype(BF16)
-    up_cols = grad_up_b.reshape(2, 2, 4, 4, 24).transpose(3, 0, 2, 1, 4)[:, :, :, None]
+    up_cols = grad_up_b.reshape(2, 2, 4, 4, 24).transpose(2, 0, 3, 1, 4)[:, :, :, None]
     up_cols = jnp.where((jnp.arange(2) == core)[:, None, None], up_cols, 0.0).reshape(WIDTH, 4)
     up_high = up_cols.astype(BF16).astype(F32)
     up_cols = jnp.pad(up_high, ((0, 0), (8, SMALL - 12))) + jnp.pad(up_cols - up_high, ((0, 0), (24, SMALL - 28)))
@@ -575,10 +625,10 @@
     down_sum = relay_end(grad_downs, got_downs, far_downs).astype(BF16)
     (far_attn,) = after([send(attn_ahead, "x", 1)], up_sum, down_sum)
     up_parts = ring_split(up_sum, x_at)
-    down_parts = ring_split(down_sum.reshape(4, 4, 24, WIDTH), x_at, 1)
+    down_parts = ring_split(down_sum, x_at)
     mlp_sum = ring_reduce(
         [
-            jnp.concatenate([u[:, :WIDTH], u[:, WIDTH:], d.reshape(96, WIDTH)])
+            jnp.concatenate([u[:, :WIDTH], u[:, WIDTH:], d])
             for u, d in zip(up_parts, down_parts)
         ],
         "x",
@@ -607,7 +657,7 @@
         + (((6,), F32),) * 8
         + (((24,), F32),),
         (((128, 128), F32),),
-        8 * 1024 * 1024,
+        limit=8 * 1024 * 1024,
     )
     gain_1, bias_1, bias_q, bias_v, bias_out, gain_2, bias_2, bias_down = vecs
     return (

time: 172 us -> 169 us (0.983)
  waiting for transfers between devices: 45.2 us -> 36.5 us
  starting transfers between devices: 74.8 us -> 80 us
    ppermute x21 -> x15, waiting for transfers between devices: 16 us -> 4.58 us  [ring(): return lax.ppermute(values, axis, [(i, (i + by) % 4) for i in range(4)])]
    all_to_all x1 -> x2, waiting for transfers between devices: 1.64 us -> 12.3 us  [the longest x1 8.59 us: shards(): lax.all_to_all(jnp.broadcast_to(downs[None], (16, 24, WIDTH)), ('x', 'z')...]
    ppermute x18, waiting for transfers between devices: 24 us -> 16.7 us  [send(): return lax.ppermute(values, AXES, along(axis, by))]
    ppermute x21 -> x15, starting transfers between devices: 23 us -> 17.7 us  [ring(): return lax.ppermute(values, axis, [(i, (i + by) % 4) for i in range(4)])]
    all_to_all x1 -> x2, starting transfers between devices: 5.98 us -> 9.93 us  [the longest x1 5.97 us: shards(): rows = lax.all_to_all(parts, EIGHT, 0, 0, tiled=True)]
    ppermute x2, starting transfers between devices: 8.48 us -> 11.8 us  [swap_items(): return lax.ppermute(values, ('c', 'yl'), [(0, 0), (1, 2), (2, 1), (3, 3)])]
    ppermute x18, starting transfers between devices: 21.1 us -> 23.5 us  [send(): return lax.ppermute(values, AXES, along(axis, by))]
  transfers between devices with their start and end apart: 49 -> 44, of which waited for: 23 -> 16; matrix products, arithmetic and copies ran while one was open for 9% -> 10% of each run, Pallas kernels for 10% -> 10%
where the time goes in v2:
time: 169 us; the launch traced here: 168 us
  starting transfers between devices  80 us (47%)
  waiting for transfers between devices  36.5 us (22%)
  Pallas kernels  31.3 us (19%)
  other arithmetic  10.4 us (6%)
  local copies, waits for them, and re-layouts  7.89 us (5%)
  between operations  2 us (1%)
    pallas_call x6, Pallas kernels, call(): pl.pallas_call(kernel, out_shape=tuple((jax.ShapeDtypeStruct(s, d) for s,...  31.3 us
    ppermute x18, starting transfers between devices, send(): return lax.ppermute(values, AXES, along(axis, by))  23.5 us
    ppermute x15, starting transfers between devices, ring(): return lax.ppermute(values, axis, [(i, (i + by) % 4) for i in range(4)])  17.7 us
    ppermute x18, waiting for transfers between devices, send(): return lax.ppermute(values, AXES, along(axis, by))  16.7 us
    ppermute x2, starting transfers between devices, swap_items(): return lax.ppermute(values, ('c', 'yl'), [(0, 0), (1, 2), (2, 1), (3, 3)])  11.8 us
    ppermute x6, starting transfers between devices, between_cores(): return lax.ppermute(values, 'c', [(0, 1), (1, 0)])  9.64 us
    all_to_all x1, waiting for transfers between devices, shards(): lax.all_to_all(jnp.broadcast_to(downs[None], (16, 24, WIDTH)), ('x', 'z')...  8.59 us
    all_to_all x1, starting transfers between devices, shards(): got = lax.all_to_all(sums, EIGHT, 0, 0, tiled=True)  7.37 us
  transfers between devices with their start and end apart: 44, of which 16 were waited for; matrix products, arithmetic and copies ran while one was open for 10% of the time, Pallas kernels for 10%

profile of v2, /device:TPU:1, one launch (start us, length us, event | category | flops | bytes accessed | tf_op | source)
XLA Modules:
  0.0 168.2 jit_solution(8819948107957129925)
XLA Ops:
  0.7 2.0 %shard_map.271 = bf16[8,6,3200]{2,1,0:T(8,128)(2,1)} custom-call(bf16[6,2304]{1,0:T(8,128)(2,1)} %qkv_ref.1, bf16[6,768]{1,0:T(8,128)(2,1)} %out_ref.1, bf16[6,3072]{1,0:T(8,128)(2,1)} %up_ref.1, bf16[6]{0:T(256)(128)(2,1)} %refs_0_.1, bf16[6]{0:T(256)(128)(2,1)} %refs_1_.1, bf16[6]{0:T(256)(128)(2,1)} %refs_2_.1, bf16[6]{0:T(256)(128)(2,1)} %refs_3_.1, ...), custom_call_target="tpu_custom_call" | custom-call | flops 1 | bytes 1 | tf_op jit(solution)/shard_map/pallas_call | solution.py:380
  2.6 6.0 %all-to-all-start = ((bf16[8,6,3200]{2,1,0:T(8,128)(2,1)}), bf16[8,6,3200]{2,1,0:T(8,128)(2,1)S(1)}, u32[]{:S(2)}, u32[]{:S(2)}) async-start(bf16[8,6,3200]{2,1,0:T(8,128)(2,1)} %shard_map.271), calls=%async_computation | async-start | bytes 819200 | tf_op jit(solution)/shard_map/all_to_all | solution.py:525
  9.6 3.5 %collective-permute-start = (bf16[128,1536]{1,0:T(8,128)(2,1)S(1)}, bf16[128,1536]{1,0:T(8,128)(2,1)S(1)}, u32[]{:S(2)}, u32[]{:S(2)}) collective-permute-start(bf16[128,1536]{1,0:T(8,128)(2,1)S(1)} %pad_maximum_fusion.2), channel_id=1, source_target_pairs={{0,0},{1,2},{2,1},{3,3},{4,4},{5,6},{6,5},{7,7},{8,8},{9,10},{10,9... | collective-permute-start | bytes 1179656 | tf_op jit(solution)/shard_map/ppermute | solution.py:400
  13.2 3.7 %all-to-all-done = bf16[8,6,3200]{2,1,0:T(8,128)(2,1)S(1)} async-done(((bf16[8,6,3200]{2,1,0:T(8,128)(2,1)}), bf16[8,6,3200]{2,1,0:T(8,128)(2,1)S(1)}, u32[]{:S(2)}, u32[]{:S(2)}) %all-to-all-start) | async-done | bytes 307232 | tf_op jit(solution)/shard_map/all_to_all | solution.py:525
  17.0 3.8 %collective-permute-start.2 = (bf16[2,24,1664]{2,1,0:T(8,128)(2,1)S(1)}, bf16[2,24,1664]{2,1,0:T(8,128)(2,1)S(1)}, u32[]{:S(2)}, u32[]{:S(2)}) collective-permute-start(bf16[2,24,1664]{2,1,0:T(8,128)(2,1)S(1)} %slice.76), channel_id=1, source_target_pairs={{0,12},{4,0},{8,4},{12,8},{1,13},{5,1},{9,5},{13,9},{2,14},{6,2},{... | collective-permute-start | bytes 479240 | tf_op jit(solution)/shard_map/ppermute | solution.py:411
  21.5 1.5 fusion.order_hbm
  23.7 2.5 %collective-permute-start.10 = (bf16[48,1536]{1,0:T(8,128)(2,1)S(1)}, bf16[48,1536]{1,0:T(8,128)(2,1)S(1)}, u32[]{:S(2)}, u32[]{:S(2)}) collective-permute-start(bf16[48,1536]{1,0:T(8,128)(2,1)S(1)} %bitcast.45), channel_id=1, source_target_pairs={{0,96},{32,0},{64,32},{96,64},{1,97},{33,1},{65,33},{97,65},{2,98}... | collective-permute-start | bytes 442376 | tf_op jit(solution)/shard_map/ppermute | solution.py:411
  26.8 1.2 collective-permute-start.12
  28.1 2.6 %collective-permute-start.1 = (bf16[128,1536]{1,0:T(8,128)(2,1)S(1)}, bf16[128,1536]{1,0:T(8,128)(2,1)}, u32[]{:S(2)}, u32[]{:S(2)}) collective-permute-start(bf16[128,1536]{1,0:T(8,128)(2,1)S(1)} %collective-permute-done), channel_id=1, source_target_pairs={{0,2},{2,0},{1,3},{3,1},{4,6},{6,4},{5,7},{7,5},{8,10},{10,8},{9,1... | collective-permute-start | bytes 1179656 | tf_op jit(solution)/shard_map/ppermute | solution.py:392
  31.3 2.5 %collective-permute-start.5 = (bf16[192,1664]{1,0:T(8,128)(2,1)S(1)}, bf16[192,1664]{1,0:T(8,128)(2,1)S(1)}, u32[]{:S(2)}, u32[]{:S(2)}) collective-permute-start(bf16[192,1664]{1,0:T(8,128)(2,1)S(1)} %bitcast.39), channel_id=1, source_target_pairs={{0,32},{1,33},{2,98},{3,99},{4,36},{5,37},{6,102},{7,103},{8,40},{... | collective-permute-start | bytes 1916936 | tf_op jit(solution)/shard_map/ppermute | solution.py:450
  34.8 4.0 %all-to-all-start.1 = ((bf16[16,24,768]{2,1,0:T(8,128)(2,1)}), bf16[16,24,768]{2,1,0:T(8,128)(2,1)S(1)}, u32[]{:S(2)}, u32[]{:S(2)}) async-start(bf16[16,24,768]{2,1,0:T(8,128)(2,1)} %broadcast_in_dim.54), calls=%async_computation.1 | async-start | bytes 1179648 | tf_op jit(solution)/shard_map/all_to_all | solution.py:532
  38.9 2.6 %collective-permute-start.13 = (bf16[192,1536]{1,0:T(8,128)(2,1)S(1)}, bf16[192,1536]{1,0:T(8,128)(2,1)}, u32[]{:S(2)}, u32[]{:S(2)}) collective-permute-start(bf16[192,1536]{1,0:T(8,128)(2,1)S(1)} %pad_maximum_fusion.1.up_0), channel_id=1, source_target_pairs={{0,4},{1,5},{2,14},{3,15},{4,8},{5,9},{6,2},{7,3},{8,12},{9,13},{1... | collective-permute-start | bytes 1769480 | tf_op jit(solution)/shard_map/ppermute | solution.py:450
  41.6 1.2 collective-permute-start.6
  42.8 8.6 %all-to-all-done.1 = bf16[16,24,768]{2,1,0:T(8,128)(2,1)S(1)} async-done(((bf16[16,24,768]{2,1,0:T(8,128)(2,1)}), bf16[16,24,768]{2,1,0:T(8,128)(2,1)S(1)}, u32[]{:S(2)}, u32[]{:S(2)}) %all-to-all-start.1) | async-done | bytes 589856 | tf_op jit(solution)/shard_map/all_to_all | solution.py:532
  53.5 1.0 constant_dynamic-update-slice_fusion
  55.5 2.0 %collective-permute-start.15 = (bf16[192,1536]{1,0:T(8,128)(2,1)}, bf16[192,1536]{1,0:T(8,128)(2,1)}, u32[]{:S(2)}, u32[]{:S(2)}) collective-permute-start(bf16[192,1536]{1,0:T(8,128)(2,1)} %collective-permute-done.13.up_1), channel_id=1, source_target_pairs={{0,4},{1,5},{2,14},{3,15},{4,8},{5,9},{6,2},{7,3},{8,12},{9,13},{1... | collective-permute-start | bytes 1769480 | tf_op jit(solution)/shard_map/ppermute | solution.py:450
  58.1 2.5 %collective-permute-done.16.down_1 = bf16[384,768]{1,0:T(8,128)(2,1)} collective-permute-done((bf16[384,768]{1,0:T(8,128)(2,1)S(1)}, bf16[384,768]{1,0:T(8,128)(2,1)}, u32[]{:S(2)}, u32[]{:S(2)}) %collective-permute-start.16) | collective-permute-done | bytes 589856 | tf_op jit(solution)/shard_map/ppermute | solution.py:450
  60.6 2.1 %collective-permute-start.18 = (bf16[384,768]{1,0:T(8,128)(2,1)}, bf16[384,768]{1,0:T(8,128)(2,1)}, u32[]{:S(2)}, u32[]{:S(2)}) collective-permute-start(bf16[384,768]{1,0:T(8,128)(2,1)} %collective-permute-done.16.down_1), channel_id=1, source_target_pairs={{0,1},{1,16},{2,19},{3,2},{4,5},{5,20},{6,23},{7,6},{8,9},{9,24},{... | collective-permute-start | bytes 1769480 | tf_op jit(solution)/shard_map/ppermute | solution.py:450
  62.7 5.6 %shard_map.272 = (bf16[256,768]{1,0:T(8,128)(2,1)}, bf16[256,1152]{1,0:T(8,128)(2,1)}, bf16[256,384]{1,0:T(8,128)(2,1)}, f32[256,128]{1,0:T(8,128)}, bf16[768,11...) custom-call(s32[4]{0:T(128)} %pad_add_fusion.1.place_ref, ...), custom_call_target="tpu_custom_call" | custom-call | flops 1 | bytes 1 | tf_op jit(solution)/shard_map/pallas_call | solution.py:380
  68.3 3.3 %collective-permute-start.9 = (bf16[768,384]{1,0:T(8,128)(2,1)}, bf16[768,384]{1,0:T(8,128)(2,1)S(1)}, u32[]{:S(2)}, u32[]{:S(2)}) collective-permute-start(bf16[768,384]{1,0:T(8,128)(2,1)} %get-tuple-element.84.own_out.own_out_ref), channel_id=1, source_target_pairs={{0,2},{2,0},{1,3},{3,1},{4,6},{6,4},{5,7},{7,5},{8,10},{10,8},{9,1... | collective-permute-start | bytes 1769480 | tf_op jit(solution)/shard_map/ppermute | solution.py:392
  71.9 1.0 slice.59
  75.1 10.8 %shard_map.273 = (f32[256,768]{1,0:T(8,128)}, f32[128,768]{1,0:T(8,128)}, f32[128,768]{1,0:T(8,128)}, f32[256,768]{1,0:T(8,128)}, f32[1,1536]{1,0:T(1,128)}, /*i...) custom-call(s32[4]{0:T(128)} %pad_add_fusion.1.place_ref, ...), custom_call_target="tpu_custom_call" | custom-call | flops 1 | bytes 1 | tf_op jit(solution)/shard_map/pallas_call | solution.py:380
  85.8 3.2 %collective-permute-start.20 = (f32[256,768]{1,0:T(8,128)}, f32[256,768]{1,0:T(8,128)S(1)}, u32[]{:S(2)}, u32[]{:S(2)}) collective-permute-start(f32[256,768]{1,0:T(8,128)} %get-tuple-element.90.own_grad_ref), channel_id=1, source_target_pairs={{0,2},{2,0},{1,3},{3,1},{4,6},{6,4},{5,7},{7,5},{8,10},{10,8},{9,1... | collective-permute-start | bytes 2359304 | tf_op jit(solution)/shard_map/ppermute | solution.py:392
  91.6 3.1 %collective-permute-start.22 = (bf16[192,1536]{1,0:T(8,128)(2,1)}, bf16[192,1536]{1,0:T(8,128)(2,1)S(1)}, u32[]{:S(2)}, u32[]{:S(2)}) collective-permute-start(bf16[192,1536]{1,0:T(8,128)(2,1)} %get-tuple-element.109), channel_id=1, source_target_pairs={{0,4},{1,5},{2,14},{3,15},{4,8},{5,9},{6,2},{7,3},{8,12},{9,13},{1... | collective-permute-start | bytes 1769480 | tf_op jit(solution)/shard_map/ppermute | solution.py:450
  94.7 1.0 pad_add_fusion.up_cols_ref
  95.7 9.5 %shard_map.274 = (bf16[192,1664]{1,0:T(8,128)(2,1)}, bf16[192,1664]{1,0:T(8,128)(2,1)}, bf16[192,1664]{1,0:T(8,128)(2,1)}, bf16[192,1664]{1,0:T(8,128)(2,1)}, f3...) custom-call(s32[4]{0:T(128)} %pad_add_fusion.1.place_ref, ...), custom_call_target="tpu_custom_call" | custom-call | flops 1 | bytes 1 | tf_op jit(solution)/shard_map/pallas_call | solution.py:380
  105.4 2.5 %collective-permute-start.24 = (bf16[192,1664]{1,0:T(8,128)(2,1)}, bf16[192,1664]{1,0:T(8,128)(2,1)S(1)}, u32[]{:S(2)}, u32[]{:S(2)}) collective-permute-start(bf16[192,1664]{1,0:T(8,128)(2,1)} %get-tuple-element.115), channel_id=1, source_target_pairs={{0,32},{1,33},{2,98},{3,99},{4,36},{5,37},{6,102},{7,103},{8,40},{... | collective-permute-start | bytes 1916936 | tf_op jit(solution)/shard_map/ppermute | solution.py:450
  108.2 1.0 add_convert_fusion.4
  109.2 2.3 %collective-permute-start.29 = (bf16[384,768]{1,0:T(8,128)(2,1)}, bf16[384,768]{1,0:T(8,128)(2,1)S(1)}, u32[]{:S(2)}, u32[]{:S(2)}) collective-permute-start(bf16[384,768]{1,0:T(8,128)(2,1)} %add_convert_fusion.4), channel_id=1, source_target_pairs={{0,1},{1,16},{2,19},{3,2},{4,5},{5,20},{6,23},{7,6},{8,9},{9,24},{... | collective-permute-start | bytes 1769480 | tf_op jit(solution)/shard_map/ppermute | solution.py:450
  112.4 2.4 %shard_map.275 = bf16[128,768]{1,0:T(8,128)(2,1)} custom-call(s32[4]{0:T(128)} %pad_add_fusion.1.place_ref, bf16[256,768]{1,0:T(8,128)(2,1)} %get-tuple-element.80.x_ref.x_hbm, f32[128,768]{1,0:T(8,128)} %get-tuple-element.106.own_x_ref, f32[128,768]{1,0:T(8,128)} %copy-done.15, f32[128,768]{1,0:T(8,128)} %get-tuple-element.113.gh_ref, ...), custom_call_target="tpu_custom_call" | custom-call | flops 1 | bytes 1 | tf_op jit(solution)/shard_map/pallas_call | solution.py:380
  114.9 1.8 %pad_maximum_fusion.3 = bf16[128,1536]{1,0:T(8,128)(2,1)} fusion(bf16[128,768]{1,0:T(8,128)(2,1)} %shard_map.275, bf16[128,768]{1,0:T(8,128)(2,1)S(1)} %add_convert_fusion.7), kind=kLoop, calls=%fused_computation.12 | loop fusion | flops 786432 | bytes 786432 | tf_op jit(solution)/shard_map/concatenate | solution.py:637
  116.6 4.6 %collective-permute-done.24 = bf16[192,1664]{1,0:T(8,128)(2,1)S(1)} collective-permute-done((bf16[192,1664]{1,0:T(8,128)(2,1)}, bf16[192,1664]{1,0:T(8,128)(2,1)S(1)}, u32[]{:S(2)}, u32[]{:S(2)}) %collective-permute-start.24) | collective-permute-done | bytes 639008 | tf_op jit(solution)/shard_map/ppermute | solution.py:450
  121.3 1.4 collective-permute-start.27
  122.7 1.5 collective-permute-done.25
  124.6 1.3 add_convert_fusion.2
  126.0 5.8 %collective-permute-done.27 = bf16[192,1536]{1,0:T(8,128)(2,1)S(1)} collective-permute-done((bf16[192,1536]{1,0:T(8,128)(2,1)}, bf16[192,1536]{1,0:T(8,128)(2,1)S(1)}, u32[]{:S(2)}, u32[]{:S(2)}) %collective-permute-start.27) | collective-permute-done | bytes 589856 | tf_op jit(solution)/shard_map/ppermute | solution.py:450
  132.1 1.8 %collective-permute-done.26 = bf16[192,1664]{1,0:T(8,128)(2,1)S(1)} collective-permute-done((bf16[192,1664]{1,0:T(8,128)(2,1)S(1)}, bf16[192,1664]{1,0:T(8,128)(2,1)S(1)}, u32[]{:S(2)}, u32[]{:S(2)}) %collective-permute-start.26) | collective-permute-done | bytes 639008 | tf_op jit(solution)/shard_map/ppermute | solution.py:450
  134.3 2.0 %collective-permute-start.33 = (bf16[2,24,1664]{2,1,0:T(8,128)(2,1)S(1)}, bf16[2,24,1664]{2,1,0:T(8,128)(2,1)S(1)}, u32[]{:S(2)}, u32[]{:S(2)}) collective-permute-start(bf16[2,24,1664]{2,1,0:T(8,128)(2,1)S(1)} %get-tuple-element.153), channel_id=1, source_target_pairs={{0,8},{4,12},{8,0},{12,4},{1,9},{5,13},{9,1},{13,5},{2,10},{6,14},... | collective-permute-start | bytes 479240 | tf_op jit(solution)/shard_map/ppermute | solution.py:411
  136.3 1.1 collective-permute-start.34
  137.5 1.7 collective-permute-start.36
  139.1 2.5 %collective-permute-done.32 = bf16[2,24,1664]{2,1,0:T(8,128)(2,1)S(1)} collective-permute-done((bf16[2,24,1664]{2,1,0:T(8,128)(2,1)S(1)}, bf16[2,24,1664]{2,1,0:T(8,128)(2,1)S(1)}, u32[]{:S(2)}, u32[]{:S(2)}) %collective-permute-start.32) | collective-permute-done | bytes 159776 | tf_op jit(solution)/shard_map/ppermute | solution.py:411
  141.7 8.2 %collective-permute-start.31 = (bf16[128,1536]{1,0:T(8,128)(2,1)}, bf16[128,1536]{1,0:T(8,128)(2,1)S(1)}, u32[]{:S(2)}, u32[]{:S(2)}) collective-permute-start(bf16[128,1536]{1,0:T(8,128)(2,1)} %pad_maximum_fusion.3), channel_id=1, source_target_pairs={{0,0},{1,2},{2,1},{3,3},{4,4},{5,6},{6,5},{7,7},{8,8},{9,10},{10,9... | collective-permute-start | bytes 1179656 | tf_op jit(solution)/shard_map/ppermute | solution.py:400
  151.4 7.4 %all-to-all-start.2 = ((bf16[8,6,3200]{2,1,0:T(8,128)(2,1)}), bf16[8,6,3200]{2,1,0:T(8,128)(2,1)S(1)}, u32[]{:S(2)}, u32[]{:S(2)}) async-start(bf16[8,6,3200]{2,1,0:T(8,128)(2,1)} %reshape.106), calls=%async_computation.2 | async-start | bytes 819200 | tf_op jit(solution)/shard_map/all_to_all | solution.py:643
  158.8 1.5 collective-permute-start.38
  160.8 2.0 %collective-permute-start.40 = (bf16[24,768]{1,0:T(8,128)(2,1)S(1)}, bf16[24,768]{1,0:T(8,128)(2,1)S(1)}, u32[]{:S(2)}, u32[]{:S(2)}) collective-permute-start(bf16[24,768]{1,0:T(8,128)(2,1)S(1)} %get-tuple-element.176), channel_id=1, source_target_pairs={{0,12},{4,0},{8,4},{12,8},{1,13},{5,1},{9,5},{13,9},{2,14},{6,2},{... | collective-permute-start | bytes 110600 | tf_op jit(solution)/shard_map/ppermute | solution.py:411
  163.5 1.3 collective-permute-done.39
  164.8 2.2 %all-to-all-done.2.got_ref = bf16[8,6,3200]{2,1,0:T(8,128)(2,1)S(1)} async-done(((bf16[8,6,3200]{2,1,0:T(8,128)(2,1)}), bf16[8,6,3200]{2,1,0:T(8,128)(2,1)S(1)}, u32[]{:S(2)}, u32[]{:S(2)}) %all-to-all-start.2) | async-done | bytes 307232 | tf_op jit(solution)/shard_map/all_to_all | solution.py:643
  167.0 1.0 shard_map.276
  (141 shorter events, 18.1 us)
Async XLA Ops:
  2.6 14.2 %all-to-all-start = ((bf16[8,6,3200]{2,1,0:T(8,128)(2,1)}), bf16[8,6,3200]{2,1,0:T(8,128)(2,1)S(1)}, u32[]{:S(2)}, u32[]{:S(2)}) async-start(bf16[8,6,3200]{2,1,0:T(8,128)(2,1)} %shard_map.271), calls=%async_computation | async-start | bytes 819200 | tf_op jit(solution)/shard_map/all_to_all | solution.py:525
  9.6 16.7 %collective-permute-start = (bf16[128,1536]{1,0:T(8,128)(2,1)S(1)}, bf16[128,1536]{1,0:T(8,128)(2,1)S(1)}, u32[]{:S(2)}, u32[]{:S(2)}) collective-permute-start(bf16[128,1536]{1,0:T(8,128)(2,1)S(1)} %pad_maximum_fusion.2), channel_id=1, source_target_pairs={{0,0},{1,2},{2,1},{3,3},{4,4},{5,6},{6,5},{7,7},{8,8},{9,10},{10,9... | collective-permute-start | bytes 1179656 | tf_op jit(solution)/shard_map/ppermute | solution.py:400
  17.0 9.8 %collective-permute-start.2 = (bf16[2,24,1664]{2,1,0:T(8,128)(2,1)S(1)}, bf16[2,24,1664]{2,1,0:T(8,128)(2,1)S(1)}, u32[]{:S(2)}, u32[]{:S(2)}) collective-permute-start(bf16[2,24,1664]{2,1,0:T(8,128)(2,1)S(1)} %slice.76), channel_id=1, source_target_pairs={{0,12},{4,0},{8,4},{12,8},{1,13},{5,1},{9,5},{13,9},{2,14},{6,2},{... | collective-permute-start | bytes 479240 | tf_op jit(solution)/shard_map/ppermute | solution.py:411
  20.8 7.2 %collective-permute-start.3 = (bf16[2,24,1664]{2,1,0:T(8,128)(2,1)S(1)}, bf16[2,24,1664]{2,1,0:T(8,128)(2,1)S(1)}, u32[]{:S(2)}, u32[]{:S(2)}) collective-permute-start(bf16[2,24,1664]{2,1,0:T(8,128)(2,1)S(1)} %slice.76), channel_id=1, source_target_pairs={{0,8},{4,12},{8,0},{12,4},{1,9},{5,13},{9,1},{13,5},{2,10},{6,14},... | collective-permute-start | bytes 479240 | tf_op jit(solution)/shard_map/ppermute | solution.py:411
  20.8 10.3 %collective-permute-start.4 = (bf16[2,24,1664]{2,1,0:T(8,128)(2,1)S(1)}, bf16[2,24,1664]{2,1,0:T(8,128)(2,1)S(1)}, u32[]{:S(2)}, u32[]{:S(2)}) collective-permute-start(bf16[2,24,1664]{2,1,0:T(8,128)(2,1)S(1)} %slice.76), channel_id=1, source_target_pairs={{0,4},{4,8},{8,12},{12,0},{1,5},{5,9},{9,13},{13,1},{2,6},{6,10},{... | collective-permute-start | bytes 479240 | tf_op jit(solution)/shard_map/ppermute | solution.py:411
  23.7 15.1 %collective-permute-start.10 = (bf16[48,1536]{1,0:T(8,128)(2,1)S(1)}, bf16[48,1536]{1,0:T(8,128)(2,1)S(1)}, u32[]{:S(2)}, u32[]{:S(2)}) collective-permute-start(bf16[48,1536]{1,0:T(8,128)(2,1)S(1)} %bitcast.45), channel_id=1, source_target_pairs={{0,96},{32,0},{64,32},{96,64},{1,97},{33,1},{65,33},{97,65},{2,98}... | collective-permute-start | bytes 442376 | tf_op jit(solution)/shard_map/ppermute | solution.py:411
  26.2 12.5 %collective-permute-start.11 = (bf16[48,1536]{1,0:T(8,128)(2,1)S(1)}, bf16[48,1536]{1,0:T(8,128)(2,1)S(1)}, u32[]{:S(2)}, u32[]{:S(2)}) collective-permute-start(bf16[48,1536]{1,0:T(8,128)(2,1)S(1)} %bitcast.46), channel_id=1, source_target_pairs={{0,64},{32,96},{64,0},{96,32},{1,65},{33,97},{65,1},{97,33},{2,66}... | collective-permute-start | bytes 442376 | tf_op jit(solution)/shard_map/ppermute | solution.py:411
  26.8 11.9 %collective-permute-start.12 = (bf16[48,1536]{1,0:T(8,128)(2,1)S(1)}, bf16[48,1536]{1,0:T(8,128)(2,1)S(1)}, u32[]{:S(2)}, u32[]{:S(2)}) collective-permute-start(bf16[48,1536]{1,0:T(8,128)(2,1)S(1)} %bitcast.47), channel_id=1, source_target_pairs={{0,32},{32,64},{64,96},{96,0},{1,33},{33,65},{65,97},{97,1},{2,34}... | collective-permute-start | bytes 442376 | tf_op jit(solution)/shard_map/ppermute | solution.py:411
  28.1 24.5 %collective-permute-start.1 = (bf16[128,1536]{1,0:T(8,128)(2,1)S(1)}, bf16[128,1536]{1,0:T(8,128)(2,1)}, u32[]{:S(2)}, u32[]{:S(2)}) collective-permute-start(bf16[128,1536]{1,0:T(8,128)(2,1)S(1)} %collective-permute-done), channel_id=1, source_target_pairs={{0,2},{2,0},{1,3},{3,1},{4,6},{6,4},{5,7},{7,5},{8,10},{10,8},{9,1... | collective-permute-start | bytes 1179656 | tf_op jit(solution)/shard_map/ppermute | solution.py:392
  31.3 10.3 %copy-start = (bf16[2,96,1664]{2,1,0:T(8,128)(2,1)}, bf16[2,96,1664]{2,1,0:T(8,128)(2,1)S(1)}, u32[]{:S(2)}) copy-start(bf16[2,96,1664]{2,1,0:T(8,128)(2,1)S(1)} %pad_maximum_fusion) | copy-start | bytes 1916932
  31.3 20.0 %collective-permute-start.5 = (bf16[192,1664]{1,0:T(8,128)(2,1)S(1)}, bf16[192,1664]{1,0:T(8,128)(2,1)S(1)}, u32[]{:S(2)}, u32[]{:S(2)}) collective-permute-start(bf16[192,1664]{1,0:T(8,128)(2,1)S(1)} %bitcast.39), channel_id=1, source_target_pairs={{0,32},{1,33},{2,98},{3,99},{4,36},{5,37},{6,102},{7,103},{8,40},{... | collective-permute-start | bytes 1916936 | tf_op jit(solution)/shard_map/ppermute | solution.py:450
  34.8 16.6 %all-to-all-start.1 = ((bf16[16,24,768]{2,1,0:T(8,128)(2,1)}), bf16[16,24,768]{2,1,0:T(8,128)(2,1)S(1)}, u32[]{:S(2)}, u32[]{:S(2)}) async-start(bf16[16,24,768]{2,1,0:T(8,128)(2,1)} %broadcast_in_dim.54), calls=%async_computation.1 | async-start | bytes 1179648 | tf_op jit(solution)/shard_map/all_to_all | solution.py:532
  38.9 16.5 %copy-start.3 = (bf16[192,1536]{1,0:T(8,128)(2,1)}, bf16[192,1536]{1,0:T(8,128)(2,1)S(1)}, u32[]{:S(2)}) copy-start(bf16[192,1536]{1,0:T(8,128)(2,1)S(1)} %pad_maximum_fusion.1.up_0) | copy-start | bytes 1769476
  38.9 16.5 %collective-permute-start.13 = (bf16[192,1536]{1,0:T(8,128)(2,1)S(1)}, bf16[192,1536]{1,0:T(8,128)(2,1)}, u32[]{:S(2)}, u32[]{:S(2)}) collective-permute-start(bf16[192,1536]{1,0:T(8,128)(2,1)S(1)} %pad_maximum_fusion.1.up_0), channel_id=1, source_target_pairs={{0,4},{1,5},{2,14},{3,15},{4,8},{5,9},{6,2},{7,3},{8,12},{9,13},{1... | collective-permute-start | bytes 1769480 | tf_op jit(solution)/shard_map/ppermute | solution.py:450
  41.6 15.9 %collective-permute-start.6 = (bf16[192,1664]{1,0:T(8,128)(2,1)S(1)}, bf16[192,1664]{1,0:T(8,128)(2,1)S(1)}, u32[]{:S(2)}, u32[]{:S(2)}) collective-permute-start(bf16[192,1664]{1,0:T(8,128)(2,1)S(1)} %bitcast.40), channel_id=1, source_target_pairs={{0,96},{1,97},{2,34},{3,35},{4,100},{5,101},{6,38},{7,39},{8,104},... | collective-permute-start | bytes 1916936 | tf_op jit(solution)/shard_map/ppermute | solution.py:450
  51.4 9.2 %collective-permute-start.16 = (bf16[384,768]{1,0:T(8,128)(2,1)S(1)}, bf16[384,768]{1,0:T(8,128)(2,1)}, u32[]{:S(2)}, u32[]{:S(2)}) collective-permute-start(bf16[384,768]{1,0:T(8,128)(2,1)S(1)} %bitcast.42), channel_id=1, source_target_pairs={{0,1},{1,16},{2,19},{3,2},{4,5},{5,20},{6,23},{7,6},{8,9},{9,24},{... | collective-permute-start | bytes 1769480 | tf_op jit(solution)/shard_map/ppermute | solution.py:450
  52.3 10.3 %collective-permute-start.7 = (bf16[192,1664]{1,0:T(8,128)(2,1)S(1)}, bf16[192,1664]{1,0:T(8,128)(2,1)}, u32[]{:S(2)}, u32[]{:S(2)}) collective-permute-start(bf16[192,1664]{1,0:T(8,128)(2,1)S(1)} %collective-permute-done.5.part_1), channel_id=1, source_target_pairs={{0,32},{1,33},{2,98},{3,99},{4,36},{5,37},{6,102},{7,103},{8,40},{... | collective-permute-start | bytes 1916936 | tf_op jit(solution)/shard_map/ppermute | solution.py:450
  52.5 19.1 %collective-permute-start.14 = (bf16[192,1536]{1,0:T(8,128)(2,1)S(1)}, bf16[192,1536]{1,0:T(8,128)(2,1)}, u32[]{:S(2)}, u32[]{:S(2)}) collective-permute-start(bf16[192,1536]{1,0:T(8,128)(2,1)S(1)} %pad_maximum_fusion.1.up_0), channel_id=1, source_target_pairs={{0,12},{1,13},{2,6},{3,7},{4,0},{5,1},{6,10},{7,11},{8,4},{9,5},{1... | collective-permute-start | bytes 1769480 | tf_op jit(solution)/shard_map/ppermute | solution.py:450
  55.5 18.4 %collective-permute-start.15 = (bf16[192,1536]{1,0:T(8,128)(2,1)}, bf16[192,1536]{1,0:T(8,128)(2,1)}, u32[]{:S(2)}, u32[]{:S(2)}) collective-permute-start(bf16[192,1536]{1,0:T(8,128)(2,1)} %collective-permute-done.13.up_1), channel_id=1, source_target_pairs={{0,4},{1,5},{2,14},{3,15},{4,8},{5,9},{6,2},{7,3},{8,12},{9,13},{1... | collective-permute-start | bytes 1769480 | tf_op jit(solution)/shard_map/ppermute | solution.py:450
  57.5 16.4 %collective-permute-start.17 = (bf16[384,768]{1,0:T(8,128)(2,1)S(1)}, bf16[384,768]{1,0:T(8,128)(2,1)}, u32[]{:S(2)}, u32[]{:S(2)}) collective-permute-start(bf16[384,768]{1,0:T(8,128)(2,1)S(1)} %bitcast.43), channel_id=1, source_target_pairs={{0,17},{1,0},{2,3},{3,18},{4,21},{5,4},{6,7},{7,22},{8,25},{9,8},{... | collective-permute-start | bytes 1769480 | tf_op jit(solution)/shard_map/ppermute | solution.py:450
  60.6 13.7 %collective-permute-start.18 = (bf16[384,768]{1,0:T(8,128)(2,1)}, bf16[384,768]{1,0:T(8,128)(2,1)}, u32[]{:S(2)}, u32[]{:S(2)}) collective-permute-start(bf16[384,768]{1,0:T(8,128)(2,1)} %collective-permute-done.16.down_1), channel_id=1, source_target_pairs={{0,1},{1,16},{2,19},{3,2},{4,5},{5,20},{6,23},{7,6},{8,9},{9,24},{... | collective-permute-start | bytes 1769480 | tf_op jit(solution)/shard_map/ppermute | solution.py:450
  68.3 5.9 %collective-permute-start.9 = (bf16[768,384]{1,0:T(8,128)(2,1)}, bf16[768,384]{1,0:T(8,128)(2,1)S(1)}, u32[]{:S(2)}, u32[]{:S(2)}) collective-permute-start(bf16[768,384]{1,0:T(8,128)(2,1)} %get-tuple-element.84.own_out.own_out_ref), channel_id=1, source_target_pairs={{0,2},{2,0},{1,3},{3,1},{4,6},{6,4},{5,7},{7,5},{8,10},{10,8},{9,1... | collective-permute-start | bytes 1769480 | tf_op jit(solution)/shard_map/ppermute | solution.py:392
  71.6 2.2 %collective-permute-start.8 = (bf16[256,384]{1,0:T(8,128)(2,1)}, bf16[256,384]{1,0:T(8,128)(2,1)S(1)}, u32[]{:S(2)}, u32[]{:S(2)}) collective-permute-start(bf16[256,384]{1,0:T(8,128)(2,1)} %get-tuple-element.83.own_o.own_o_ref), channel_id=1, source_target_pairs={{0,2},{2,0},{1,3},{3,1},{4,6},{6,4},{5,7},{7,5},{8,10},{10,8},{9,1... | collective-permute-start | bytes 589832 | tf_op jit(solution)/shard_map/ppermute | solution.py:392
  85.8 5.3 %collective-permute-start.20 = (f32[256,768]{1,0:T(8,128)}, f32[256,768]{1,0:T(8,128)S(1)}, u32[]{:S(2)}, u32[]{:S(2)}) collective-permute-start(f32[256,768]{1,0:T(8,128)} %get-tuple-element.90.own_grad_ref), channel_id=1, source_target_pairs={{0,2},{2,0},{1,3},{3,1},{4,6},{6,4},{5,7},{7,5},{8,10},{10,8},{9,1... | collective-permute-start | bytes 2359304 | tf_op jit(solution)/shard_map/ppermute | solution.py:392
  89.0 6.6 %collective-permute-start.19 = (f32[128,768]{1,0:T(8,128)}, f32[128,768]{1,0:T(8,128)S(1)}, u32[]{:S(2)}, u32[]{:S(2)}) collective-permute-start(f32[128,768]{1,0:T(8,128)} %get-tuple-element.88), channel_id=1, source_target_pairs={{0,2},{2,0},{1,3},{3,1},{4,6},{6,4},{5,7},{7,5},{8,10},{10,8},{9,1... | collective-permute-start | bytes 1179656 | tf_op jit(solution)/shard_map/ppermute | solution.py:392
  91.2 16.7 %collective-permute-start.23 = (bf16[384,768]{1,0:T(8,128)(2,1)}, bf16[384,768]{1,0:T(8,128)(2,1)S(1)}, u32[]{:S(2)}, u32[]{:S(2)}) collective-permute-start(bf16[384,768]{1,0:T(8,128)(2,1)} %get-tuple-element.111), channel_id=1, source_target_pairs={{0,1},{1,16},{2,19},{3,2},{4,5},{5,20},{6,23},{7,6},{8,9},{9,24},{... | collective-permute-start | bytes 1769480 | tf_op jit(solution)/shard_map/ppermute | solution.py:450
  91.6 17.6 %collective-permute-start.22 = (bf16[192,1536]{1,0:T(8,128)(2,1)}, bf16[192,1536]{1,0:T(8,128)(2,1)S(1)}, u32[]{:S(2)}, u32[]{:S(2)}) collective-permute-start(bf16[192,1536]{1,0:T(8,128)(2,1)} %get-tuple-element.109), channel_id=1, source_target_pairs={{0,4},{1,5},{2,14},{3,15},{4,8},{5,9},{6,2},{7,3},{8,12},{9,13},{1... | collective-permute-start | bytes 1769480 | tf_op jit(solution)/shard_map/ppermute | solution.py:450
  95.7 12.5 %copy-start.11 = (bf16[384,768]{1,0:T(8,128)(2,1)S(1)}, bf16[384,768]{1,0:T(8,128)(2,1)}, u32[]{:S(2)}) copy-start(bf16[384,768]{1,0:T(8,128)(2,1)} %get-tuple-element.110) | copy-start | bytes 1769476
  105.3 6.4 %collective-permute-start.21 = (f32[128,768]{1,0:T(8,128)}, f32[128,768]{1,0:T(8,128)S(1)}, u32[]{:S(2)}, u32[]{:S(2)}) collective-permute-start(f32[128,768]{1,0:T(8,128)} %get-tuple-element.107), channel_id=1, source_target_pairs={{0,2},{2,0},{1,3},{3,1},{4,6},{6,4},{5,7},{7,5},{8,10},{10,8},{9,1... | collective-permute-start | bytes 1179656 | tf_op jit(solution)/shard_map/ppermute | solution.py:392
  105.4 15.9 %collective-permute-start.24 = (bf16[192,1664]{1,0:T(8,128)(2,1)}, bf16[192,1664]{1,0:T(8,128)(2,1)S(1)}, u32[]{:S(2)}, u32[]{:S(2)}) collective-permute-start(bf16[192,1664]{1,0:T(8,128)(2,1)} %get-tuple-element.115), channel_id=1, source_target_pairs={{0,32},{1,33},{2,98},{3,99},{4,36},{5,37},{6,102},{7,103},{8,40},{... | collective-permute-start | bytes 1916936 | tf_op jit(solution)/shard_map/ppermute | solution.py:450
  107.9 16.3 %collective-permute-start.25 = (bf16[192,1664]{1,0:T(8,128)(2,1)}, bf16[192,1664]{1,0:T(8,128)(2,1)S(1)}, u32[]{:S(2)}, u32[]{:S(2)}) collective-permute-start(bf16[192,1664]{1,0:T(8,128)(2,1)} %get-tuple-element.116), channel_id=1, source_target_pairs={{0,96},{1,97},{2,34},{3,35},{4,100},{5,101},{6,38},{7,39},{8,104},... | collective-permute-start | bytes 1916936 | tf_op jit(solution)/shard_map/ppermute | solution.py:450
  107.9 16.7 %collective-permute-start.30 = (bf16[384,768]{1,0:T(8,128)(2,1)}, bf16[384,768]{1,0:T(8,128)(2,1)}, u32[]{:S(2)}, u32[]{:S(2)}) collective-permute-start(bf16[384,768]{1,0:T(8,128)(2,1)} %get-tuple-element.124), channel_id=1, source_target_pairs={{0,17},{1,0},{2,3},{3,18},{4,21},{5,4},{6,7},{7,22},{8,25},{9,8},{... | collective-permute-start | bytes 1769480 | tf_op jit(solution)/shard_map/ppermute | solution.py:450
  109.2 15.4 %collective-permute-start.29 = (bf16[384,768]{1,0:T(8,128)(2,1)}, bf16[384,768]{1,0:T(8,128)(2,1)S(1)}, u32[]{:S(2)}, u32[]{:S(2)}) collective-permute-start(bf16[384,768]{1,0:T(8,128)(2,1)} %add_convert_fusion.4), channel_id=1, source_target_pairs={{0,1},{1,16},{2,19},{3,2},{4,5},{5,20},{6,23},{7,6},{8,9},{9,24},{... | collective-permute-start | bytes 1769480 | tf_op jit(solution)/shard_map/ppermute | solution.py:450
  111.7 12.9 %collective-permute-start.28 = (bf16[192,1536]{1,0:T(8,128)(2,1)S(1)}, bf16[192,1536]{1,0:T(8,128)(2,1)S(1)}, u32[]{:S(2)}, u32[]{:S(2)}) collective-permute-start(bf16[192,1536]{1,0:T(8,128)(2,1)S(1)} %add_convert_fusion.5), channel_id=1, source_target_pairs={{0,4},{1,5},{2,14},{3,15},{4,8},{5,9},{6,2},{7,3},{8,12},{9,13},{1... | collective-permute-start | bytes 1769480 | tf_op jit(solution)/shard_map/ppermute | solution.py:450
  112.4 11.7 %copy-start.9 = (bf16[192,1664]{1,0:T(8,128)(2,1)S(1)}, bf16[192,1664]{1,0:T(8,128)(2,1)}, u32[]{:S(2)}) copy-start(bf16[192,1664]{1,0:T(8,128)(2,1)} %get-tuple-element.118) | copy-start | bytes 1916932
  121.3 10.4 %collective-permute-start.27 = (bf16[192,1536]{1,0:T(8,128)(2,1)}, bf16[192,1536]{1,0:T(8,128)(2,1)S(1)}, u32[]{:S(2)}, u32[]{:S(2)}) collective-permute-start(bf16[192,1536]{1,0:T(8,128)(2,1)} %get-tuple-element.121), channel_id=1, source_target_pairs={{0,12},{1,13},{2,6},{3,7},{4,0},{5,1},{6,10},{7,11},{8,4},{9,5},{1... | collective-permute-start | bytes 1769480 | tf_op jit(solution)/shard_map/ppermute | solution.py:450
  124.3 9.6 %collective-permute-start.26 = (bf16[192,1664]{1,0:T(8,128)(2,1)S(1)}, bf16[192,1664]{1,0:T(8,128)(2,1)S(1)}, u32[]{:S(2)}, u32[]{:S(2)}) collective-permute-start(bf16[192,1664]{1,0:T(8,128)(2,1)S(1)} %add_convert_fusion.1), channel_id=1, source_target_pairs={{0,32},{1,33},{2,98},{3,99},{4,36},{5,37},{6,102},{7,103},{8,40},{... | collective-permute-start | bytes 1916936 | tf_op jit(solution)/shard_map/ppermute | solution.py:450
  132.1 18.0 %collective-permute-start.35 = (bf16[192,768]{1,0:T(8,128)(2,1)S(1)}, bf16[192,768]{1,0:T(8,128)(2,1)S(1)}, u32[]{:S(2)}, u32[]{:S(2)}) collective-permute-start(bf16[192,768]{1,0:T(8,128)(2,1)S(1)} %pad_maximum_fusion.5), channel_id=1, source_target_pairs={{0,32},{32,64},{64,96},{96,0},{1,33},{33,65},{65,97},{97,1},{2,34}... | collective-permute-start | bytes 884744 | tf_op jit(solution)/shard_map/ppermute | solution.py:411
  134.3 7.4 %collective-permute-start.32 = (bf16[2,24,1664]{2,1,0:T(8,128)(2,1)S(1)}, bf16[2,24,1664]{2,1,0:T(8,128)(2,1)S(1)}, u32[]{:S(2)}, u32[]{:S(2)}) collective-permute-start(bf16[2,24,1664]{2,1,0:T(8,128)(2,1)S(1)} %get-tuple-element.151), channel_id=1, source_target_pairs={{0,4},{4,8},{8,12},{12,0},{1,5},{5,9},{9,13},{13,1},{2,6},{6,10},{... | collective-permute-start | bytes 479240 | tf_op jit(solution)/shard_map/ppermute | solution.py:411
  134.3 7.3 %collective-permute-start.33 = (bf16[2,24,1664]{2,1,0:T(8,128)(2,1)S(1)}, bf16[2,24,1664]{2,1,0:T(8,128)(2,1)S(1)}, u32[]{:S(2)}, u32[]{:S(2)}) collective-permute-start(bf16[2,24,1664]{2,1,0:T(8,128)(2,1)S(1)} %get-tuple-element.153), channel_id=1, source_target_pairs={{0,8},{4,12},{8,0},{12,4},{1,9},{5,13},{9,1},{13,5},{2,10},{6,14},... | collective-permute-start | bytes 479240 | tf_op jit(solution)/shard_map/ppermute | solution.py:411
  136.3 13.6 %collective-permute-start.34 = (bf16[2,24,1664]{2,1,0:T(8,128)(2,1)S(1)}, bf16[2,24,1664]{2,1,0:T(8,128)(2,1)S(1)}, u32[]{:S(2)}, u32[]{:S(2)}) collective-permute-start(bf16[2,24,1664]{2,1,0:T(8,128)(2,1)S(1)} %get-tuple-element.152), channel_id=1, source_target_pairs={{0,12},{4,0},{8,4},{12,8},{1,13},{5,1},{9,5},{13,9},{2,14},{6,2},{... | collective-permute-start | bytes 479240 | tf_op jit(solution)/shard_map/ppermute | solution.py:411
  137.5 12.6 %collective-permute-start.36 = (bf16[192,768]{1,0:T(8,128)(2,1)S(1)}, bf16[192,768]{1,0:T(8,128)(2,1)S(1)}, u32[]{:S(2)}, u32[]{:S(2)}) collective-permute-start(bf16[192,768]{1,0:T(8,128)(2,1)S(1)} %pad_maximum_fusion.6), channel_id=1, source_target_pairs={{0,64},{32,96},{64,0},{96,32},{1,65},{33,97},{65,1},{97,33},{2,66}... | collective-permute-start | bytes 884744 | tf_op jit(solution)/shard_map/ppermute | solution.py:411
  141.7 8.6 %collective-permute-start.37 = (bf16[192,768]{1,0:T(8,128)(2,1)S(1)}, bf16[192,768]{1,0:T(8,128)(2,1)S(1)}, u32[]{:S(2)}, u32[]{:S(2)}) collective-permute-start(bf16[192,768]{1,0:T(8,128)(2,1)S(1)} %pad_maximum_fusion.7), channel_id=1, source_target_pairs={{0,96},{32,0},{64,32},{96,64},{1,97},{33,1},{65,33},{97,65},{2,98}... | collective-permute-start | bytes 884744 | tf_op jit(solution)/shard_map/ppermute | solution.py:411
  141.7 21.1 %collective-permute-start.31 = (bf16[128,1536]{1,0:T(8,128)(2,1)}, bf16[128,1536]{1,0:T(8,128)(2,1)S(1)}, u32[]{:S(2)}, u32[]{:S(2)}) collective-permute-start(bf16[128,1536]{1,0:T(8,128)(2,1)} %pad_maximum_fusion.3), channel_id=1, source_target_pairs={{0,0},{1,2},{2,1},{3,3},{4,4},{5,6},{6,5},{7,7},{8,8},{9,10},{10,9... | collective-permute-start | bytes 1179656 | tf_op jit(solution)/shard_map/ppermute | solution.py:400
  151.4 15.6 %all-to-all-start.2 = ((bf16[8,6,3200]{2,1,0:T(8,128)(2,1)}), bf16[8,6,3200]{2,1,0:T(8,128)(2,1)S(1)}, u32[]{:S(2)}, u32[]{:S(2)}) async-start(bf16[8,6,3200]{2,1,0:T(8,128)(2,1)} %reshape.106), calls=%async_computation.2 | async-start | bytes 819200 | tf_op jit(solution)/shard_map/all_to_all | solution.py:643
  158.8 4.8 %collective-permute-start.38 = (bf16[24,768]{1,0:T(8,128)(2,1)S(1)}, bf16[24,768]{1,0:T(8,128)(2,1)S(1)}, u32[]{:S(2)}, u32[]{:S(2)}) collective-permute-start(bf16[24,768]{1,0:T(8,128)(2,1)S(1)} %get-tuple-element.178), channel_id=1, source_target_pairs={{0,4},{4,8},{8,12},{12,0},{1,5},{5,9},{9,13},{13,1},{2,6},{6,10},{... | collective-permute-start | bytes 110600 | tf_op jit(solution)/shard_map/ppermute | solution.py:411
  160.2 4.6 %collective-permute-start.39 = (bf16[24,768]{1,0:T(8,128)(2,1)S(1)}, bf16[24,768]{1,0:T(8,128)(2,1)S(1)}, u32[]{:S(2)}, u32[]{:S(2)}) collective-permute-start(bf16[24,768]{1,0:T(8,128)(2,1)S(1)} %get-tuple-element.177), channel_id=1, source_target_pairs={{0,8},{4,12},{8,0},{12,4},{1,9},{5,13},{9,1},{13,5},{2,10},{6,14},... | collective-permute-start | bytes 110600 | tf_op jit(solution)/shard_map/ppermute | solution.py:411
  160.8 4.0 %collective-permute-start.40 = (bf16[24,768]{1,0:T(8,128)(2,1)S(1)}, bf16[24,768]{1,0:T(8,128)(2,1)S(1)}, u32[]{:S(2)}, u32[]{:S(2)}) collective-permute-start(bf16[24,768]{1,0:T(8,128)(2,1)S(1)} %get-tuple-element.176), channel_id=1, source_target_pairs={{0,12},{4,0},{8,4},{12,8},{1,13},{5,1},{9,5},{13,9},{2,14},{6,2},{... | collective-permute-start | bytes 110600 | tf_op jit(solution)/shard_map/ppermute | solution.py:411
  (15 other events, 78.4 us)

commit v3 on v2

--- a/solution.py
+++ b/solution.py
@@ -587,16 +587,16 @@
         in_any=2,
         out_any=range(6, 14),
     )
-    grad_a_far = between_cores(grad_a_own)
+    up_cols = grad_up_b.reshape(2, 2, 4, 4, 24).transpose(2, 0, 3, 1, 4)[:, :, :, None]
+    up_cols = jnp.where((jnp.arange(2) == core)[:, None, None], up_cols, 0.0).reshape(WIDTH, 4)
+    up_high = up_cols.astype(BF16).astype(F32)
+    up_cols = jnp.pad(up_high, ((0, 0), (8, SMALL - 12))) + jnp.pad(up_cols - up_high, ((0, 0), (24, SMALL - 28)))
+
+    (grad_a_far,) = after([between_cores(grad_a_own)], up_cols)
     grad_a_far, *grads = lax.optimization_barrier((grad_a_far, *grads))
     grad_ups, grad_downs = grads[:4], grads[4:]
     got_ups, got_downs = relay_start(grad_ups, "z"), relay_start(grad_downs, "y")
     block = (m_own + between_cores(m_far)).astype(BF16)
-    up_cols = grad_up_b.reshape(2, 2, 4, 4, 24).transpose(2, 0, 3, 1, 4)[:, :, :, None]
-    up_cols = jnp.where((jnp.arange(2) == core)[:, None, None], up_cols, 0.0).reshape(WIDTH, 4)
-    up_high = up_cols.astype(BF16).astype(F32)
-    up_cols = jnp.pad(up_high, ((0, 0), (8, SMALL - 12))) + jnp.pad(up_cols - up_high, ((0, 0), (24, SMALL - 28)))
-
     *grad_attn, own_x, far_x, gh = call(
         back_kernel,
         place,
@@ -623,26 +623,21 @@
     far_ups, far_downs = after([send(ups_ahead, "z", 1), send(downs_ahead, "y", 1)], attn_ahead)
     up_sum = relay_end(grad_ups, got_ups, far_ups).astype(BF16)
     down_sum = relay_end(grad_downs, got_downs, far_downs).astype(BF16)
-    (far_attn,) = after([send(attn_ahead, "x", 1)], up_sum, down_sum)
-    up_parts = ring_split(up_sum, x_at)
-    down_parts = ring_split(down_sum, x_at)
-    mlp_sum = ring_reduce(
-        [
-            jnp.concatenate([u[:, :WIDTH], u[:, WIDTH:], d])
-            for u, d in zip(up_parts, down_parts)
-        ],
-        "x",
-    )
+    (far_attn,) = after([send(attn_ahead, "x", 1)], up_sum)
+    up_sum = ring_reduce(ring_split(up_sum, x_at), "x").reshape(2, 24, UP)
     attn_sum = relay_end(grad_attn, got_attn, far_attn).astype(BF16).reshape(2, 4, 24, ATTN)
     results = swap_items(after([jnp.concatenate([block, grad_x], axis=1)], attn_sum)[0])
-    attn_sum = ring_reduce([a[:, 0] for a in ring_split(attn_sum, z_at, 1)], "z")
+    attn_parts = [a[:, 0] for a in ring_split(attn_sum, z_at, 1)]
+    attn_got = ring_sent(attn_parts, "z")
+    down_parts = [d.reshape(96, WIDTH) for d in ring_split(after([down_sum], attn_got[1])[0].reshape(4, 4, 24, WIDTH), z_at, 1)]
+    down_sum = ring_total(down_parts, ring_sent(down_parts, "z")).astype(BF16)
+    attn_sum = ring_total(attn_parts, attn_got)
     block_out = jnp.where(present_rows, results[:, :WIDTH], 0).reshape(tokens.shape)
-    up_sum = jnp.concatenate([mlp_sum[:48], mlp_sum[48:96]], axis=1).reshape(2, 24, UP)
     sums = jnp.concatenate([attn_sum.astype(BF16), up_sum.astype(BF16)], axis=2)
     sums = sums.reshape(8, 6, ATTN + UP)
     got = lax.all_to_all(sums, EIGHT, 0, 0, tiled=True)
-    down_parts = ring_split(mlp_sum[96:].astype(BF16), z_at)
-    down_sum = ring_total(down_parts, after(ring_sent(down_parts, "z"), got))
+    down_parts = ring_split(down_sum, x_at)
+    down_sum = ring_total(down_parts, after(ring_sent(down_parts, "x"), got))
     out_qkv, out_out, out_up, out_down, grad_tokens, *vecs, out_up_b = call(
         outputs_kernel,
         None,

time: 169 us -> 168 us (level)
  waiting for transfers between devices: 36.5 us -> 31.9 us
  starting transfers between devices: 80 us -> 83.5 us
    ppermute x2, starting transfers between devices: 11.8 us -> 14.9 us  [swap_items(): return lax.ppermute(values, ('c', 'yl'), [(0, 0), (1, 2), (2, 1), (3, 3)])]
    ppermute x15 -> x18, starting transfers between devices: 17.7 us -> 20.7 us  [ring(): return lax.ppermute(values, axis, [(i, (i + by) % 4) for i in range(4)])]
    ppermute x18, waiting for transfers between devices: 16.7 us -> 14.3 us  [send(): return lax.ppermute(values, AXES, along(axis, by))]
    all_to_all x1, starting transfers between devices: 7.37 us -> 5.07 us  [shards(): got = lax.all_to_all(sums, EIGHT, 0, 0, tiled=True)]
    ppermute x15 -> x18, waiting for transfers between devices: 4.58 us -> 3.98 us  [ring(): return lax.ppermute(values, axis, [(i, (i + by) % 4) for i in range(4)])]
  transfers between devices with their start and end apart: 44 -> 47, of which waited for: 16 -> 17; matrix products, arithmetic and copies ran while one was open for 10% -> 10% of each run, Pallas kernels for 10% -> 11%
where the time goes in v3:
time: 168 us; the launch traced here: 167 us
  starting transfers between devices  83.5 us (50%)
  waiting for transfers between devices  31.9 us (19%)
  Pallas kernels  31.3 us (19%)
  other arithmetic  10.6 us (6%)
  local copies, waits for them, and re-layouts  7.87 us (5%)
  between operations  2 us (1%)
    pallas_call x6, Pallas kernels, call(): pl.pallas_call(kernel, out_shape=tuple((jax.ShapeDtypeStruct(s, d) for s,...  31.3 us
    ppermute x18, starting transfers between devices, send(): return lax.ppermute(values, AXES, along(axis, by))  23.4 us
    ppermute x18, starting transfers between devices, ring(): return lax.ppermute(values, axis, [(i, (i + by) % 4) for i in range(4)])  20.7 us
    ppermute x2, starting transfers between devices, swap_items(): return lax.ppermute(values, ('c', 'yl'), [(0, 0), (1, 2), (2, 1), (3, 3)])  14.9 us
    ppermute x18, waiting for transfers between devices, send(): return lax.ppermute(values, AXES, along(axis, by))  14.3 us
    ppermute x6, starting transfers between devices, between_cores(): return lax.ppermute(values, 'c', [(0, 1), (1, 0)])  9.51 us
    all_to_all x1, waiting for transfers between devices, shards(): lax.all_to_all(jnp.broadcast_to(downs[None], (16, 24, WIDTH)), ('x', 'z')...  8.64 us
    all_to_all x1, starting transfers between devices, shards(): rows = lax.all_to_all(parts, EIGHT, 0, 0, tiled=True)  5.97 us
  transfers between devices with their start and end apart: 47, of which 17 were waited for; matrix products, arithmetic and copies ran while one was open for 10% of the time, Pallas kernels for 11%

profile of v3, /device:TPU:1, one launch (start us, length us, event | category | flops | bytes accessed | tf_op | source)
XLA Modules:
  0.0 167.1 jit_solution(6659316636335738640)
XLA Ops:
  0.7 2.0 %shard_map.271 = bf16[8,6,3200]{2,1,0:T(8,128)(2,1)} custom-call(bf16[6,2304]{1,0:T(8,128)(2,1)} %qkv_ref.1, bf16[6,768]{1,0:T(8,128)(2,1)} %out_ref.1, bf16[6,3072]{1,0:T(8,128)(2,1)} %up_ref.1, bf16[6]{0:T(256)(128)(2,1)} %refs_0_.1, bf16[6]{0:T(256)(128)(2,1)} %refs_1_.1, bf16[6]{0:T(256)(128)(2,1)} %refs_2_.1, bf16[6]{0:T(256)(128)(2,1)} %refs_3_.1, ...), custom_call_target="tpu_custom_call" | custom-call | flops 1 | bytes 1 | tf_op jit(solution)/shard_map/pallas_call | solution.py:380
  2.6 6.0 %all-to-all-start = ((bf16[8,6,3200]{2,1,0:T(8,128)(2,1)}), bf16[8,6,3200]{2,1,0:T(8,128)(2,1)S(1)}, u32[]{:S(2)}, u32[]{:S(2)}) async-start(bf16[8,6,3200]{2,1,0:T(8,128)(2,1)} %shard_map.271), calls=%async_computation | async-start | bytes 819200 | tf_op jit(solution)/shard_map/all_to_all | solution.py:525
  9.6 3.5 %collective-permute-start = (bf16[128,1536]{1,0:T(8,128)(2,1)S(1)}, bf16[128,1536]{1,0:T(8,128)(2,1)S(1)}, u32[]{:S(2)}, u32[]{:S(2)}) collective-permute-start(bf16[128,1536]{1,0:T(8,128)(2,1)S(1)} %pad_maximum_fusion.2), channel_id=1, source_target_pairs={{0,0},{1,2},{2,1},{3,3},{4,4},{5,6},{6,5},{7,7},{8,8},{9,10},{10,9... | collective-permute-start | bytes 1179656 | tf_op jit(solution)/shard_map/ppermute | solution.py:400
  13.2 3.7 %all-to-all-done = bf16[8,6,3200]{2,1,0:T(8,128)(2,1)S(1)} async-done(((bf16[8,6,3200]{2,1,0:T(8,128)(2,1)}), bf16[8,6,3200]{2,1,0:T(8,128)(2,1)S(1)}, u32[]{:S(2)}, u32[]{:S(2)}) %all-to-all-start) | async-done | bytes 307232 | tf_op jit(solution)/shard_map/all_to_all | solution.py:525
  17.0 3.8 %collective-permute-start.2 = (bf16[2,24,1664]{2,1,0:T(8,128)(2,1)S(1)}, bf16[2,24,1664]{2,1,0:T(8,128)(2,1)S(1)}, u32[]{:S(2)}, u32[]{:S(2)}) collective-permute-start(bf16[2,24,1664]{2,1,0:T(8,128)(2,1)S(1)} %slice.29), channel_id=1, source_target_pairs={{0,12},{4,0},{8,4},{12,8},{1,13},{5,1},{9,5},{13,9},{2,14},{6,2},{... | collective-permute-start | bytes 479240 | tf_op jit(solution)/shard_map/ppermute | solution.py:411
  21.5 1.5 fusion.order_hbm
  23.7 2.5 %collective-permute-start.10 = (bf16[48,1536]{1,0:T(8,128)(2,1)S(1)}, bf16[48,1536]{1,0:T(8,128)(2,1)S(1)}, u32[]{:S(2)}, u32[]{:S(2)}) collective-permute-start(bf16[48,1536]{1,0:T(8,128)(2,1)S(1)} %bitcast.61), channel_id=1, source_target_pairs={{0,96},{32,0},{64,32},{96,64},{1,97},{33,1},{65,33},{97,65},{2,98}... | collective-permute-start | bytes 442376 | tf_op jit(solution)/shard_map/ppermute | solution.py:411
  26.8 1.2 collective-permute-start.12
  28.1 2.6 %collective-permute-start.1 = (bf16[128,1536]{1,0:T(8,128)(2,1)S(1)}, bf16[128,1536]{1,0:T(8,128)(2,1)}, u32[]{:S(2)}, u32[]{:S(2)}) collective-permute-start(bf16[128,1536]{1,0:T(8,128)(2,1)S(1)} %collective-permute-done), channel_id=1, source_target_pairs={{0,2},{2,0},{1,3},{3,1},{4,6},{6,4},{5,7},{7,5},{8,10},{10,8},{9,1... | collective-permute-start | bytes 1179656 | tf_op jit(solution)/shard_map/ppermute | solution.py:392
  31.3 2.5 %collective-permute-start.5 = (bf16[192,1664]{1,0:T(8,128)(2,1)S(1)}, bf16[192,1664]{1,0:T(8,128)(2,1)S(1)}, u32[]{:S(2)}, u32[]{:S(2)}) collective-permute-start(bf16[192,1664]{1,0:T(8,128)(2,1)S(1)} %bitcast.54), channel_id=1, source_target_pairs={{0,32},{1,33},{2,98},{3,99},{4,36},{5,37},{6,102},{7,103},{8,40},{... | collective-permute-start | bytes 1916936 | tf_op jit(solution)/shard_map/ppermute | solution.py:450
  34.8 4.0 %all-to-all-start.1 = ((bf16[16,24,768]{2,1,0:T(8,128)(2,1)}), bf16[16,24,768]{2,1,0:T(8,128)(2,1)S(1)}, u32[]{:S(2)}, u32[]{:S(2)}) async-start(bf16[16,24,768]{2,1,0:T(8,128)(2,1)} %broadcast_in_dim.54), calls=%async_computation.1 | async-start | bytes 1179648 | tf_op jit(solution)/shard_map/all_to_all | solution.py:532
  38.9 2.6 %collective-permute-start.13 = (bf16[192,1536]{1,0:T(8,128)(2,1)S(1)}, bf16[192,1536]{1,0:T(8,128)(2,1)}, u32[]{:S(2)}, u32[]{:S(2)}) collective-permute-start(bf16[192,1536]{1,0:T(8,128)(2,1)S(1)} %pad_maximum_fusion.1.up_0), channel_id=1, source_target_pairs={{0,4},{1,5},{2,14},{3,15},{4,8},{5,9},{6,2},{7,3},{8,12},{9,13},{1... | collective-permute-start | bytes 1769480 | tf_op jit(solution)/shard_map/ppermute | solution.py:450
  41.6 1.2 collective-permute-start.6
  42.7 8.6 %all-to-all-done.1 = bf16[16,24,768]{2,1,0:T(8,128)(2,1)S(1)} async-done(((bf16[16,24,768]{2,1,0:T(8,128)(2,1)}), bf16[16,24,768]{2,1,0:T(8,128)(2,1)S(1)}, u32[]{:S(2)}, u32[]{:S(2)}) %all-to-all-start.1) | async-done | bytes 589856 | tf_op jit(solution)/shard_map/all_to_all | solution.py:532
  53.5 1.0 constant_dynamic-update-slice_fusion
  55.5 2.0 %collective-permute-start.15 = (bf16[192,1536]{1,0:T(8,128)(2,1)}, bf16[192,1536]{1,0:T(8,128)(2,1)}, u32[]{:S(2)}, u32[]{:S(2)}) collective-permute-start(bf16[192,1536]{1,0:T(8,128)(2,1)} %collective-permute-done.13.up_1), channel_id=1, source_target_pairs={{0,4},{1,5},{2,14},{3,15},{4,8},{5,9},{6,2},{7,3},{8,12},{9,13},{1... | collective-permute-start | bytes 1769480 | tf_op jit(solution)/shard_map/ppermute | solution.py:450
  58.1 2.5 %collective-permute-done.16.down_1 = bf16[384,768]{1,0:T(8,128)(2,1)} collective-permute-done((bf16[384,768]{1,0:T(8,128)(2,1)S(1)}, bf16[384,768]{1,0:T(8,128)(2,1)}, u32[]{:S(2)}, u32[]{:S(2)}) %collective-permute-start.16) | collective-permute-done | bytes 589856 | tf_op jit(solution)/shard_map/ppermute | solution.py:450
  60.6 2.1 %collective-permute-start.18 = (bf16[384,768]{1,0:T(8,128)(2,1)}, bf16[384,768]{1,0:T(8,128)(2,1)}, u32[]{:S(2)}, u32[]{:S(2)}) collective-permute-start(bf16[384,768]{1,0:T(8,128)(2,1)} %collective-permute-done.16.down_1), channel_id=1, source_target_pairs={{0,1},{1,16},{2,19},{3,2},{4,5},{5,20},{6,23},{7,6},{8,9},{9,24},{... | collective-permute-start | bytes 1769480 | tf_op jit(solution)/shard_map/ppermute | solution.py:450
  62.7 5.6 %shard_map.272 = (bf16[256,768]{1,0:T(8,128)(2,1)}, bf16[256,1152]{1,0:T(8,128)(2,1)}, bf16[256,384]{1,0:T(8,128)(2,1)}, f32[256,128]{1,0:T(8,128)}, bf16[768,11...) custom-call(s32[4]{0:T(128)} %pad_add_fusion.1.place_ref, ...), custom_call_target="tpu_custom_call" | custom-call | flops 1 | bytes 1 | tf_op jit(solution)/shard_map/pallas_call | solution.py:380
  68.3 3.3 %collective-permute-start.9 = (bf16[768,384]{1,0:T(8,128)(2,1)}, bf16[768,384]{1,0:T(8,128)(2,1)S(1)}, u32[]{:S(2)}, u32[]{:S(2)}) collective-permute-start(bf16[768,384]{1,0:T(8,128)(2,1)} %get-tuple-element.86.own_out.own_out_ref), channel_id=1, source_target_pairs={{0,2},{2,0},{1,3},{3,1},{4,6},{6,4},{5,7},{7,5},{8,10},{10,8},{9,1... | collective-permute-start | bytes 1769480 | tf_op jit(solution)/shard_map/ppermute | solution.py:392
  71.9 1.0 slice.23
  75.1 10.8 %shard_map.273 = (f32[256,768]{1,0:T(8,128)}, f32[128,768]{1,0:T(8,128)}, f32[128,768]{1,0:T(8,128)}, f32[256,768]{1,0:T(8,128)}, f32[1,1536]{1,0:T(1,128)}, /*i...) custom-call(s32[4]{0:T(128)} %pad_add_fusion.1.place_ref, ...), custom_call_target="tpu_custom_call" | custom-call | flops 1 | bytes 1 | tf_op jit(solution)/shard_map/pallas_call | solution.py:380
  85.9 3.2 %collective-permute-start.20 = (f32[256,768]{1,0:T(8,128)}, f32[256,768]{1,0:T(8,128)S(1)}, u32[]{:S(2)}, u32[]{:S(2)}) collective-permute-start(f32[256,768]{1,0:T(8,128)} %get-tuple-element.92.own_grad_ref), channel_id=1, source_target_pairs={{0,2},{2,0},{1,3},{3,1},{4,6},{6,4},{5,7},{7,5},{8,10},{10,8},{9,1... | collective-permute-start | bytes 2359304 | tf_op jit(solution)/shard_map/ppermute | solution.py:392
  90.4 1.0 pad_add_fusion.up_cols_ref
  91.8 2.9 %collective-permute-start.22 = (bf16[192,1536]{1,0:T(8,128)(2,1)}, bf16[192,1536]{1,0:T(8,128)(2,1)S(1)}, u32[]{:S(2)}, u32[]{:S(2)}) collective-permute-start(bf16[192,1536]{1,0:T(8,128)(2,1)} %get-tuple-element.112), channel_id=1, source_target_pairs={{0,4},{1,5},{2,14},{3,15},{4,8},{5,9},{6,2},{7,3},{8,12},{9,13},{1... | collective-permute-start | bytes 1769480 | tf_op jit(solution)/shard_map/ppermute | solution.py:450
  94.8 9.5 %shard_map.274 = (bf16[192,1664]{1,0:T(8,128)(2,1)}, bf16[192,1664]{1,0:T(8,128)(2,1)}, bf16[192,1664]{1,0:T(8,128)(2,1)}, bf16[192,1664]{1,0:T(8,128)(2,1)}, f3...) custom-call(s32[4]{0:T(128)} %pad_add_fusion.1.place_ref, ...), custom_call_target="tpu_custom_call" | custom-call | flops 1 | bytes 1 | tf_op jit(solution)/shard_map/pallas_call | solution.py:380
  104.5 2.3 %collective-permute-start.24 = (bf16[192,1664]{1,0:T(8,128)(2,1)}, bf16[192,1664]{1,0:T(8,128)(2,1)S(1)}, u32[]{:S(2)}, u32[]{:S(2)}) collective-permute-start(bf16[192,1664]{1,0:T(8,128)(2,1)} %get-tuple-element.118), channel_id=1, source_target_pairs={{0,32},{1,33},{2,98},{3,99},{4,36},{5,37},{6,102},{7,103},{8,40},{... | collective-permute-start | bytes 1916936 | tf_op jit(solution)/shard_map/ppermute | solution.py:450
  107.3 1.0 add_convert_fusion.4
  108.2 2.7 %collective-permute-start.29 = (bf16[384,768]{1,0:T(8,128)(2,1)}, bf16[384,768]{1,0:T(8,128)(2,1)S(1)}, u32[]{:S(2)}, u32[]{:S(2)}) collective-permute-start(bf16[384,768]{1,0:T(8,128)(2,1)} %add_convert_fusion.4), channel_id=1, source_target_pairs={{0,1},{1,16},{2,19},{3,2},{4,5},{5,20},{6,23},{7,6},{8,9},{9,24},{... | collective-permute-start | bytes 1769480 | tf_op jit(solution)/shard_map/ppermute | solution.py:450
  111.8 2.4 %shard_map.275 = bf16[128,768]{1,0:T(8,128)(2,1)} custom-call(s32[4]{0:T(128)} %pad_add_fusion.1.place_ref, bf16[256,768]{1,0:T(8,128)(2,1)} %get-tuple-element.82.x_ref.x_hbm, f32[128,768]{1,0:T(8,128)} %get-tuple-element.109.own_x_ref, f32[128,768]{1,0:T(8,128)} %copy-done.15, f32[128,768]{1,0:T(8,128)} %get-tuple-element.116.gh_ref, ...), custom_call_target="tpu_custom_call" | custom-call | flops 1 | bytes 1 | tf_op jit(solution)/shard_map/pallas_call | solution.py:380
  114.3 1.8 %pad_maximum_fusion.3 = bf16[128,1536]{1,0:T(8,128)(2,1)} fusion(bf16[128,768]{1,0:T(8,128)(2,1)} %shard_map.275, bf16[128,768]{1,0:T(8,128)(2,1)S(1)} %add_convert_fusion.6), kind=kLoop, calls=%fused_computation.11 | loop fusion | flops 786432 | bytes 786432 | tf_op jit(solution)/shard_map/concatenate | solution.py:629
  116.0 4.3 %collective-permute-done.24 = bf16[192,1664]{1,0:T(8,128)(2,1)S(1)} collective-permute-done((bf16[192,1664]{1,0:T(8,128)(2,1)}, bf16[192,1664]{1,0:T(8,128)(2,1)S(1)}, u32[]{:S(2)}, u32[]{:S(2)}) %collective-permute-start.24) | collective-permute-done | bytes 639008 | tf_op jit(solution)/shard_map/ppermute | solution.py:450
  120.4 1.2 collective-permute-start.37
  121.5 1.8 %collective-permute-done.25 = bf16[192,1664]{1,0:T(8,128)(2,1)S(1)} collective-permute-done((bf16[192,1664]{1,0:T(8,128)(2,1)}, bf16[192,1664]{1,0:T(8,128)(2,1)S(1)}, u32[]{:S(2)}, u32[]{:S(2)}) %collective-permute-start.25) | collective-permute-done | bytes 639008 | tf_op jit(solution)/shard_map/ppermute | solution.py:450
  124.0 1.5 add_convert_fusion.3
  125.5 1.1 collective-permute-start.34
  126.7 1.5 collective-permute-start.35
  129.1 1.7 %collective-permute-done.37 = bf16[384,768]{1,0:T(8,128)(2,1)S(1)} collective-permute-done((bf16[384,768]{1,0:T(8,128)(2,1)}, bf16[384,768]{1,0:T(8,128)(2,1)S(1)}, u32[]{:S(2)}, u32[]{:S(2)}) %collective-permute-start.37) | collective-permute-done | bytes 589856 | tf_op jit(solution)/shard_map/ppermute | solution.py:450
  131.0 3.1 %collective-permute-done.26 = bf16[192,1664]{1,0:T(8,128)(2,1)S(1)} collective-permute-done((bf16[192,1664]{1,0:T(8,128)(2,1)S(1)}, bf16[192,1664]{1,0:T(8,128)(2,1)S(1)}, u32[]{:S(2)}, u32[]{:S(2)}) %collective-permute-start.26) | collective-permute-done | bytes 639008 | tf_op jit(solution)/shard_map/ppermute | solution.py:450
  134.6 1.5 collective-permute-start.31
  136.1 1.3 collective-permute-start.33
  137.3 11.4 %collective-permute-start.30 = (bf16[128,1536]{1,0:T(8,128)(2,1)}, bf16[128,1536]{1,0:T(8,128)(2,1)S(1)}, u32[]{:S(2)}, u32[]{:S(2)}) collective-permute-start(bf16[128,1536]{1,0:T(8,128)(2,1)} %pad_maximum_fusion.3), channel_id=1, source_target_pairs={{0,0},{1,2},{2,1},{3,3},{4,4},{5,6},{6,5},{7,7},{8,8},{9,10},{10,9... | collective-permute-start | bytes 1179656 | tf_op jit(solution)/shard_map/ppermute | solution.py:400
  149.0 1.3 collective-permute-start.39
  150.3 1.4 collective-permute-start.40
  152.6 5.1 %all-to-all-start.2 = ((bf16[8,6,3200]{2,1,0:T(8,128)(2,1)}), bf16[8,6,3200]{2,1,0:T(8,128)(2,1)S(1)}, u32[]{:S(2)}, u32[]{:S(2)}) async-start(bf16[8,6,3200]{2,1,0:T(8,128)(2,1)} %reshape.121), calls=%async_computation.2 | async-start | bytes 819200 | tf_op jit(solution)/shard_map/all_to_all | solution.py:638
  157.7 1.2 collective-permute-done.38
  159.5 2.6 %collective-permute-start.43 = (bf16[24,768]{1,0:T(8,128)(2,1)S(1)}, bf16[24,768]{1,0:T(8,128)(2,1)S(1)}, u32[]{:S(2)}, u32[]{:S(2)}) collective-permute-start(bf16[24,768]{1,0:T(8,128)(2,1)S(1)} %get-tuple-element.173), channel_id=1, source_target_pairs={{0,96},{32,0},{64,32},{96,64},{1,97},{33,1},{65,33},{97,65},{2,98}... | collective-permute-start | bytes 110600 | tf_op jit(solution)/shard_map/ppermute | solution.py:411
  164.7 1.2 all-to-all-done.2.got_ref
  (142 shorter events, 21.1 us)
Async XLA Ops:
  2.6 14.2 %all-to-all-start = ((bf16[8,6,3200]{2,1,0:T(8,128)(2,1)}), bf16[8,6,3200]{2,1,0:T(8,128)(2,1)S(1)}, u32[]{:S(2)}, u32[]{:S(2)}) async-start(bf16[8,6,3200]{2,1,0:T(8,128)(2,1)} %shard_map.271), calls=%async_computation | async-start | bytes 819200 | tf_op jit(solution)/shard_map/all_to_all | solution.py:525
  9.6 16.6 %collective-permute-start = (bf16[128,1536]{1,0:T(8,128)(2,1)S(1)}, bf16[128,1536]{1,0:T(8,128)(2,1)S(1)}, u32[]{:S(2)}, u32[]{:S(2)}) collective-permute-start(bf16[128,1536]{1,0:T(8,128)(2,1)S(1)} %pad_maximum_fusion.2), channel_id=1, source_target_pairs={{0,0},{1,2},{2,1},{3,3},{4,4},{5,6},{6,5},{7,7},{8,8},{9,10},{10,9... | collective-permute-start | bytes 1179656 | tf_op jit(solution)/shard_map/ppermute | solution.py:400
  17.0 9.8 %collective-permute-start.2 = (bf16[2,24,1664]{2,1,0:T(8,128)(2,1)S(1)}, bf16[2,24,1664]{2,1,0:T(8,128)(2,1)S(1)}, u32[]{:S(2)}, u32[]{:S(2)}) collective-permute-start(bf16[2,24,1664]{2,1,0:T(8,128)(2,1)S(1)} %slice.29), channel_id=1, source_target_pairs={{0,12},{4,0},{8,4},{12,8},{1,13},{5,1},{9,5},{13,9},{2,14},{6,2},{... | collective-permute-start | bytes 479240 | tf_op jit(solution)/shard_map/ppermute | solution.py:411
  20.8 7.2 %collective-permute-start.3 = (bf16[2,24,1664]{2,1,0:T(8,128)(2,1)S(1)}, bf16[2,24,1664]{2,1,0:T(8,128)(2,1)S(1)}, u32[]{:S(2)}, u32[]{:S(2)}) collective-permute-start(bf16[2,24,1664]{2,1,0:T(8,128)(2,1)S(1)} %slice.29), channel_id=1, source_target_pairs={{0,8},{4,12},{8,0},{12,4},{1,9},{5,13},{9,1},{13,5},{2,10},{6,14},... | collective-permute-start | bytes 479240 | tf_op jit(solution)/shard_map/ppermute | solution.py:411
  20.8 10.3 %collective-permute-start.4 = (bf16[2,24,1664]{2,1,0:T(8,128)(2,1)S(1)}, bf16[2,24,1664]{2,1,0:T(8,128)(2,1)S(1)}, u32[]{:S(2)}, u32[]{:S(2)}) collective-permute-start(bf16[2,24,1664]{2,1,0:T(8,128)(2,1)S(1)} %slice.29), channel_id=1, source_target_pairs={{0,4},{4,8},{8,12},{12,0},{1,5},{5,9},{9,13},{13,1},{2,6},{6,10},{... | collective-permute-start | bytes 479240 | tf_op jit(solution)/shard_map/ppermute | solution.py:411
  23.7 15.1 %collective-permute-start.10 = (bf16[48,1536]{1,0:T(8,128)(2,1)S(1)}, bf16[48,1536]{1,0:T(8,128)(2,1)S(1)}, u32[]{:S(2)}, u32[]{:S(2)}) collective-permute-start(bf16[48,1536]{1,0:T(8,128)(2,1)S(1)} %bitcast.61), channel_id=1, source_target_pairs={{0,96},{32,0},{64,32},{96,64},{1,97},{33,1},{65,33},{97,65},{2,98}... | collective-permute-start | bytes 442376 | tf_op jit(solution)/shard_map/ppermute | solution.py:411
  26.2 12.5 %collective-permute-start.11 = (bf16[48,1536]{1,0:T(8,128)(2,1)S(1)}, bf16[48,1536]{1,0:T(8,128)(2,1)S(1)}, u32[]{:S(2)}, u32[]{:S(2)}) collective-permute-start(bf16[48,1536]{1,0:T(8,128)(2,1)S(1)} %bitcast.62), channel_id=1, source_target_pairs={{0,64},{32,96},{64,0},{96,32},{1,65},{33,97},{65,1},{97,33},{2,66}... | collective-permute-start | bytes 442376 | tf_op jit(solution)/shard_map/ppermute | solution.py:411
  26.8 11.9 %collective-permute-start.12 = (bf16[48,1536]{1,0:T(8,128)(2,1)S(1)}, bf16[48,1536]{1,0:T(8,128)(2,1)S(1)}, u32[]{:S(2)}, u32[]{:S(2)}) collective-permute-start(bf16[48,1536]{1,0:T(8,128)(2,1)S(1)} %bitcast.63), channel_id=1, source_target_pairs={{0,32},{32,64},{64,96},{96,0},{1,33},{33,65},{65,97},{97,1},{2,34}... | collective-permute-start | bytes 442376 | tf_op jit(solution)/shard_map/ppermute | solution.py:411
  28.1 24.5 %collective-permute-start.1 = (bf16[128,1536]{1,0:T(8,128)(2,1)S(1)}, bf16[128,1536]{1,0:T(8,128)(2,1)}, u32[]{:S(2)}, u32[]{:S(2)}) collective-permute-start(bf16[128,1536]{1,0:T(8,128)(2,1)S(1)} %collective-permute-done), channel_id=1, source_target_pairs={{0,2},{2,0},{1,3},{3,1},{4,6},{6,4},{5,7},{7,5},{8,10},{10,8},{9,1... | collective-permute-start | bytes 1179656 | tf_op jit(solution)/shard_map/ppermute | solution.py:392
  31.3 20.1 %collective-permute-start.5 = (bf16[192,1664]{1,0:T(8,128)(2,1)S(1)}, bf16[192,1664]{1,0:T(8,128)(2,1)S(1)}, u32[]{:S(2)}, u32[]{:S(2)}) collective-permute-start(bf16[192,1664]{1,0:T(8,128)(2,1)S(1)} %bitcast.54), channel_id=1, source_target_pairs={{0,32},{1,33},{2,98},{3,99},{4,36},{5,37},{6,102},{7,103},{8,40},{... | collective-permute-start | bytes 1916936 | tf_op jit(solution)/shard_map/ppermute | solution.py:450
  34.8 16.6 %all-to-all-start.1 = ((bf16[16,24,768]{2,1,0:T(8,128)(2,1)}), bf16[16,24,768]{2,1,0:T(8,128)(2,1)S(1)}, u32[]{:S(2)}, u32[]{:S(2)}) async-start(bf16[16,24,768]{2,1,0:T(8,128)(2,1)} %broadcast_in_dim.54), calls=%async_computation.1 | async-start | bytes 1179648 | tf_op jit(solution)/shard_map/all_to_all | solution.py:532
  38.9 16.5 %copy-start.3 = (bf16[192,1536]{1,0:T(8,128)(2,1)}, bf16[192,1536]{1,0:T(8,128)(2,1)S(1)}, u32[]{:S(2)}) copy-start(bf16[192,1536]{1,0:T(8,128)(2,1)S(1)} %pad_maximum_fusion.1.up_0) | copy-start | bytes 1769476
  38.9 16.5 %collective-permute-start.13 = (bf16[192,1536]{1,0:T(8,128)(2,1)S(1)}, bf16[192,1536]{1,0:T(8,128)(2,1)}, u32[]{:S(2)}, u32[]{:S(2)}) collective-permute-start(bf16[192,1536]{1,0:T(8,128)(2,1)S(1)} %pad_maximum_fusion.1.up_0), channel_id=1, source_target_pairs={{0,4},{1,5},{2,14},{3,15},{4,8},{5,9},{6,2},{7,3},{8,12},{9,13},{1... | collective-permute-start | bytes 1769480 | tf_op jit(solution)/shard_map/ppermute | solution.py:450
  41.6 15.9 %collective-permute-start.6 = (bf16[192,1664]{1,0:T(8,128)(2,1)S(1)}, bf16[192,1664]{1,0:T(8,128)(2,1)S(1)}, u32[]{:S(2)}, u32[]{:S(2)}) collective-permute-start(bf16[192,1664]{1,0:T(8,128)(2,1)S(1)} %bitcast.55), channel_id=1, source_target_pairs={{0,96},{1,97},{2,34},{3,35},{4,100},{5,101},{6,38},{7,39},{8,104},... | collective-permute-start | bytes 1916936 | tf_op jit(solution)/shard_map/ppermute | solution.py:450
  51.4 9.2 %collective-permute-start.16 = (bf16[384,768]{1,0:T(8,128)(2,1)S(1)}, bf16[384,768]{1,0:T(8,128)(2,1)}, u32[]{:S(2)}, u32[]{:S(2)}) collective-permute-start(bf16[384,768]{1,0:T(8,128)(2,1)S(1)} %bitcast.57), channel_id=1, source_target_pairs={{0,1},{1,16},{2,19},{3,2},{4,5},{5,20},{6,23},{7,6},{8,9},{9,24},{... | collective-permute-start | bytes 1769480 | tf_op jit(solution)/shard_map/ppermute | solution.py:450
  52.3 10.3 %collective-permute-start.7 = (bf16[192,1664]{1,0:T(8,128)(2,1)S(1)}, bf16[192,1664]{1,0:T(8,128)(2,1)}, u32[]{:S(2)}, u32[]{:S(2)}) collective-permute-start(bf16[192,1664]{1,0:T(8,128)(2,1)S(1)} %collective-permute-done.5.part_1), channel_id=1, source_target_pairs={{0,32},{1,33},{2,98},{3,99},{4,36},{5,37},{6,102},{7,103},{8,40},{... | collective-permute-start | bytes 1916936 | tf_op jit(solution)/shard_map/ppermute | solution.py:450
  52.5 19.0 %collective-permute-start.14 = (bf16[192,1536]{1,0:T(8,128)(2,1)S(1)}, bf16[192,1536]{1,0:T(8,128)(2,1)}, u32[]{:S(2)}, u32[]{:S(2)}) collective-permute-start(bf16[192,1536]{1,0:T(8,128)(2,1)S(1)} %pad_maximum_fusion.1.up_0), channel_id=1, source_target_pairs={{0,12},{1,13},{2,6},{3,7},{4,0},{5,1},{6,10},{7,11},{8,4},{9,5},{1... | collective-permute-start | bytes 1769480 | tf_op jit(solution)/shard_map/ppermute | solution.py:450
  55.5 18.4 %collective-permute-start.15 = (bf16[192,1536]{1,0:T(8,128)(2,1)}, bf16[192,1536]{1,0:T(8,128)(2,1)}, u32[]{:S(2)}, u32[]{:S(2)}) collective-permute-start(bf16[192,1536]{1,0:T(8,128)(2,1)} %collective-permute-done.13.up_1), channel_id=1, source_target_pairs={{0,4},{1,5},{2,14},{3,15},{4,8},{5,9},{6,2},{7,3},{8,12},{9,13},{1... | collective-permute-start | bytes 1769480 | tf_op jit(solution)/shard_map/ppermute | solution.py:450
  57.5 16.3 %collective-permute-start.17 = (bf16[384,768]{1,0:T(8,128)(2,1)S(1)}, bf16[384,768]{1,0:T(8,128)(2,1)}, u32[]{:S(2)}, u32[]{:S(2)}) collective-permute-start(bf16[384,768]{1,0:T(8,128)(2,1)S(1)} %bitcast.58), channel_id=1, source_target_pairs={{0,17},{1,0},{2,3},{3,18},{4,21},{5,4},{6,7},{7,22},{8,25},{9,8},{... | collective-permute-start | bytes 1769480 | tf_op jit(solution)/shard_map/ppermute | solution.py:450
  60.6 13.7 %collective-permute-start.18 = (bf16[384,768]{1,0:T(8,128)(2,1)}, bf16[384,768]{1,0:T(8,128)(2,1)}, u32[]{:S(2)}, u32[]{:S(2)}) collective-permute-start(bf16[384,768]{1,0:T(8,128)(2,1)} %collective-permute-done.16.down_1), channel_id=1, source_target_pairs={{0,1},{1,16},{2,19},{3,2},{4,5},{5,20},{6,23},{7,6},{8,9},{9,24},{... | collective-permute-start | bytes 1769480 | tf_op jit(solution)/shard_map/ppermute | solution.py:450
  68.3 5.9 %collective-permute-start.9 = (bf16[768,384]{1,0:T(8,128)(2,1)}, bf16[768,384]{1,0:T(8,128)(2,1)S(1)}, u32[]{:S(2)}, u32[]{:S(2)}) collective-permute-start(bf16[768,384]{1,0:T(8,128)(2,1)} %get-tuple-element.86.own_out.own_out_ref), channel_id=1, source_target_pairs={{0,2},{2,0},{1,3},{3,1},{4,6},{6,4},{5,7},{7,5},{8,10},{10,8},{9,1... | collective-permute-start | bytes 1769480 | tf_op jit(solution)/shard_map/ppermute | solution.py:392
  71.6 2.2 %collective-permute-start.8 = (bf16[256,384]{1,0:T(8,128)(2,1)}, bf16[256,384]{1,0:T(8,128)(2,1)S(1)}, u32[]{:S(2)}, u32[]{:S(2)}) collective-permute-start(bf16[256,384]{1,0:T(8,128)(2,1)} %get-tuple-element.85.own_o.own_o_ref), channel_id=1, source_target_pairs={{0,2},{2,0},{1,3},{3,1},{4,6},{6,4},{5,7},{7,5},{8,10},{10,8},{9,1... | collective-permute-start | bytes 589832 | tf_op jit(solution)/shard_map/ppermute | solution.py:392
  85.9 5.5 %collective-permute-start.20 = (f32[256,768]{1,0:T(8,128)}, f32[256,768]{1,0:T(8,128)S(1)}, u32[]{:S(2)}, u32[]{:S(2)}) collective-permute-start(f32[256,768]{1,0:T(8,128)} %get-tuple-element.92.own_grad_ref), channel_id=1, source_target_pairs={{0,2},{2,0},{1,3},{3,1},{4,6},{6,4},{5,7},{7,5},{8,10},{10,8},{9,1... | collective-permute-start | bytes 2359304 | tf_op jit(solution)/shard_map/ppermute | solution.py:392
  89.1 5.7 %collective-permute-start.19 = (f32[128,768]{1,0:T(8,128)}, f32[128,768]{1,0:T(8,128)S(1)}, u32[]{:S(2)}, u32[]{:S(2)}) collective-permute-start(f32[128,768]{1,0:T(8,128)} %get-tuple-element.90), channel_id=1, source_target_pairs={{0,2},{2,0},{1,3},{3,1},{4,6},{6,4},{5,7},{7,5},{8,10},{10,8},{9,1... | collective-permute-start | bytes 1179656 | tf_op jit(solution)/shard_map/ppermute | solution.py:392
  91.4 15.4 %collective-permute-start.23 = (bf16[384,768]{1,0:T(8,128)(2,1)}, bf16[384,768]{1,0:T(8,128)(2,1)S(1)}, u32[]{:S(2)}, u32[]{:S(2)}) collective-permute-start(bf16[384,768]{1,0:T(8,128)(2,1)} %get-tuple-element.114), channel_id=1, source_target_pairs={{0,1},{1,16},{2,19},{3,2},{4,5},{5,20},{6,23},{7,6},{8,9},{9,24},{... | collective-permute-start | bytes 1769480 | tf_op jit(solution)/shard_map/ppermute | solution.py:450
  91.8 16.4 %collective-permute-start.22 = (bf16[192,1536]{1,0:T(8,128)(2,1)}, bf16[192,1536]{1,0:T(8,128)(2,1)S(1)}, u32[]{:S(2)}, u32[]{:S(2)}) collective-permute-start(bf16[192,1536]{1,0:T(8,128)(2,1)} %get-tuple-element.112), channel_id=1, source_target_pairs={{0,4},{1,5},{2,14},{3,15},{4,8},{5,9},{6,2},{7,3},{8,12},{9,13},{1... | collective-permute-start | bytes 1769480 | tf_op jit(solution)/shard_map/ppermute | solution.py:450
  104.4 6.7 %collective-permute-start.21 = (f32[128,768]{1,0:T(8,128)}, f32[128,768]{1,0:T(8,128)S(1)}, u32[]{:S(2)}, u32[]{:S(2)}) collective-permute-start(f32[128,768]{1,0:T(8,128)} %get-tuple-element.110), channel_id=1, source_target_pairs={{0,2},{2,0},{1,3},{3,1},{4,6},{6,4},{5,7},{7,5},{8,10},{10,8},{9,1... | collective-permute-start | bytes 1179656 | tf_op jit(solution)/shard_map/ppermute | solution.py:392
  104.5 15.9 %collective-permute-start.24 = (bf16[192,1664]{1,0:T(8,128)(2,1)}, bf16[192,1664]{1,0:T(8,128)(2,1)S(1)}, u32[]{:S(2)}, u32[]{:S(2)}) collective-permute-start(bf16[192,1664]{1,0:T(8,128)(2,1)} %get-tuple-element.118), channel_id=1, source_target_pairs={{0,32},{1,33},{2,98},{3,99},{4,36},{5,37},{6,102},{7,103},{8,40},{... | collective-permute-start | bytes 1916936 | tf_op jit(solution)/shard_map/ppermute | solution.py:450
  106.8 16.5 %collective-permute-start.25 = (bf16[192,1664]{1,0:T(8,128)(2,1)}, bf16[192,1664]{1,0:T(8,128)(2,1)S(1)}, u32[]{:S(2)}, u32[]{:S(2)}) collective-permute-start(bf16[192,1664]{1,0:T(8,128)(2,1)} %get-tuple-element.119), channel_id=1, source_target_pairs={{0,96},{1,97},{2,34},{3,35},{4,100},{5,101},{6,38},{7,39},{8,104},... | collective-permute-start | bytes 1916936 | tf_op jit(solution)/shard_map/ppermute | solution.py:450
  106.8 17.2 %collective-permute-start.27 = (bf16[192,1536]{1,0:T(8,128)(2,1)}, bf16[192,1536]{1,0:T(8,128)(2,1)}, u32[]{:S(2)}, u32[]{:S(2)}) collective-permute-start(bf16[192,1536]{1,0:T(8,128)(2,1)} %get-tuple-element.124), channel_id=1, source_target_pairs={{0,12},{1,13},{2,6},{3,7},{4,0},{5,1},{6,10},{7,11},{8,4},{9,5},{1... | collective-permute-start | bytes 1769480 | tf_op jit(solution)/shard_map/ppermute | solution.py:450
  108.2 15.4 %collective-permute-start.29 = (bf16[384,768]{1,0:T(8,128)(2,1)}, bf16[384,768]{1,0:T(8,128)(2,1)S(1)}, u32[]{:S(2)}, u32[]{:S(2)}) collective-permute-start(bf16[384,768]{1,0:T(8,128)(2,1)} %add_convert_fusion.4), channel_id=1, source_target_pairs={{0,1},{1,16},{2,19},{3,2},{4,5},{5,20},{6,23},{7,6},{8,9},{9,24},{... | collective-permute-start | bytes 1769480 | tf_op jit(solution)/shard_map/ppermute | solution.py:450
  111.1 13.0 %collective-permute-start.28 = (bf16[192,1536]{1,0:T(8,128)(2,1)S(1)}, bf16[192,1536]{1,0:T(8,128)(2,1)}, u32[]{:S(2)}, u32[]{:S(2)}) collective-permute-start(bf16[192,1536]{1,0:T(8,128)(2,1)S(1)} %add_convert_fusion.5), channel_id=1, source_target_pairs={{0,4},{1,5},{2,14},{3,15},{4,8},{5,9},{6,2},{7,3},{8,12},{9,13},{1... | collective-permute-start | bytes 1769480 | tf_op jit(solution)/shard_map/ppermute | solution.py:450
  120.4 10.4 %collective-permute-start.37 = (bf16[384,768]{1,0:T(8,128)(2,1)}, bf16[384,768]{1,0:T(8,128)(2,1)S(1)}, u32[]{:S(2)}, u32[]{:S(2)}) collective-permute-start(bf16[384,768]{1,0:T(8,128)(2,1)} %get-tuple-element.129), channel_id=1, source_target_pairs={{0,17},{1,0},{2,3},{3,18},{4,21},{5,4},{6,7},{7,22},{8,25},{9,8},{... | collective-permute-start | bytes 1769480 | tf_op jit(solution)/shard_map/ppermute | solution.py:450
  123.5 10.7 %collective-permute-start.26 = (bf16[192,1664]{1,0:T(8,128)(2,1)S(1)}, bf16[192,1664]{1,0:T(8,128)(2,1)S(1)}, u32[]{:S(2)}, u32[]{:S(2)}) collective-permute-start(bf16[192,1664]{1,0:T(8,128)(2,1)S(1)} %add_convert_fusion.1), channel_id=1, source_target_pairs={{0,32},{1,33},{2,98},{3,99},{4,36},{5,37},{6,102},{7,103},{8,40},{... | collective-permute-start | bytes 1916936 | tf_op jit(solution)/shard_map/ppermute | solution.py:450
  125.5 10.5 %collective-permute-start.34 = (bf16[48,1536]{1,0:T(8,128)(2,1)S(1)}, bf16[48,1536]{1,0:T(8,128)(2,1)S(1)}, u32[]{:S(2)}, u32[]{:S(2)}) collective-permute-start(bf16[48,1536]{1,0:T(8,128)(2,1)S(1)} %get-tuple-element.162), channel_id=1, source_target_pairs={{0,32},{32,64},{64,96},{96,0},{1,33},{33,65},{65,97},{97,1},{2,34}... | collective-permute-start | bytes 442376 | tf_op jit(solution)/shard_map/ppermute | solution.py:411
  126.7 10.7 %collective-permute-start.35 = (bf16[48,1536]{1,0:T(8,128)(2,1)S(1)}, bf16[48,1536]{1,0:T(8,128)(2,1)S(1)}, u32[]{:S(2)}, u32[]{:S(2)}) collective-permute-start(bf16[48,1536]{1,0:T(8,128)(2,1)S(1)} %get-tuple-element.164), channel_id=1, source_target_pairs={{0,64},{32,96},{64,0},{96,32},{1,65},{33,97},{65,1},{97,33},{2,66}... | collective-permute-start | bytes 442376 | tf_op jit(solution)/shard_map/ppermute | solution.py:411
  128.2 20.5 %collective-permute-start.36 = (bf16[48,1536]{1,0:T(8,128)(2,1)S(1)}, bf16[48,1536]{1,0:T(8,128)(2,1)S(1)}, u32[]{:S(2)}, u32[]{:S(2)}) collective-permute-start(bf16[48,1536]{1,0:T(8,128)(2,1)S(1)} %get-tuple-element.163), channel_id=1, source_target_pairs={{0,96},{32,0},{64,32},{96,64},{1,97},{33,1},{65,33},{97,65},{2,98}... | collective-permute-start | bytes 442376 | tf_op jit(solution)/shard_map/ppermute | solution.py:411
  134.5 14.3 %collective-permute-start.32 = (bf16[2,24,1664]{2,1,0:T(8,128)(2,1)S(1)}, bf16[2,24,1664]{2,1,0:T(8,128)(2,1)S(1)}, u32[]{:S(2)}, u32[]{:S(2)}) collective-permute-start(bf16[2,24,1664]{2,1,0:T(8,128)(2,1)S(1)} %get-tuple-element.157), channel_id=1, source_target_pairs={{0,8},{4,12},{8,0},{12,4},{1,9},{5,13},{9,1},{13,5},{2,10},{6,14},... | collective-permute-start | bytes 479240 | tf_op jit(solution)/shard_map/ppermute | solution.py:411
  134.6 15.7 %collective-permute-start.31 = (bf16[2,24,1664]{2,1,0:T(8,128)(2,1)S(1)}, bf16[2,24,1664]{2,1,0:T(8,128)(2,1)S(1)}, u32[]{:S(2)}, u32[]{:S(2)}) collective-permute-start(bf16[2,24,1664]{2,1,0:T(8,128)(2,1)S(1)} %get-tuple-element.155), channel_id=1, source_target_pairs={{0,4},{4,8},{8,12},{12,0},{1,5},{5,9},{9,13},{13,1},{2,6},{6,10},{... | collective-permute-start | bytes 479240 | tf_op jit(solution)/shard_map/ppermute | solution.py:411
  136.1 15.6 %collective-permute-start.33 = (bf16[2,24,1664]{2,1,0:T(8,128)(2,1)S(1)}, bf16[2,24,1664]{2,1,0:T(8,128)(2,1)S(1)}, u32[]{:S(2)}, u32[]{:S(2)}) collective-permute-start(bf16[2,24,1664]{2,1,0:T(8,128)(2,1)S(1)} %get-tuple-element.156), channel_id=1, source_target_pairs={{0,12},{4,0},{8,4},{12,8},{1,13},{5,1},{9,5},{13,9},{2,14},{6,2},{... | collective-permute-start | bytes 479240 | tf_op jit(solution)/shard_map/ppermute | solution.py:411
  137.3 24.8 %collective-permute-start.30 = (bf16[128,1536]{1,0:T(8,128)(2,1)}, bf16[128,1536]{1,0:T(8,128)(2,1)S(1)}, u32[]{:S(2)}, u32[]{:S(2)}) collective-permute-start(bf16[128,1536]{1,0:T(8,128)(2,1)} %pad_maximum_fusion.3), channel_id=1, source_target_pairs={{0,0},{1,2},{2,1},{3,3},{4,4},{5,6},{6,5},{7,7},{8,8},{9,10},{10,9... | collective-permute-start | bytes 1179656 | tf_op jit(solution)/shard_map/ppermute | solution.py:400
  148.9 10.0 %collective-permute-start.38 = (bf16[96,768]{1,0:T(8,128)(2,1)S(1)}, bf16[96,768]{1,0:T(8,128)(2,1)S(1)}, u32[]{:S(2)}, u32[]{:S(2)}) collective-permute-start(bf16[96,768]{1,0:T(8,128)(2,1)S(1)} %bitcast.69), channel_id=1, source_target_pairs={{0,4},{4,8},{8,12},{12,0},{1,5},{5,9},{9,13},{13,1},{2,6},{6,10},{... | collective-permute-start | bytes 442376 | tf_op jit(solution)/shard_map/ppermute | solution.py:411
  149.0 9.9 %collective-permute-start.39 = (bf16[96,768]{1,0:T(8,128)(2,1)S(1)}, bf16[96,768]{1,0:T(8,128)(2,1)S(1)}, u32[]{:S(2)}, u32[]{:S(2)}) collective-permute-start(bf16[96,768]{1,0:T(8,128)(2,1)S(1)} %bitcast.68), channel_id=1, source_target_pairs={{0,8},{4,12},{8,0},{12,4},{1,9},{5,13},{9,1},{13,5},{2,10},{6,14},... | collective-permute-start | bytes 442376 | tf_op jit(solution)/shard_map/ppermute | solution.py:411
  150.3 9.0 %collective-permute-start.40 = (bf16[96,768]{1,0:T(8,128)(2,1)S(1)}, bf16[96,768]{1,0:T(8,128)(2,1)S(1)}, u32[]{:S(2)}, u32[]{:S(2)}) collective-permute-start(bf16[96,768]{1,0:T(8,128)(2,1)S(1)} %bitcast.67), channel_id=1, source_target_pairs={{0,12},{4,0},{8,4},{12,8},{1,13},{5,1},{9,5},{13,9},{2,14},{6,2},{... | collective-permute-start | bytes 442376 | tf_op jit(solution)/shard_map/ppermute | solution.py:411
  152.6 13.3 %all-to-all-start.2 = ((bf16[8,6,3200]{2,1,0:T(8,128)(2,1)}), bf16[8,6,3200]{2,1,0:T(8,128)(2,1)S(1)}, u32[]{:S(2)}, u32[]{:S(2)}) async-start(bf16[8,6,3200]{2,1,0:T(8,128)(2,1)} %reshape.121), calls=%async_computation.2 | async-start | bytes 819200 | tf_op jit(solution)/shard_map/all_to_all | solution.py:638
  159.4 4.4 %collective-permute-start.41 = (bf16[24,768]{1,0:T(8,128)(2,1)S(1)}, bf16[24,768]{1,0:T(8,128)(2,1)S(1)}, u32[]{:S(2)}, u32[]{:S(2)}) collective-permute-start(bf16[24,768]{1,0:T(8,128)(2,1)S(1)} %get-tuple-element.175), channel_id=1, source_target_pairs={{0,32},{32,64},{64,96},{96,0},{1,33},{33,65},{65,97},{97,1},{2,34}... | collective-permute-start | bytes 110600 | tf_op jit(solution)/shard_map/ppermute | solution.py:411
  159.4 4.4 %collective-permute-start.42 = (bf16[24,768]{1,0:T(8,128)(2,1)S(1)}, bf16[24,768]{1,0:T(8,128)(2,1)S(1)}, u32[]{:S(2)}, u32[]{:S(2)}) collective-permute-start(bf16[24,768]{1,0:T(8,128)(2,1)S(1)} %get-tuple-element.174), channel_id=1, source_target_pairs={{0,64},{32,96},{64,0},{96,32},{1,65},{33,97},{65,1},{97,33},{2,66}... | collective-permute-start | bytes 110600 | tf_op jit(solution)/shard_map/ppermute | solution.py:411
  159.5 5.2 %collective-permute-start.43 = (bf16[24,768]{1,0:T(8,128)(2,1)S(1)}, bf16[24,768]{1,0:T(8,128)(2,1)S(1)}, u32[]{:S(2)}, u32[]{:S(2)}) collective-permute-start(bf16[24,768]{1,0:T(8,128)(2,1)S(1)} %get-tuple-element.173), channel_id=1, source_target_pairs={{0,96},{32,0},{64,32},{96,64},{1,97},{33,1},{65,33},{97,65},{2,98}... | collective-permute-start | bytes 110600 | tf_op jit(solution)/shard_map/ppermute | solution.py:411
  (18 other events, 117.2 us)

commit v4 on v3

--- a/solution.py
+++ b/solution.py
@@ -283,9 +283,7 @@
         grad_up_b_ref[:, first] = sums[:, :DOWN_ROWS]
         grad_up_b_ref[:, second] = sums[:, DOWN_ROWS:]
         grad_a += dot_nt(gu, up)
-    high = grad_a.astype(BF16)
-    low = (grad_a - high.astype(F32)).astype(BF16)
-    grad_a_ref[...] = dot_nt(high, order_ref[...]) + dot_nt(low, order_ref[...])
+    grad_a_ref[...] = dot_nt(grad_a.astype(BF16), order_ref[...]).astype(BF16)
     m_own_ref[...] = branch[:OWN] + h_ref[0:OWN, :] + vec_ref[7:8, :]
     m_far_ref[...] = branch[OWN:]
     grad_down_b_ref[...] = total(g_ref[0:OWN, :])
@@ -302,7 +300,7 @@
     here = pl.multiple_of(core * HALF, 128)
     there = pl.multiple_of((1 - core) * HALF, 128)
     rows_ref[...] = jnp.zeros((128, WIDTH), F32)
-    grad_a = own_grad_ref[...] + swap_halves(far_grad_ref[...])
+    grad_a = own_grad_ref[...].astype(F32) + swap_halves(far_grad_ref[...]).astype(F32)
     unit, scale = normalised(h_ref[...])
     grad_h = g_ref[...].astype(F32) + norm_back(grad_a, unit, scale, vec_ref[5:6, :])
     gh_ref[...] = grad_h[:OWN]
@@ -528,8 +526,8 @@
 
     attn = ring_gather(attn, "z")
     ups = ring_gather(ups, "x")
-    (downs,) = after([w_down], *attn)
-    downs = lax.all_to_all(jnp.broadcast_to(downs[None], (16, 24, WIDTH)), ("x", "z"), 0, 0, tiled=True)
+    (downs,) = after([jnp.broadcast_to(w_down[None], (16, 24, WIDTH))], *attn[:3])
+    downs = lax.all_to_all(downs, ("x", "z"), 0, 0, tiled=True)
     item = jnp.concatenate([mine, between_cores(mine)], axis=0)
     x, g = item[:, :WIDTH], item[:, WIDTH:]
     attn = jnp.concatenate(ring_order(attn, z_at), axis=1).reshape(BLOCK, ATTN)
@@ -569,7 +567,7 @@
             ((ROWS, WIDTH), F32),
             ((OWN, WIDTH), F32),
             ((OWN, WIDTH), F32),
-            ((ROWS, WIDTH), F32),
+            ((ROWS, WIDTH), BF16),
             ((1, UP), F32),
             ((1, WIDTH), F32),
         )

time: 168 us -> 168 us (level)
  transfers between devices with their start and end apart: 47 -> 47, of which waited for: 17 -> 18; matrix products, arithmetic and copies ran while one was open for 10% -> 10% of each run, Pallas kernels for 11% -> 10%
where the time goes in v4:
time: 168 us; the launch traced here: 167 us
  starting transfers between devices  83.4 us (50%)
  waiting for transfers between devices  32.2 us (19%)
  Pallas kernels  30.9 us (18%)
  other arithmetic  10.7 us (6%)
  local copies, waits for them, and re-layouts  7.65 us (5%)
  between operations  2.01 us (1%)
    pallas_call x6, Pallas kernels, call(): pl.pallas_call(kernel, out_shape=tuple((jax.ShapeDtypeStruct(s, d) for s,...  30.9 us
    ppermute x18, starting transfers between devices, send(): return lax.ppermute(values, AXES, along(axis, by))  24 us
    ppermute x18, starting transfers between devices, ring(): return lax.ppermute(values, axis, [(i, (i + by) % 4) for i in range(4)])  20.6 us
    ppermute x2, starting transfers between devices, swap_items(): return lax.ppermute(values, ('c', 'yl'), [(0, 0), (1, 2), (2, 1), (3, 3)])  14.8 us
    ppermute x18, waiting for transfers between devices, send(): return lax.ppermute(values, AXES, along(axis, by))  14.2 us
    ppermute x6, starting transfers between devices, between_cores(): return lax.ppermute(values, 'c', [(0, 1), (1, 0)])  9.22 us
    all_to_all x1, waiting for transfers between devices, shards(): downs = lax.all_to_all(downs, ('x', 'z'), 0, 0, tiled=True)  8.46 us
    all_to_all x1, starting transfers between devices, shards(): rows = lax.all_to_all(parts, EIGHT, 0, 0, tiled=True)  5.97 us
  transfers between devices with their start and end apart: 47, of which 18 were waited for; matrix products, arithmetic and copies ran while one was open for 10% of the time, Pallas kernels for 10%

profile of v4, /device:TPU:1, one launch (start us, length us, event | category | flops | bytes accessed | tf_op | source)
XLA Modules:
  0.0 167.0 jit_solution(8696621251018031212)
XLA Ops:
  0.7 2.0 %shard_map.271 = bf16[8,6,3200]{2,1,0:T(8,128)(2,1)} custom-call(bf16[6,2304]{1,0:T(8,128)(2,1)} %qkv_ref.1, bf16[6,768]{1,0:T(8,128)(2,1)} %out_ref.1, bf16[6,3072]{1,0:T(8,128)(2,1)} %up_ref.1, bf16[6]{0:T(256)(128)(2,1)} %refs_0_.1, bf16[6]{0:T(256)(128)(2,1)} %refs_1_.1, bf16[6]{0:T(256)(128)(2,1)} %refs_2_.1, bf16[6]{0:T(256)(128)(2,1)} %refs_3_.1, ...), custom_call_target="tpu_custom_call" | custom-call | flops 1 | bytes 1 | tf_op jit(solution)/shard_map/pallas_call | solution.py:378
  2.6 6.0 %all-to-all-start = ((bf16[8,6,3200]{2,1,0:T(8,128)(2,1)}), bf16[8,6,3200]{2,1,0:T(8,128)(2,1)S(1)}, u32[]{:S(2)}, u32[]{:S(2)}) async-start(bf16[8,6,3200]{2,1,0:T(8,128)(2,1)} %shard_map.271), calls=%async_computation | async-start | bytes 819200 | tf_op jit(solution)/shard_map/all_to_all | solution.py:523
  9.6 3.5 %collective-permute-start = (bf16[128,1536]{1,0:T(8,128)(2,1)S(1)}, bf16[128,1536]{1,0:T(8,128)(2,1)S(1)}, u32[]{:S(2)}, u32[]{:S(2)}) collective-permute-start(bf16[128,1536]{1,0:T(8,128)(2,1)S(1)} %pad_maximum_fusion.2), channel_id=1, source_target_pairs={{0,0},{1,2},{2,1},{3,3},{4,4},{5,6},{6,5},{7,7},{8,8},{9,10},{10,9... | collective-permute-start | bytes 1179656 | tf_op jit(solution)/shard_map/ppermute | solution.py:398
  13.2 3.7 %all-to-all-done = bf16[8,6,3200]{2,1,0:T(8,128)(2,1)S(1)} async-done(((bf16[8,6,3200]{2,1,0:T(8,128)(2,1)}), bf16[8,6,3200]{2,1,0:T(8,128)(2,1)S(1)}, u32[]{:S(2)}, u32[]{:S(2)}) %all-to-all-start) | async-done | bytes 307232 | tf_op jit(solution)/shard_map/all_to_all | solution.py:523
  17.0 3.8 %collective-permute-start.2 = (bf16[2,24,1664]{2,1,0:T(8,128)(2,1)S(1)}, bf16[2,24,1664]{2,1,0:T(8,128)(2,1)S(1)}, u32[]{:S(2)}, u32[]{:S(2)}) collective-permute-start(bf16[2,24,1664]{2,1,0:T(8,128)(2,1)S(1)} %slice.29), channel_id=1, source_target_pairs={{0,12},{4,0},{8,4},{12,8},{1,13},{5,1},{9,5},{13,9},{2,14},{6,2},{... | collective-permute-start | bytes 479240 | tf_op jit(solution)/shard_map/ppermute | solution.py:409
  21.5 1.5 fusion.order_hbm
  23.6 2.5 %collective-permute-start.10 = (bf16[48,1536]{1,0:T(8,128)(2,1)S(1)}, bf16[48,1536]{1,0:T(8,128)(2,1)S(1)}, u32[]{:S(2)}, u32[]{:S(2)}) collective-permute-start(bf16[48,1536]{1,0:T(8,128)(2,1)S(1)} %bitcast.61), channel_id=1, source_target_pairs={{0,96},{32,0},{64,32},{96,64},{1,97},{33,1},{65,33},{97,65},{2,98}... | collective-permute-start | bytes 442376 | tf_op jit(solution)/shard_map/ppermute | solution.py:409
  26.8 1.2 collective-permute-start.12
  28.1 2.6 %collective-permute-start.1 = (bf16[128,1536]{1,0:T(8,128)(2,1)S(1)}, bf16[128,1536]{1,0:T(8,128)(2,1)}, u32[]{:S(2)}, u32[]{:S(2)}) collective-permute-start(bf16[128,1536]{1,0:T(8,128)(2,1)S(1)} %collective-permute-done), channel_id=1, source_target_pairs={{0,2},{2,0},{1,3},{3,1},{4,6},{6,4},{5,7},{7,5},{8,10},{10,8},{9,1... | collective-permute-start | bytes 1179656 | tf_op jit(solution)/shard_map/ppermute | solution.py:390
  31.3 2.5 %collective-permute-start.5 = (bf16[192,1664]{1,0:T(8,128)(2,1)S(1)}, bf16[192,1664]{1,0:T(8,128)(2,1)S(1)}, u32[]{:S(2)}, u32[]{:S(2)}) collective-permute-start(bf16[192,1664]{1,0:T(8,128)(2,1)S(1)} %bitcast.54), channel_id=1, source_target_pairs={{0,32},{1,33},{2,98},{3,99},{4,36},{5,37},{6,102},{7,103},{8,40},{... | collective-permute-start | bytes 1916936 | tf_op jit(solution)/shard_map/ppermute | solution.py:448
  34.7 4.0 %all-to-all-start.1 = ((bf16[16,24,768]{2,1,0:T(8,128)(2,1)}), bf16[16,24,768]{2,1,0:T(8,128)(2,1)S(1)}, u32[]{:S(2)}, u32[]{:S(2)}) async-start(bf16[16,24,768]{2,1,0:T(8,128)(2,1)} %broadcast_in_dim.54), calls=%async_computation.1 | async-start | bytes 1179648 | tf_op jit(solution)/shard_map/all_to_all | solution.py:530
  38.9 2.6 %collective-permute-start.13 = (bf16[192,1536]{1,0:T(8,128)(2,1)S(1)}, bf16[192,1536]{1,0:T(8,128)(2,1)}, u32[]{:S(2)}, u32[]{:S(2)}) collective-permute-start(bf16[192,1536]{1,0:T(8,128)(2,1)S(1)} %pad_maximum_fusion.1.up_0), channel_id=1, source_target_pairs={{0,4},{1,5},{2,14},{3,15},{4,8},{5,9},{6,2},{7,3},{8,12},{9,13},{1... | collective-permute-start | bytes 1769480 | tf_op jit(solution)/shard_map/ppermute | solution.py:448
  41.5 1.2 collective-permute-start.6
  42.7 8.5 %all-to-all-done.1 = bf16[16,24,768]{2,1,0:T(8,128)(2,1)S(1)} async-done(((bf16[16,24,768]{2,1,0:T(8,128)(2,1)}), bf16[16,24,768]{2,1,0:T(8,128)(2,1)S(1)}, u32[]{:S(2)}, u32[]{:S(2)}) %all-to-all-start.1) | async-done | bytes 589856 | tf_op jit(solution)/shard_map/all_to_all | solution.py:530
  51.2 1.0 collective-permute-start.16
  52.4 1.0 collective-permute-start.14
  53.4 1.0 constant_dynamic-update-slice_fusion
  55.4 2.1 %collective-permute-start.15 = (bf16[192,1536]{1,0:T(8,128)(2,1)}, bf16[192,1536]{1,0:T(8,128)(2,1)}, u32[]{:S(2)}, u32[]{:S(2)}) collective-permute-start(bf16[192,1536]{1,0:T(8,128)(2,1)} %collective-permute-done.13.up_1), channel_id=1, source_target_pairs={{0,4},{1,5},{2,14},{3,15},{4,8},{5,9},{6,2},{7,3},{8,12},{9,13},{1... | collective-permute-start | bytes 1769480 | tf_op jit(solution)/shard_map/ppermute | solution.py:448
  58.2 2.2 %collective-permute-done.16.down_1 = bf16[384,768]{1,0:T(8,128)(2,1)} collective-permute-done((bf16[384,768]{1,0:T(8,128)(2,1)S(1)}, bf16[384,768]{1,0:T(8,128)(2,1)}, u32[]{:S(2)}, u32[]{:S(2)}) %collective-permute-start.16) | collective-permute-done | bytes 589856 | tf_op jit(solution)/shard_map/ppermute | solution.py:448
  60.4 2.1 %collective-permute-start.18 = (bf16[384,768]{1,0:T(8,128)(2,1)}, bf16[384,768]{1,0:T(8,128)(2,1)}, u32[]{:S(2)}, u32[]{:S(2)}) collective-permute-start(bf16[384,768]{1,0:T(8,128)(2,1)} %collective-permute-done.16.down_1), channel_id=1, source_target_pairs={{0,1},{1,16},{2,19},{3,2},{4,5},{5,20},{6,23},{7,6},{8,9},{9,24},{... | collective-permute-start | bytes 1769480 | tf_op jit(solution)/shard_map/ppermute | solution.py:448
  62.5 5.6 %shard_map.272 = (bf16[256,768]{1,0:T(8,128)(2,1)}, bf16[256,1152]{1,0:T(8,128)(2,1)}, bf16[256,384]{1,0:T(8,128)(2,1)}, f32[256,128]{1,0:T(8,128)}, bf16[768,11...) custom-call(s32[4]{0:T(128)} %pad_add_fusion.1.place_ref, ...), custom_call_target="tpu_custom_call" | custom-call | flops 1 | bytes 1 | tf_op jit(solution)/shard_map/pallas_call | solution.py:378
  68.1 3.2 %collective-permute-start.9 = (bf16[768,384]{1,0:T(8,128)(2,1)}, bf16[768,384]{1,0:T(8,128)(2,1)S(1)}, u32[]{:S(2)}, u32[]{:S(2)}) collective-permute-start(bf16[768,384]{1,0:T(8,128)(2,1)} %get-tuple-element.86.own_out.own_out_ref), channel_id=1, source_target_pairs={{0,2},{2,0},{1,3},{3,1},{4,6},{6,4},{5,7},{7,5},{8,10},{10,8},{9,1... | collective-permute-start | bytes 1769480 | tf_op jit(solution)/shard_map/ppermute | solution.py:390
  71.6 1.0 slice.23
  75.1 10.7 %shard_map.273 = (f32[256,768]{1,0:T(8,128)}, f32[128,768]{1,0:T(8,128)}, f32[128,768]{1,0:T(8,128)}, bf16[256,768]{1,0:T(8,128)(2,1)}, f32[1,1536]{1,0:T(1,128)...) custom-call(s32[4]{0:T(128)} %pad_add_fusion.1.place_ref, ...), custom_call_target="tpu_custom_call" | custom-call | flops 1 | bytes 1 | tf_op jit(solution)/shard_map/pallas_call | solution.py:378
  85.8 2.9 %collective-permute-start.19 = (f32[128,768]{1,0:T(8,128)}, f32[128,768]{1,0:T(8,128)S(1)}, u32[]{:S(2)}, u32[]{:S(2)}) collective-permute-start(f32[128,768]{1,0:T(8,128)} %get-tuple-element.90), channel_id=1, source_target_pairs={{0,2},{2,0},{1,3},{3,1},{4,6},{6,4},{5,7},{7,5},{8,10},{10,8},{9,1... | collective-permute-start | bytes 1179656 | tf_op jit(solution)/shard_map/ppermute | solution.py:390
  90.0 1.0 pad_add_fusion.up_cols_ref
  92.0 3.0 %collective-permute-start.22 = (bf16[192,1536]{1,0:T(8,128)(2,1)}, bf16[192,1536]{1,0:T(8,128)(2,1)S(1)}, u32[]{:S(2)}, u32[]{:S(2)}) collective-permute-start(bf16[192,1536]{1,0:T(8,128)(2,1)} %get-tuple-element.112), channel_id=1, source_target_pairs={{0,4},{1,5},{2,14},{3,15},{4,8},{5,9},{6,2},{7,3},{8,12},{9,13},{1... | collective-permute-start | bytes 1769480 | tf_op jit(solution)/shard_map/ppermute | solution.py:448
  95.0 9.2 %shard_map.274 = (bf16[192,1664]{1,0:T(8,128)(2,1)}, bf16[192,1664]{1,0:T(8,128)(2,1)}, bf16[192,1664]{1,0:T(8,128)(2,1)}, bf16[192,1664]{1,0:T(8,128)(2,1)}, f3...) custom-call(s32[4]{0:T(128)} %pad_add_fusion.1.place_ref, ...), custom_call_target="tpu_custom_call" | custom-call | flops 1 | bytes 1 | tf_op jit(solution)/shard_map/pallas_call | solution.py:378
  104.3 2.6 %collective-permute-start.24 = (bf16[192,1664]{1,0:T(8,128)(2,1)}, bf16[192,1664]{1,0:T(8,128)(2,1)S(1)}, u32[]{:S(2)}, u32[]{:S(2)}) collective-permute-start(bf16[192,1664]{1,0:T(8,128)(2,1)} %get-tuple-element.118), channel_id=1, source_target_pairs={{0,32},{1,33},{2,98},{3,99},{4,36},{5,37},{6,102},{7,103},{8,40},{... | collective-permute-start | bytes 1916936 | tf_op jit(solution)/shard_map/ppermute | solution.py:448
  107.3 2.5 %collective-permute-start.29 = (bf16[384,768]{1,0:T(8,128)(2,1)S(1)}, bf16[384,768]{1,0:T(8,128)(2,1)}, u32[]{:S(2)}, u32[]{:S(2)}) collective-permute-start(bf16[384,768]{1,0:T(8,128)(2,1)S(1)} %add_convert_fusion.4), channel_id=1, source_target_pairs={{0,1},{1,16},{2,19},{3,2},{4,5},{5,20},{6,23},{7,6},{8,9},{9,24},{... | collective-permute-start | bytes 1769480 | tf_op jit(solution)/shard_map/ppermute | solution.py:448
  110.6 2.4 %shard_map.275 = bf16[128,768]{1,0:T(8,128)(2,1)} custom-call(s32[4]{0:T(128)} %pad_add_fusion.1.place_ref, bf16[256,768]{1,0:T(8,128)(2,1)} %get-tuple-element.82.x_ref.x_hbm, f32[128,768]{1,0:T(8,128)} %get-tuple-element.109.own_x_ref, f32[128,768]{1,0:T(8,128)} %copy-done.15, f32[128,768]{1,0:T(8,128)} %get-tuple-element.116.gh_ref, ...), custom_call_target="tpu_custom_call" | custom-call | flops 1 | bytes 1 | tf_op jit(solution)/shard_map/pallas_call | solution.py:378
  113.1 1.8 %pad_maximum_fusion.3 = bf16[128,1536]{1,0:T(8,128)(2,1)} fusion(bf16[128,768]{1,0:T(8,128)(2,1)} %shard_map.275, bf16[128,768]{1,0:T(8,128)(2,1)S(1)} %add_convert_fusion.6), kind=kLoop, calls=%fused_computation.11 | loop fusion | flops 786432 | bytes 786432 | tf_op jit(solution)/shard_map/concatenate | solution.py:627
  114.8 5.4 %collective-permute-done.24 = bf16[192,1664]{1,0:T(8,128)(2,1)S(1)} collective-permute-done((bf16[192,1664]{1,0:T(8,128)(2,1)}, bf16[192,1664]{1,0:T(8,128)(2,1)S(1)}, u32[]{:S(2)}, u32[]{:S(2)}) %collective-permute-start.24) | collective-permute-done | bytes 639008 | tf_op jit(solution)/shard_map/ppermute | solution.py:448
  120.2 1.3 collective-permute-start.37
  121.6 1.6 collective-permute-done.25
  124.0 1.5 add_convert_fusion.3
  125.6 1.0 collective-permute-start.34
  126.6 1.9 %collective-permute-start.35 = (bf16[48,1536]{1,0:T(8,128)(2,1)S(1)}, bf16[48,1536]{1,0:T(8,128)(2,1)S(1)}, u32[]{:S(2)}, u32[]{:S(2)}) collective-permute-start(bf16[48,1536]{1,0:T(8,128)(2,1)S(1)} %get-tuple-element.164), channel_id=1, source_target_pairs={{0,64},{32,96},{64,0},{96,32},{1,65},{33,97},{65,1},{97,33},{2,66}... | collective-permute-start | bytes 442376 | tf_op jit(solution)/shard_map/ppermute | solution.py:409
  129.1 1.6 collective-permute-done.37
  130.7 1.3 add_convert_fusion.2
  132.0 2.4 %collective-permute-done.26 = bf16[192,1664]{1,0:T(8,128)(2,1)S(1)} collective-permute-done((bf16[192,1664]{1,0:T(8,128)(2,1)S(1)}, bf16[192,1664]{1,0:T(8,128)(2,1)S(1)}, u32[]{:S(2)}, u32[]{:S(2)}) %collective-permute-start.26) | collective-permute-done | bytes 639008 | tf_op jit(solution)/shard_map/ppermute | solution.py:448
  135.1 2.3 %collective-permute-start.33 = (bf16[2,24,1664]{2,1,0:T(8,128)(2,1)S(1)}, bf16[2,24,1664]{2,1,0:T(8,128)(2,1)S(1)}, u32[]{:S(2)}, u32[]{:S(2)}) collective-permute-start(bf16[2,24,1664]{2,1,0:T(8,128)(2,1)S(1)} %get-tuple-element.156), channel_id=1, source_target_pairs={{0,12},{4,0},{8,4},{12,8},{1,13},{5,1},{9,5},{13,9},{2,14},{6,2},{... | collective-permute-start | bytes 479240 | tf_op jit(solution)/shard_map/ppermute | solution.py:409
  137.5 11.2 %collective-permute-start.30 = (bf16[128,1536]{1,0:T(8,128)(2,1)}, bf16[128,1536]{1,0:T(8,128)(2,1)S(1)}, u32[]{:S(2)}, u32[]{:S(2)}) collective-permute-start(bf16[128,1536]{1,0:T(8,128)(2,1)} %pad_maximum_fusion.3), channel_id=1, source_target_pairs={{0,0},{1,2},{2,1},{3,3},{4,4},{5,6},{6,5},{7,7},{8,8},{9,10},{10,9... | collective-permute-start | bytes 1179656 | tf_op jit(solution)/shard_map/ppermute | solution.py:398
  149.9 1.8 %collective-permute-start.40 = (bf16[96,768]{1,0:T(8,128)(2,1)S(1)}, bf16[96,768]{1,0:T(8,128)(2,1)S(1)}, u32[]{:S(2)}, u32[]{:S(2)}) collective-permute-start(bf16[96,768]{1,0:T(8,128)(2,1)S(1)} %bitcast.67), channel_id=1, source_target_pairs={{0,12},{4,0},{8,4},{12,8},{1,13},{5,1},{9,5},{13,9},{2,14},{6,2},{... | collective-permute-start | bytes 442376 | tf_op jit(solution)/shard_map/ppermute | solution.py:409
  152.6 4.9 %all-to-all-start.2 = ((bf16[8,6,3200]{2,1,0:T(8,128)(2,1)}), bf16[8,6,3200]{2,1,0:T(8,128)(2,1)S(1)}, u32[]{:S(2)}, u32[]{:S(2)}) async-start(bf16[8,6,3200]{2,1,0:T(8,128)(2,1)} %reshape.121), calls=%async_computation.2 | async-start | bytes 819200 | tf_op jit(solution)/shard_map/all_to_all | solution.py:636
  157.6 1.5 collective-permute-done.38
  159.8 2.6 %collective-permute-start.43 = (bf16[24,768]{1,0:T(8,128)(2,1)S(1)}, bf16[24,768]{1,0:T(8,128)(2,1)S(1)}, u32[]{:S(2)}, u32[]{:S(2)}) collective-permute-start(bf16[24,768]{1,0:T(8,128)(2,1)S(1)} %get-tuple-element.173), channel_id=1, source_target_pairs={{0,96},{32,0},{64,32},{96,64},{1,97},{33,1},{65,33},{97,65},{2,98}... | collective-permute-start | bytes 110600 | tf_op jit(solution)/shard_map/ppermute | solution.py:409
  165.9 1.0 shard_map.276
  (142 shorter events, 20.7 us)
Async XLA Ops:
  2.6 14.2 %all-to-all-start = ((bf16[8,6,3200]{2,1,0:T(8,128)(2,1)}), bf16[8,6,3200]{2,1,0:T(8,128)(2,1)S(1)}, u32[]{:S(2)}, u32[]{:S(2)}) async-start(bf16[8,6,3200]{2,1,0:T(8,128)(2,1)} %shard_map.271), calls=%async_computation | async-start | bytes 819200 | tf_op jit(solution)/shard_map/all_to_all | solution.py:523
  9.6 16.6 %collective-permute-start = (bf16[128,1536]{1,0:T(8,128)(2,1)S(1)}, bf16[128,1536]{1,0:T(8,128)(2,1)S(1)}, u32[]{:S(2)}, u32[]{:S(2)}) collective-permute-start(bf16[128,1536]{1,0:T(8,128)(2,1)S(1)} %pad_maximum_fusion.2), channel_id=1, source_target_pairs={{0,0},{1,2},{2,1},{3,3},{4,4},{5,6},{6,5},{7,7},{8,8},{9,10},{10,9... | collective-permute-start | bytes 1179656 | tf_op jit(solution)/shard_map/ppermute | solution.py:398
  17.0 9.8 %collective-permute-start.2 = (bf16[2,24,1664]{2,1,0:T(8,128)(2,1)S(1)}, bf16[2,24,1664]{2,1,0:T(8,128)(2,1)S(1)}, u32[]{:S(2)}, u32[]{:S(2)}) collective-permute-start(bf16[2,24,1664]{2,1,0:T(8,128)(2,1)S(1)} %slice.29), channel_id=1, source_target_pairs={{0,12},{4,0},{8,4},{12,8},{1,13},{5,1},{9,5},{13,9},{2,14},{6,2},{... | collective-permute-start | bytes 479240 | tf_op jit(solution)/shard_map/ppermute | solution.py:409
  20.8 7.2 %collective-permute-start.3 = (bf16[2,24,1664]{2,1,0:T(8,128)(2,1)S(1)}, bf16[2,24,1664]{2,1,0:T(8,128)(2,1)S(1)}, u32[]{:S(2)}, u32[]{:S(2)}) collective-permute-start(bf16[2,24,1664]{2,1,0:T(8,128)(2,1)S(1)} %slice.29), channel_id=1, source_target_pairs={{0,8},{4,12},{8,0},{12,4},{1,9},{5,13},{9,1},{13,5},{2,10},{6,14},... | collective-permute-start | bytes 479240 | tf_op jit(solution)/shard_map/ppermute | solution.py:409
  20.8 10.3 %collective-permute-start.4 = (bf16[2,24,1664]{2,1,0:T(8,128)(2,1)S(1)}, bf16[2,24,1664]{2,1,0:T(8,128)(2,1)S(1)}, u32[]{:S(2)}, u32[]{:S(2)}) collective-permute-start(bf16[2,24,1664]{2,1,0:T(8,128)(2,1)S(1)} %slice.29), channel_id=1, source_target_pairs={{0,4},{4,8},{8,12},{12,0},{1,5},{5,9},{9,13},{13,1},{2,6},{6,10},{... | collective-permute-start | bytes 479240 | tf_op jit(solution)/shard_map/ppermute | solution.py:409
  23.6 15.1 %collective-permute-start.10 = (bf16[48,1536]{1,0:T(8,128)(2,1)S(1)}, bf16[48,1536]{1,0:T(8,128)(2,1)S(1)}, u32[]{:S(2)}, u32[]{:S(2)}) collective-permute-start(bf16[48,1536]{1,0:T(8,128)(2,1)S(1)} %bitcast.61), channel_id=1, source_target_pairs={{0,96},{32,0},{64,32},{96,64},{1,97},{33,1},{65,33},{97,65},{2,98}... | collective-permute-start | bytes 442376 | tf_op jit(solution)/shard_map/ppermute | solution.py:409
  26.1 12.6 %collective-permute-start.11 = (bf16[48,1536]{1,0:T(8,128)(2,1)S(1)}, bf16[48,1536]{1,0:T(8,128)(2,1)S(1)}, u32[]{:S(2)}, u32[]{:S(2)}) collective-permute-start(bf16[48,1536]{1,0:T(8,128)(2,1)S(1)} %bitcast.62), channel_id=1, source_target_pairs={{0,64},{32,96},{64,0},{96,32},{1,65},{33,97},{65,1},{97,33},{2,66}... | collective-permute-start | bytes 442376 | tf_op jit(solution)/shard_map/ppermute | solution.py:409
  26.8 11.9 %collective-permute-start.12 = (bf16[48,1536]{1,0:T(8,128)(2,1)S(1)}, bf16[48,1536]{1,0:T(8,128)(2,1)S(1)}, u32[]{:S(2)}, u32[]{:S(2)}) collective-permute-start(bf16[48,1536]{1,0:T(8,128)(2,1)S(1)} %bitcast.63), channel_id=1, source_target_pairs={{0,32},{32,64},{64,96},{96,0},{1,33},{33,65},{65,97},{97,1},{2,34}... | collective-permute-start | bytes 442376 | tf_op jit(solution)/shard_map/ppermute | solution.py:409
  28.1 24.4 %collective-permute-start.1 = (bf16[128,1536]{1,0:T(8,128)(2,1)S(1)}, bf16[128,1536]{1,0:T(8,128)(2,1)}, u32[]{:S(2)}, u32[]{:S(2)}) collective-permute-start(bf16[128,1536]{1,0:T(8,128)(2,1)S(1)} %collective-permute-done), channel_id=1, source_target_pairs={{0,2},{2,0},{1,3},{3,1},{4,6},{6,4},{5,7},{7,5},{8,10},{10,8},{9,1... | collective-permute-start | bytes 1179656 | tf_op jit(solution)/shard_map/ppermute | solution.py:390
  31.3 19.9 %collective-permute-start.5 = (bf16[192,1664]{1,0:T(8,128)(2,1)S(1)}, bf16[192,1664]{1,0:T(8,128)(2,1)S(1)}, u32[]{:S(2)}, u32[]{:S(2)}) collective-permute-start(bf16[192,1664]{1,0:T(8,128)(2,1)S(1)} %bitcast.54), channel_id=1, source_target_pairs={{0,32},{1,33},{2,98},{3,99},{4,36},{5,37},{6,102},{7,103},{8,40},{... | collective-permute-start | bytes 1916936 | tf_op jit(solution)/shard_map/ppermute | solution.py:448
  34.7 16.4 %all-to-all-start.1 = ((bf16[16,24,768]{2,1,0:T(8,128)(2,1)}), bf16[16,24,768]{2,1,0:T(8,128)(2,1)S(1)}, u32[]{:S(2)}, u32[]{:S(2)}) async-start(bf16[16,24,768]{2,1,0:T(8,128)(2,1)} %broadcast_in_dim.54), calls=%async_computation.1 | async-start | bytes 1179648 | tf_op jit(solution)/shard_map/all_to_all | solution.py:530
  38.9 16.5 %copy-start.3 = (bf16[192,1536]{1,0:T(8,128)(2,1)}, bf16[192,1536]{1,0:T(8,128)(2,1)S(1)}, u32[]{:S(2)}) copy-start(bf16[192,1536]{1,0:T(8,128)(2,1)S(1)} %pad_maximum_fusion.1.up_0) | copy-start | bytes 1769476
  38.9 16.5 %collective-permute-start.13 = (bf16[192,1536]{1,0:T(8,128)(2,1)S(1)}, bf16[192,1536]{1,0:T(8,128)(2,1)}, u32[]{:S(2)}, u32[]{:S(2)}) collective-permute-start(bf16[192,1536]{1,0:T(8,128)(2,1)S(1)} %pad_maximum_fusion.1.up_0), channel_id=1, source_target_pairs={{0,4},{1,5},{2,14},{3,15},{4,8},{5,9},{6,2},{7,3},{8,12},{9,13},{1... | collective-permute-start | bytes 1769480 | tf_op jit(solution)/shard_map/ppermute | solution.py:448
  41.5 16.0 %collective-permute-start.6 = (bf16[192,1664]{1,0:T(8,128)(2,1)S(1)}, bf16[192,1664]{1,0:T(8,128)(2,1)S(1)}, u32[]{:S(2)}, u32[]{:S(2)}) collective-permute-start(bf16[192,1664]{1,0:T(8,128)(2,1)S(1)} %bitcast.55), channel_id=1, source_target_pairs={{0,96},{1,97},{2,34},{3,35},{4,100},{5,101},{6,38},{7,39},{8,104},... | collective-permute-start | bytes 1916936 | tf_op jit(solution)/shard_map/ppermute | solution.py:448
  51.2 9.2 %collective-permute-start.16 = (bf16[384,768]{1,0:T(8,128)(2,1)S(1)}, bf16[384,768]{1,0:T(8,128)(2,1)}, u32[]{:S(2)}, u32[]{:S(2)}) collective-permute-start(bf16[384,768]{1,0:T(8,128)(2,1)S(1)} %bitcast.57), channel_id=1, source_target_pairs={{0,1},{1,16},{2,19},{3,2},{4,5},{5,20},{6,23},{7,6},{8,9},{9,24},{... | collective-permute-start | bytes 1769480 | tf_op jit(solution)/shard_map/ppermute | solution.py:448
  52.1 10.3 %collective-permute-start.7 = (bf16[192,1664]{1,0:T(8,128)(2,1)S(1)}, bf16[192,1664]{1,0:T(8,128)(2,1)}, u32[]{:S(2)}, u32[]{:S(2)}) collective-permute-start(bf16[192,1664]{1,0:T(8,128)(2,1)S(1)} %collective-permute-done.5.part_1), channel_id=1, source_target_pairs={{0,32},{1,33},{2,98},{3,99},{4,36},{5,37},{6,102},{7,103},{8,40},{... | collective-permute-start | bytes 1916936 | tf_op jit(solution)/shard_map/ppermute | solution.py:448
  52.4 18.9 %collective-permute-start.14 = (bf16[192,1536]{1,0:T(8,128)(2,1)S(1)}, bf16[192,1536]{1,0:T(8,128)(2,1)}, u32[]{:S(2)}, u32[]{:S(2)}) collective-permute-start(bf16[192,1536]{1,0:T(8,128)(2,1)S(1)} %pad_maximum_fusion.1.up_0), channel_id=1, source_target_pairs={{0,12},{1,13},{2,6},{3,7},{4,0},{5,1},{6,10},{7,11},{8,4},{9,5},{1... | collective-permute-start | bytes 1769480 | tf_op jit(solution)/shard_map/ppermute | solution.py:448
  55.4 18.2 %collective-permute-start.15 = (bf16[192,1536]{1,0:T(8,128)(2,1)}, bf16[192,1536]{1,0:T(8,128)(2,1)}, u32[]{:S(2)}, u32[]{:S(2)}) collective-permute-start(bf16[192,1536]{1,0:T(8,128)(2,1)} %collective-permute-done.13.up_1), channel_id=1, source_target_pairs={{0,4},{1,5},{2,14},{3,15},{4,8},{5,9},{6,2},{7,3},{8,12},{9,13},{1... | collective-permute-start | bytes 1769480 | tf_op jit(solution)/shard_map/ppermute | solution.py:448
  57.5 16.1 %collective-permute-start.17 = (bf16[384,768]{1,0:T(8,128)(2,1)S(1)}, bf16[384,768]{1,0:T(8,128)(2,1)}, u32[]{:S(2)}, u32[]{:S(2)}) collective-permute-start(bf16[384,768]{1,0:T(8,128)(2,1)S(1)} %bitcast.58), channel_id=1, source_target_pairs={{0,17},{1,0},{2,3},{3,18},{4,21},{5,4},{6,7},{7,22},{8,25},{9,8},{... | collective-permute-start | bytes 1769480 | tf_op jit(solution)/shard_map/ppermute | solution.py:448
  60.4 13.9 %collective-permute-start.18 = (bf16[384,768]{1,0:T(8,128)(2,1)}, bf16[384,768]{1,0:T(8,128)(2,1)}, u32[]{:S(2)}, u32[]{:S(2)}) collective-permute-start(bf16[384,768]{1,0:T(8,128)(2,1)} %collective-permute-done.16.down_1), channel_id=1, source_target_pairs={{0,1},{1,16},{2,19},{3,2},{4,5},{5,20},{6,23},{7,6},{8,9},{9,24},{... | collective-permute-start | bytes 1769480 | tf_op jit(solution)/shard_map/ppermute | solution.py:448
  68.1 6.2 %collective-permute-start.9 = (bf16[768,384]{1,0:T(8,128)(2,1)}, bf16[768,384]{1,0:T(8,128)(2,1)S(1)}, u32[]{:S(2)}, u32[]{:S(2)}) collective-permute-start(bf16[768,384]{1,0:T(8,128)(2,1)} %get-tuple-element.86.own_out.own_out_ref), channel_id=1, source_target_pairs={{0,2},{2,0},{1,3},{3,1},{4,6},{6,4},{5,7},{7,5},{8,10},{10,8},{9,1... | collective-permute-start | bytes 1769480 | tf_op jit(solution)/shard_map/ppermute | solution.py:390
  71.4 2.2 %collective-permute-start.8 = (bf16[256,384]{1,0:T(8,128)(2,1)}, bf16[256,384]{1,0:T(8,128)(2,1)S(1)}, u32[]{:S(2)}, u32[]{:S(2)}) collective-permute-start(bf16[256,384]{1,0:T(8,128)(2,1)} %get-tuple-element.85.own_o.own_o_ref), channel_id=1, source_target_pairs={{0,2},{2,0},{1,3},{3,1},{4,6},{6,4},{5,7},{7,5},{8,10},{10,8},{9,1... | collective-permute-start | bytes 589832 | tf_op jit(solution)/shard_map/ppermute | solution.py:390
  85.8 21.1 %collective-permute-start.19 = (f32[128,768]{1,0:T(8,128)}, f32[128,768]{1,0:T(8,128)S(1)}, u32[]{:S(2)}, u32[]{:S(2)}) collective-permute-start(f32[128,768]{1,0:T(8,128)} %get-tuple-element.90), channel_id=1, source_target_pairs={{0,2},{2,0},{1,3},{3,1},{4,6},{6,4},{5,7},{7,5},{8,10},{10,8},{9,1... | collective-permute-start | bytes 1179656 | tf_op jit(solution)/shard_map/ppermute | solution.py:390
  89.6 2.0 %collective-permute-start.20 = (bf16[256,768]{1,0:T(8,128)(2,1)}, bf16[256,768]{1,0:T(8,128)(2,1)S(1)}, u32[]{:S(2)}, u32[]{:S(2)}) collective-permute-start(bf16[256,768]{1,0:T(8,128)(2,1)} %get-tuple-element.92.own_grad_ref), channel_id=1, source_target_pairs={{0,2},{2,0},{1,3},{3,1},{4,6},{6,4},{5,7},{7,5},{8,10},{10,8},{9,1... | collective-permute-start | bytes 1179656 | tf_op jit(solution)/shard_map/ppermute | solution.py:390
  91.6 15.4 %collective-permute-start.23 = (bf16[384,768]{1,0:T(8,128)(2,1)}, bf16[384,768]{1,0:T(8,128)(2,1)S(1)}, u32[]{:S(2)}, u32[]{:S(2)}) collective-permute-start(bf16[384,768]{1,0:T(8,128)(2,1)} %get-tuple-element.114), channel_id=1, source_target_pairs={{0,1},{1,16},{2,19},{3,2},{4,5},{5,20},{6,23},{7,6},{8,9},{9,24},{... | collective-permute-start | bytes 1769480 | tf_op jit(solution)/shard_map/ppermute | solution.py:448
  92.0 15.2 %collective-permute-start.22 = (bf16[192,1536]{1,0:T(8,128)(2,1)}, bf16[192,1536]{1,0:T(8,128)(2,1)S(1)}, u32[]{:S(2)}, u32[]{:S(2)}) collective-permute-start(bf16[192,1536]{1,0:T(8,128)(2,1)} %get-tuple-element.112), channel_id=1, source_target_pairs={{0,4},{1,5},{2,14},{3,15},{4,8},{5,9},{6,2},{7,3},{8,12},{9,13},{1... | collective-permute-start | bytes 1769480 | tf_op jit(solution)/shard_map/ppermute | solution.py:448
  104.2 5.6 %collective-permute-start.21 = (f32[128,768]{1,0:T(8,128)}, f32[128,768]{1,0:T(8,128)S(1)}, u32[]{:S(2)}, u32[]{:S(2)}) collective-permute-start(f32[128,768]{1,0:T(8,128)} %get-tuple-element.110), channel_id=1, source_target_pairs={{0,2},{2,0},{1,3},{3,1},{4,6},{6,4},{5,7},{7,5},{8,10},{10,8},{9,1... | collective-permute-start | bytes 1179656 | tf_op jit(solution)/shard_map/ppermute | solution.py:390
  104.3 15.9 %collective-permute-start.24 = (bf16[192,1664]{1,0:T(8,128)(2,1)}, bf16[192,1664]{1,0:T(8,128)(2,1)S(1)}, u32[]{:S(2)}, u32[]{:S(2)}) collective-permute-start(bf16[192,1664]{1,0:T(8,128)(2,1)} %get-tuple-element.118), channel_id=1, source_target_pairs={{0,32},{1,33},{2,98},{3,99},{4,36},{5,37},{6,102},{7,103},{8,40},{... | collective-permute-start | bytes 1916936 | tf_op jit(solution)/shard_map/ppermute | solution.py:448
  106.9 16.3 %collective-permute-start.25 = (bf16[192,1664]{1,0:T(8,128)(2,1)}, bf16[192,1664]{1,0:T(8,128)(2,1)S(1)}, u32[]{:S(2)}, u32[]{:S(2)}) collective-permute-start(bf16[192,1664]{1,0:T(8,128)(2,1)} %get-tuple-element.119), channel_id=1, source_target_pairs={{0,96},{1,97},{2,34},{3,35},{4,100},{5,101},{6,38},{7,39},{8,104},... | collective-permute-start | bytes 1916936 | tf_op jit(solution)/shard_map/ppermute | solution.py:448
  107.0 17.0 %collective-permute-start.27 = (bf16[192,1536]{1,0:T(8,128)(2,1)}, bf16[192,1536]{1,0:T(8,128)(2,1)}, u32[]{:S(2)}, u32[]{:S(2)}) collective-permute-start(bf16[192,1536]{1,0:T(8,128)(2,1)} %get-tuple-element.124), channel_id=1, source_target_pairs={{0,12},{1,13},{2,6},{3,7},{4,0},{5,1},{6,10},{7,11},{8,4},{9,5},{1... | collective-permute-start | bytes 1769480 | tf_op jit(solution)/shard_map/ppermute | solution.py:448
  107.3 16.5 %collective-permute-start.29 = (bf16[384,768]{1,0:T(8,128)(2,1)S(1)}, bf16[384,768]{1,0:T(8,128)(2,1)}, u32[]{:S(2)}, u32[]{:S(2)}) collective-permute-start(bf16[384,768]{1,0:T(8,128)(2,1)S(1)} %add_convert_fusion.4), channel_id=1, source_target_pairs={{0,1},{1,16},{2,19},{3,2},{4,5},{5,20},{6,23},{7,6},{8,9},{9,24},{... | collective-permute-start | bytes 1769480 | tf_op jit(solution)/shard_map/ppermute | solution.py:448
  109.9 14.1 %collective-permute-start.28 = (bf16[192,1536]{1,0:T(8,128)(2,1)S(1)}, bf16[192,1536]{1,0:T(8,128)(2,1)}, u32[]{:S(2)}, u32[]{:S(2)}) collective-permute-start(bf16[192,1536]{1,0:T(8,128)(2,1)S(1)} %add_convert_fusion.5), channel_id=1, source_target_pairs={{0,4},{1,5},{2,14},{3,15},{4,8},{5,9},{6,2},{7,3},{8,12},{9,13},{1... | collective-permute-start | bytes 1769480 | tf_op jit(solution)/shard_map/ppermute | solution.py:448
  120.2 10.4 %collective-permute-start.37 = (bf16[384,768]{1,0:T(8,128)(2,1)}, bf16[384,768]{1,0:T(8,128)(2,1)S(1)}, u32[]{:S(2)}, u32[]{:S(2)}) collective-permute-start(bf16[384,768]{1,0:T(8,128)(2,1)} %get-tuple-element.129), channel_id=1, source_target_pairs={{0,17},{1,0},{2,3},{3,18},{4,21},{5,4},{6,7},{7,22},{8,25},{9,8},{... | collective-permute-start | bytes 1769480 | tf_op jit(solution)/shard_map/ppermute | solution.py:448
  123.4 10.9 %collective-permute-start.26 = (bf16[192,1664]{1,0:T(8,128)(2,1)S(1)}, bf16[192,1664]{1,0:T(8,128)(2,1)S(1)}, u32[]{:S(2)}, u32[]{:S(2)}) collective-permute-start(bf16[192,1664]{1,0:T(8,128)(2,1)S(1)} %add_convert_fusion.1), channel_id=1, source_target_pairs={{0,32},{1,33},{2,98},{3,99},{4,36},{5,37},{6,102},{7,103},{8,40},{... | collective-permute-start | bytes 1916936 | tf_op jit(solution)/shard_map/ppermute | solution.py:448
  125.6 9.6 %collective-permute-start.34 = (bf16[48,1536]{1,0:T(8,128)(2,1)S(1)}, bf16[48,1536]{1,0:T(8,128)(2,1)S(1)}, u32[]{:S(2)}, u32[]{:S(2)}) collective-permute-start(bf16[48,1536]{1,0:T(8,128)(2,1)S(1)} %get-tuple-element.162), channel_id=1, source_target_pairs={{0,32},{32,64},{64,96},{96,0},{1,33},{33,65},{65,97},{97,1},{2,34}... | collective-permute-start | bytes 442376 | tf_op jit(solution)/shard_map/ppermute | solution.py:409
  126.6 10.9 %collective-permute-start.35 = (bf16[48,1536]{1,0:T(8,128)(2,1)S(1)}, bf16[48,1536]{1,0:T(8,128)(2,1)S(1)}, u32[]{:S(2)}, u32[]{:S(2)}) collective-permute-start(bf16[48,1536]{1,0:T(8,128)(2,1)S(1)} %get-tuple-element.164), channel_id=1, source_target_pairs={{0,64},{32,96},{64,0},{96,32},{1,65},{33,97},{65,1},{97,33},{2,66}... | collective-permute-start | bytes 442376 | tf_op jit(solution)/shard_map/ppermute | solution.py:409
  128.5 20.3 %collective-permute-start.36 = (bf16[48,1536]{1,0:T(8,128)(2,1)S(1)}, bf16[48,1536]{1,0:T(8,128)(2,1)S(1)}, u32[]{:S(2)}, u32[]{:S(2)}) collective-permute-start(bf16[48,1536]{1,0:T(8,128)(2,1)S(1)} %get-tuple-element.163), channel_id=1, source_target_pairs={{0,96},{32,0},{64,32},{96,64},{1,97},{33,1},{65,33},{97,65},{2,98}... | collective-permute-start | bytes 442376 | tf_op jit(solution)/shard_map/ppermute | solution.py:409
  134.6 14.2 %collective-permute-start.32 = (bf16[2,24,1664]{2,1,0:T(8,128)(2,1)S(1)}, bf16[2,24,1664]{2,1,0:T(8,128)(2,1)S(1)}, u32[]{:S(2)}, u32[]{:S(2)}) collective-permute-start(bf16[2,24,1664]{2,1,0:T(8,128)(2,1)S(1)} %get-tuple-element.157), channel_id=1, source_target_pairs={{0,8},{4,12},{8,0},{12,4},{1,9},{5,13},{9,1},{13,5},{2,10},{6,14},... | collective-permute-start | bytes 479240 | tf_op jit(solution)/shard_map/ppermute | solution.py:409
  134.7 15.1 %collective-permute-start.31 = (bf16[2,24,1664]{2,1,0:T(8,128)(2,1)S(1)}, bf16[2,24,1664]{2,1,0:T(8,128)(2,1)S(1)}, u32[]{:S(2)}, u32[]{:S(2)}) collective-permute-start(bf16[2,24,1664]{2,1,0:T(8,128)(2,1)S(1)} %get-tuple-element.155), channel_id=1, source_target_pairs={{0,4},{4,8},{8,12},{12,0},{1,5},{5,9},{9,13},{13,1},{2,6},{6,10},{... | collective-permute-start | bytes 479240 | tf_op jit(solution)/shard_map/ppermute | solution.py:409
  135.1 16.5 %collective-permute-start.33 = (bf16[2,24,1664]{2,1,0:T(8,128)(2,1)S(1)}, bf16[2,24,1664]{2,1,0:T(8,128)(2,1)S(1)}, u32[]{:S(2)}, u32[]{:S(2)}) collective-permute-start(bf16[2,24,1664]{2,1,0:T(8,128)(2,1)S(1)} %get-tuple-element.156), channel_id=1, source_target_pairs={{0,12},{4,0},{8,4},{12,8},{1,13},{5,1},{9,5},{13,9},{2,14},{6,2},{... | collective-permute-start | bytes 479240 | tf_op jit(solution)/shard_map/ppermute | solution.py:409
  137.5 24.9 %collective-permute-start.30 = (bf16[128,1536]{1,0:T(8,128)(2,1)}, bf16[128,1536]{1,0:T(8,128)(2,1)S(1)}, u32[]{:S(2)}, u32[]{:S(2)}) collective-permute-start(bf16[128,1536]{1,0:T(8,128)(2,1)} %pad_maximum_fusion.3), channel_id=1, source_target_pairs={{0,0},{1,2},{2,1},{3,3},{4,4},{5,6},{6,5},{7,7},{8,8},{9,10},{10,9... | collective-permute-start | bytes 1179656 | tf_op jit(solution)/shard_map/ppermute | solution.py:398
  148.9 10.2 %collective-permute-start.38 = (bf16[96,768]{1,0:T(8,128)(2,1)S(1)}, bf16[96,768]{1,0:T(8,128)(2,1)S(1)}, u32[]{:S(2)}, u32[]{:S(2)}) collective-permute-start(bf16[96,768]{1,0:T(8,128)(2,1)S(1)} %bitcast.69), channel_id=1, source_target_pairs={{0,4},{4,8},{8,12},{12,0},{1,5},{5,9},{9,13},{13,1},{2,6},{6,10},{... | collective-permute-start | bytes 442376 | tf_op jit(solution)/shard_map/ppermute | solution.py:409
  149.0 10.1 %collective-permute-start.39 = (bf16[96,768]{1,0:T(8,128)(2,1)S(1)}, bf16[96,768]{1,0:T(8,128)(2,1)S(1)}, u32[]{:S(2)}, u32[]{:S(2)}) collective-permute-start(bf16[96,768]{1,0:T(8,128)(2,1)S(1)} %bitcast.68), channel_id=1, source_target_pairs={{0,8},{4,12},{8,0},{12,4},{1,9},{5,13},{9,1},{13,5},{2,10},{6,14},... | collective-permute-start | bytes 442376 | tf_op jit(solution)/shard_map/ppermute | solution.py:409
  149.9 9.6 %collective-permute-start.40 = (bf16[96,768]{1,0:T(8,128)(2,1)S(1)}, bf16[96,768]{1,0:T(8,128)(2,1)S(1)}, u32[]{:S(2)}, u32[]{:S(2)}) collective-permute-start(bf16[96,768]{1,0:T(8,128)(2,1)S(1)} %bitcast.67), channel_id=1, source_target_pairs={{0,12},{4,0},{8,4},{12,8},{1,13},{5,1},{9,5},{13,9},{2,14},{6,2},{... | collective-permute-start | bytes 442376 | tf_op jit(solution)/shard_map/ppermute | solution.py:409
  152.6 13.2 %all-to-all-start.2 = ((bf16[8,6,3200]{2,1,0:T(8,128)(2,1)}), bf16[8,6,3200]{2,1,0:T(8,128)(2,1)S(1)}, u32[]{:S(2)}, u32[]{:S(2)}) async-start(bf16[8,6,3200]{2,1,0:T(8,128)(2,1)} %reshape.121), calls=%async_computation.2 | async-start | bytes 819200 | tf_op jit(solution)/shard_map/all_to_all | solution.py:636
  159.6 4.4 %collective-permute-start.41 = (bf16[24,768]{1,0:T(8,128)(2,1)S(1)}, bf16[24,768]{1,0:T(8,128)(2,1)S(1)}, u32[]{:S(2)}, u32[]{:S(2)}) collective-permute-start(bf16[24,768]{1,0:T(8,128)(2,1)S(1)} %get-tuple-element.175), channel_id=1, source_target_pairs={{0,32},{32,64},{64,96},{96,0},{1,33},{33,65},{65,97},{97,1},{2,34}... | collective-permute-start | bytes 110600 | tf_op jit(solution)/shard_map/ppermute | solution.py:409
  159.7 4.4 %collective-permute-start.42 = (bf16[24,768]{1,0:T(8,128)(2,1)S(1)}, bf16[24,768]{1,0:T(8,128)(2,1)S(1)}, u32[]{:S(2)}, u32[]{:S(2)}) collective-permute-start(bf16[24,768]{1,0:T(8,128)(2,1)S(1)} %get-tuple-element.174), channel_id=1, source_target_pairs={{0,64},{32,96},{64,0},{96,32},{1,65},{33,97},{65,1},{97,33},{2,66}... | collective-permute-start | bytes 110600 | tf_op jit(solution)/shard_map/ppermute | solution.py:409
  159.8 5.2 %collective-permute-start.43 = (bf16[24,768]{1,0:T(8,128)(2,1)S(1)}, bf16[24,768]{1,0:T(8,128)(2,1)S(1)}, u32[]{:S(2)}, u32[]{:S(2)}) collective-permute-start(bf16[24,768]{1,0:T(8,128)(2,1)S(1)} %get-tuple-element.173), channel_id=1, source_target_pairs={{0,96},{32,0},{64,32},{96,64},{1,97},{33,1},{65,33},{97,65},{2,98}... | collective-permute-start | bytes 110600 | tf_op jit(solution)/shard_map/ppermute | solution.py:409
  (18 other events, 113.7 us)
